TPU v7x, 256 devices: a whole 4x4x8 slice. The times are simulated.
256 devices in a mesh: grp: 16 (over x, y_hi, core), dev: 16 (over z, y_lo).
Axes of the slice: x: 4, y: 4 (y_hi: 2, y_lo: 2; y = y_hi * 2 + y_lo), z: 8, core: 2. Of those that a mesh axis runs over, the one named last changes fastest.
Arguments:
- queries: bfloat16 [1024, 8192], P(('grp', 'dev')), may hold values from -10 to 10
- root_keys: bfloat16 [32768, 1024], P(('grp', 'dev')), may hold values from -4 to 4
- root_values: bfloat16 [32768, 1024], P(('grp', 'dev')), may hold values from -12 to 12
- prefix_keys: bfloat16 [16, 16, 8, 64, 1024], P('grp', 'dev'), may hold values from -6 to 6
- prefix_values: bfloat16 [16, 16, 8, 64, 1024], P('grp', 'dev'), may hold values from -12 to 12
- page_table: int32 [4, 16, 4], P(None, 'dev'), may hold values from 0 to 7, as said below
- task_ids: int32 [16], P('grp'), may hold values from 0 to 3
- suffix_keys: bfloat16 [1024, 128, 1024], P(('grp', 'dev')), may hold values from -6.375 to 6.375
- suffix_values: bfloat16 [1024, 128, 1024], P(('grp', 'dev')), may hold values from -12 to 12
- suffix_lengths: int32 [1024], P(('grp', 'dev')), may hold values from 1 to 128, as said below
Outputs:
- attended: bfloat16 [1024, 8192], P(('grp', 'dev'))
Inputs may be any that keep to these rules, and one draw needn't show every extreme that they name: `page_table`: entries of one task and one member name distinct pages of that member's pool. `suffix_lengths`: every device holds a row with all 128 slots live.
All inputs are finite; a program needn't handle non-finite values.
Results may differ from a plain program's by a relative error of at most 0.013.
Values may be sent and summed in bfloat16 or wider, within the bound.
No kernel may reach another device: no remote copies, remote signals or barrier semaphores. Data moves between devices by JAX's collectives and lax.ppermute only.
A program may use at most 64 MiB of HBM per device.

v0:
```python
import jax
import jax.numpy as jnp
from jax import lax
from jax.sharding import PartitionSpec as P

HD = 128
KVH = 8
QPK = 8


def passed_along(array, axis, by):
    size = lax.axis_size(axis)
    return lax.ppermute(array, axis, [(i, (i + by) % size) for i in range(size)])


def partial_attention(query_heads, key_rows, value_rows):
    key_count = key_rows.shape[0]
    key_heads = key_rows.reshape(key_count, KVH, HD)
    value_heads = value_rows.reshape(key_count, KVH, HD)
    scores = jnp.einsum(
        "rkgd,tkd->rkgt", query_heads, key_heads, preferred_element_type=jnp.float32
    ) * HD ** (-0.5)
    peaks = jnp.max(scores, axis=-1)
    weights = jnp.exp(scores - peaks[..., None])
    totals = jnp.sum(weights, axis=-1)
    weighted = jnp.einsum(
        "rkgt,tkd->rkgd",
        weights.astype(jnp.bfloat16),
        value_heads,
        preferred_element_type=jnp.float32,
    )
    return (peaks, totals, weighted)


def combine_states(former, latter):
    peaks = jnp.maximum(former[0], latter[0])
    scale_former = jnp.exp(former[0] - peaks)
    scale_latter = jnp.exp(latter[0] - peaks)
    totals = former[1] * scale_former + latter[1] * scale_latter
    weighted = former[2] * scale_former[..., None] + latter[2] * scale_latter[..., None]
    return (peaks, totals, weighted)


def reduce_sources(pieces):
    peak_pieces, total_pieces, weighted_pieces = pieces
    peaks = jnp.max(peak_pieces, axis=0)
    factor = jnp.exp(peak_pieces - peaks[None])
    return (
        peaks,
        jnp.sum(total_pieces * factor, axis=0),
        jnp.sum(weighted_pieces * factor[..., None], axis=0),
    )


def per_device(
    queries,
    root_keys,
    root_values,
    prefix_keys,
    prefix_values,
    page_table,
    task_ids,
    suffix_keys,
    suffix_values,
    suffix_lengths,
):
    own_rows = queries.shape[0]
    group_queries = lax.all_gather(queries, "dev", axis=0, tiled=True)
    query_heads = group_queries.reshape(group_queries.shape[0], KVH, QPK, HD)
    page_rows = lax.dynamic_index_in_dim(page_table[:, 0, :], task_ids[0], 0, keepdims=False)
    prefix_key_rows = jnp.take(prefix_keys[0, 0], page_rows, axis=0)
    prefix_key_rows = prefix_key_rows.reshape(-1, prefix_key_rows.shape[-1])
    prefix_value_rows = jnp.take(prefix_values[0, 0], page_rows, axis=0)
    prefix_value_rows = prefix_value_rows.reshape(-1, prefix_value_rows.shape[-1])
    state = partial_attention(query_heads, prefix_key_rows, prefix_value_rows)

    def attend_pair(stacked_pair):
        return partial_attention(query_heads, stacked_pair[0], stacked_pair[1])

    stacked = jnp.stack((root_keys, root_values))
    state = combine_states(state, attend_pair(stacked))
    groups = lax.axis_size("grp")

    def single_turn(turn_index, carry):
        current, carried = carry
        current = passed_along(current, "grp", 1)
        return (current, combine_states(carried, attend_pair(current)))

    current, state = lax.fori_loop(0, groups - 1, single_turn, (stacked, state))
    peaks, totals, weighted = state
    merged = reduce_sources(
        (
            lax.all_to_all(peaks[None], "dev", split_axis=1, concat_axis=0, tiled=True),
            lax.all_to_all(totals[None], "dev", split_axis=1, concat_axis=0, tiled=True),
            lax.all_to_all(weighted[None], "dev", split_axis=1, concat_axis=0, tiled=True),
        )
    )
    query_own = queries.reshape(own_rows, KVH, QPK, HD)
    slot_total = suffix_keys.shape[1]
    suffix_key_heads = suffix_keys.reshape(own_rows, slot_total, KVH, HD)
    suffix_value_heads = suffix_values.reshape(own_rows, slot_total, KVH, HD)
    suffix_scores = jnp.einsum(
        "rkgd,rskd->rkgs", query_own, suffix_key_heads, preferred_element_type=jnp.float32
    ) * HD ** (-0.5)
    live_slots = (jnp.arange(slot_total, dtype=jnp.int32)[None, :] < suffix_lengths[:, None])[
        :, None, None, :
    ]
    suffix_scores = jnp.where(live_slots, suffix_scores, -1e30)
    suffix_peaks = jnp.max(suffix_scores, axis=-1)
    suffix_weights = jnp.where(live_slots, jnp.exp(suffix_scores - suffix_peaks[..., None]), 0.0)
    suffix_totals = jnp.sum(suffix_weights, axis=-1)
    suffix_weighted = jnp.einsum(
        "rkgs,rskd->rkgd",
        suffix_weights.astype(jnp.bfloat16),
        suffix_value_heads,
        preferred_element_type=jnp.float32,
    )
    final_state = combine_states(merged, (suffix_peaks, suffix_totals, suffix_weighted))
    result = final_state[2] / final_state[1][..., None]
    return result.astype(jnp.bfloat16).reshape(own_rows, KVH * QPK * HD)


def solution(mesh):
    placed = (
        P(("grp", "dev"), None),
        P(("grp", "dev"), None),
        P(("grp", "dev"), None),
        P("grp", "dev", None, None, None),
        P("grp", "dev", None, None, None),
        P(None, "dev", None),
        P("grp"),
        P(("grp", "dev"), None, None),
        P(("grp", "dev"), None, None),
        P(("grp", "dev")),
    )
    return jax.shard_map(
        per_device, mesh=mesh, in_specs=placed, out_specs=P(("grp", "dev"), None), check_vma=False
    )
```

profile of v0, /device:TPU:8, one launch (start us, length us, event | category | flops | bytes accessed | tf_op | source)
XLA Modules:
  0.0 461.1 jit_solution(2400235448609533309)
XLA Ops:
  15.1 65.5 %all-gather.3.cloned.1.call-done = bf16[16,4,8192]{2,1,0:T(4,128)(2,1)} async-done(((bf16[1,4,8192]{2,1,0:T(4,128)(2,1)}), bf16[16,4,8192]{2,1,0:T(4,128)(2,1)}) %all-gather.3.cloned.1.call-update) | async-done | bytes 1048592 | tf_op jit(solution)/shard_map/all_gather | solution.py:68
  95.9 286.0 %while.16 = (s32[]{:T(128)}, bf16[2,128,1024]{1,2,0:T(8,128)(2,1)S(1)}, f32[64,8,8]{0,2,1:T(8,128)S(1)}, f32[64,8,8]{0,2,1:T(8,128)S(1)}, f32[64,8,8,128]{3,2,0,...) while((s32[]{:T(128)}, bf16[2,128,1024]{1,2,0:T(8,128)(2,1)S(1)}, f32[64,8,8]{0,2,1:T(8,128)S(1)}, ...), condition=%wide.region_7.9_spmd, body=%wide.region_4.0_spmd.sunk | while | flops 273170432 | bytes 16531573 | solution.py:89
  95.9 12.2 %collective-permute-done = bf16[2,128,1024]{1,2,0:T(8,128)(2,1)S(1)} collective-permute-done((bf16[2,128,1024]{1,2,0:T(8,128)(2,1)S(1)}, bf16[2,128,1024]{1,2,0:T(8,128)(2,1)S(1)}, u32[]{:S(2)}, u32[]{:S(2)}) %collective-permute-start) | collective-permute-done | bytes 524320 | tf_op jit(solution)/shard_map/while/body/eval_jaxpr/ppermute | solution.py:13
  114.9 12.2 %collective-permute-done = bf16[2,128,1024]{1,2,0:T(8,128)(2,1)S(1)} collective-permute-done((bf16[2,128,1024]{1,2,0:T(8,128)(2,1)S(1)}, bf16[2,128,1024]{1,2,0:T(8,128)(2,1)S(1)}, u32[]{:S(2)}, u32[]{:S(2)}) %collective-permute-start) | collective-permute-done | bytes 524320 | tf_op jit(solution)/shard_map/while/body/eval_jaxpr/ppermute | solution.py:13
  130.1 3.8 fusion.72
  134.0 12.2 %collective-permute-done = bf16[2,128,1024]{1,2,0:T(8,128)(2,1)S(1)} collective-permute-done((bf16[2,128,1024]{1,2,0:T(8,128)(2,1)S(1)}, bf16[2,128,1024]{1,2,0:T(8,128)(2,1)S(1)}, u32[]{:S(2)}, u32[]{:S(2)}) %collective-permute-start) | collective-permute-done | bytes 524320 | tf_op jit(solution)/shard_map/while/body/eval_jaxpr/ppermute | solution.py:13
  149.2 3.8 fusion.72
  153.1 12.2 %collective-permute-done = bf16[2,128,1024]{1,2,0:T(8,128)(2,1)S(1)} collective-permute-done((bf16[2,128,1024]{1,2,0:T(8,128)(2,1)S(1)}, bf16[2,128,1024]{1,2,0:T(8,128)(2,1)S(1)}, u32[]{:S(2)}, u32[]{:S(2)}) %collective-permute-start) | collective-permute-done | bytes 524320 | tf_op jit(solution)/shard_map/while/body/eval_jaxpr/ppermute | solution.py:13
  172.1 12.2 %collective-permute-done = bf16[2,128,1024]{1,2,0:T(8,128)(2,1)S(1)} collective-permute-done((bf16[2,128,1024]{1,2,0:T(8,128)(2,1)S(1)}, bf16[2,128,1024]{1,2,0:T(8,128)(2,1)S(1)}, u32[]{:S(2)}, u32[]{:S(2)}) %collective-permute-start) | collective-permute-done | bytes 524320 | tf_op jit(solution)/shard_map/while/body/eval_jaxpr/ppermute | solution.py:13
  187.3 3.8 fusion.72
  191.2 12.2 %collective-permute-done = bf16[2,128,1024]{1,2,0:T(8,128)(2,1)S(1)} collective-permute-done((bf16[2,128,1024]{1,2,0:T(8,128)(2,1)S(1)}, bf16[2,128,1024]{1,2,0:T(8,128)(2,1)S(1)}, u32[]{:S(2)}, u32[]{:S(2)}) %collective-permute-start) | collective-permute-done | bytes 524320 | tf_op jit(solution)/shard_map/while/body/eval_jaxpr/ppermute | solution.py:13
  206.4 3.8 fusion.72
  210.3 12.2 %collective-permute-done = bf16[2,128,1024]{1,2,0:T(8,128)(2,1)S(1)} collective-permute-done((bf16[2,128,1024]{1,2,0:T(8,128)(2,1)S(1)}, bf16[2,128,1024]{1,2,0:T(8,128)(2,1)S(1)}, u32[]{:S(2)}, u32[]{:S(2)}) %collective-permute-start) | collective-permute-done | bytes 524320 | tf_op jit(solution)/shard_map/while/body/eval_jaxpr/ppermute | solution.py:13
  225.4 3.8 fusion.72
  229.3 12.2 %collective-permute-done = bf16[2,128,1024]{1,2,0:T(8,128)(2,1)S(1)} collective-permute-done((bf16[2,128,1024]{1,2,0:T(8,128)(2,1)S(1)}, bf16[2,128,1024]{1,2,0:T(8,128)(2,1)S(1)}, u32[]{:S(2)}, u32[]{:S(2)}) %collective-permute-start) | collective-permute-done | bytes 524320 | tf_op jit(solution)/shard_map/while/body/eval_jaxpr/ppermute | solution.py:13
  244.5 3.8 fusion.72
  248.4 12.2 %collective-permute-done = bf16[2,128,1024]{1,2,0:T(8,128)(2,1)S(1)} collective-permute-done((bf16[2,128,1024]{1,2,0:T(8,128)(2,1)S(1)}, bf16[2,128,1024]{1,2,0:T(8,128)(2,1)S(1)}, u32[]{:S(2)}, u32[]{:S(2)}) %collective-permute-start) | collective-permute-done | bytes 524320 | tf_op jit(solution)/shard_map/while/body/eval_jaxpr/ppermute | solution.py:13
  263.6 3.8 fusion.72
  267.5 12.2 %collective-permute-done = bf16[2,128,1024]{1,2,0:T(8,128)(2,1)S(1)} collective-permute-done((bf16[2,128,1024]{1,2,0:T(8,128)(2,1)S(1)}, bf16[2,128,1024]{1,2,0:T(8,128)(2,1)S(1)}, u32[]{:S(2)}, u32[]{:S(2)}) %collective-permute-start) | collective-permute-done | bytes 524320 | tf_op jit(solution)/shard_map/while/body/eval_jaxpr/ppermute | solution.py:13
  282.6 3.8 fusion.72
  286.5 12.2 %collective-permute-done = bf16[2,128,1024]{1,2,0:T(8,128)(2,1)S(1)} collective-permute-done((bf16[2,128,1024]{1,2,0:T(8,128)(2,1)S(1)}, bf16[2,128,1024]{1,2,0:T(8,128)(2,1)S(1)}, u32[]{:S(2)}, u32[]{:S(2)}) %collective-permute-start) | collective-permute-done | bytes 524320 | tf_op jit(solution)/shard_map/while/body/eval_jaxpr/ppermute | solution.py:13
  301.7 3.8 fusion.72
  305.6 12.2 %collective-permute-done = bf16[2,128,1024]{1,2,0:T(8,128)(2,1)S(1)} collective-permute-done((bf16[2,128,1024]{1,2,0:T(8,128)(2,1)S(1)}, bf16[2,128,1024]{1,2,0:T(8,128)(2,1)S(1)}, u32[]{:S(2)}, u32[]{:S(2)}) %collective-permute-start) | collective-permute-done | bytes 524320 | tf_op jit(solution)/shard_map/while/body/eval_jaxpr/ppermute | solution.py:13
  324.7 12.2 %collective-permute-done = bf16[2,128,1024]{1,2,0:T(8,128)(2,1)S(1)} collective-permute-done((bf16[2,128,1024]{1,2,0:T(8,128)(2,1)S(1)}, bf16[2,128,1024]{1,2,0:T(8,128)(2,1)S(1)}, u32[]{:S(2)}, u32[]{:S(2)}) %collective-permute-start) | collective-permute-done | bytes 524320 | tf_op jit(solution)/shard_map/while/body/eval_jaxpr/ppermute | solution.py:13
  343.7 12.2 %collective-permute-done = bf16[2,128,1024]{1,2,0:T(8,128)(2,1)S(1)} collective-permute-done((bf16[2,128,1024]{1,2,0:T(8,128)(2,1)S(1)}, bf16[2,128,1024]{1,2,0:T(8,128)(2,1)S(1)}, u32[]{:S(2)}, u32[]{:S(2)}) %collective-permute-start) | collective-permute-done | bytes 524320 | tf_op jit(solution)/shard_map/while/body/eval_jaxpr/ppermute | solution.py:13
  362.8 12.3 %collective-permute-done = bf16[2,128,1024]{1,2,0:T(8,128)(2,1)S(1)} collective-permute-done((bf16[2,128,1024]{1,2,0:T(8,128)(2,1)S(1)}, bf16[2,128,1024]{1,2,0:T(8,128)(2,1)S(1)}, u32[]{:S(2)}, u32[]{:S(2)}) %collective-permute-start) | collective-permute-done | bytes 524320 | tf_op jit(solution)/shard_map/while/body/eval_jaxpr/ppermute | solution.py:13
  382.8 7.0 %all-to-all-start.1 = ((f32[16,1,256]{2,1,0:T(1,128)}), f32[16,1,256]{2,1,0:T(1,128)S(1)}, u32[]{:S(2)}, u32[]{:S(2)}) async-start(f32[16,1,256]{2,1,0:T(1,128)} %reshape.140), calls=%async_computation.1 | async-start | bytes 32768 | tf_op jit(solution)/shard_map/all_to_all | solution.py:93
  390.8 6.3 %all-to-all-done.1 = f32[16,1,256]{2,1,0:T(1,128)S(1)} async-done(((f32[16,1,256]{2,1,0:T(1,128)}), f32[16,1,256]{2,1,0:T(1,128)S(1)}, u32[]{:S(2)}, u32[]{:S(2)}) %all-to-all-start.1) | async-done | bytes 16416 | tf_op jit(solution)/shard_map/all_to_all | solution.py:93
  397.0 4.7 %all-to-all-start.2 = ((f32[16,1,256]{2,1,0:T(1,128)}), f32[16,1,256]{2,1,0:T(1,128)S(1)}, u32[]{:S(2)}, u32[]{:S(2)}) async-start(f32[16,1,256]{2,1,0:T(1,128)} %reshape.142), calls=%async_computation.2 | async-start | bytes 32768 | tf_op jit(solution)/shard_map/all_to_all | solution.py:94
  404.9 4.9 %all-to-all-done.2 = f32[16,1,256]{2,1,0:T(1,128)S(1)} async-done(((f32[16,1,256]{2,1,0:T(1,128)}), f32[16,1,256]{2,1,0:T(1,128)S(1)}, u32[]{:S(2)}, u32[]{:S(2)}) %all-to-all-start.2) | async-done | bytes 16416 | tf_op jit(solution)/shard_map/all_to_all | solution.py:94
  409.8 6.7 %all-to-all-start = ((f32[1,64,8,8,128]{4,3,2,0,1:T(8,128)}), f32[1,64,8,8,128]{4,3,2,0,1:T(8,128)}, u32[]{:S(2)}, u32[]{:S(2)}) async-start(f32[1,64,8,8,128]{4,3,2,0,1:T(8,128)} %bitcast.147), calls=%async_computation | async-start | bytes 4194304 | tf_op jit(solution)/shard_map/all_to_all | solution.py:95
  420.0 31.1 %all-to-all-done = f32[1,64,8,8,128]{4,3,2,0,1:T(8,128)} async-done(((f32[1,64,8,8,128]{4,3,2,0,1:T(8,128)}), f32[1,64,8,8,128]{4,3,2,0,1:T(8,128)}, u32[]{:S(2)}, u32[]{:S(2)}) %all-to-all-start) | async-done | bytes 2097184 | tf_op jit(solution)/shard_map/all_to_all | solution.py:95
  (192 shorter events, 102.7 us)
Async XLA Ops:
  6.5 2.0 copy-start
  6.5 74.0 %all-gather.3.cloned.1.call-start = ((), (), s32[]{:S(2)}) async-start(), calls=%async_computation.3 | async-start | bytes 1114112 | tf_op jit(solution)/shard_map/all_gather | solution.py:68
  9.2 3.0 copy-start.3
  11.2 2.8 copy-start.4
  83.4 2.3 copy-start.5
  86.8 1.4 copy-start.1
  93.3 2.6 copy-start.6
  95.9 12.2 %collective-permute-start = (bf16[2,128,1024]{1,2,0:T(8,128)(2,1)S(1)}, bf16[2,128,1024]{1,2,0:T(8,128)(2,1)S(1)}, u32[]{:S(2)}, u32[]{:S(2)}) collective-permute-start(bf16[2,128,1024]{1,2,0:T(8,128)(2,1)S(1)} %get-tuple-element.167), channel_id=1, source_target_pairs={{0,16},{16,32},{32,48},{48,64},{64,80},{80,96},{96,112},{112,128},... | collective-permute-start | bytes 1572872 | tf_op jit(solution)/shard_map/while/body/eval_jaxpr/ppermute | solution.py:13
  114.9 12.3 %collective-permute-start = (bf16[2,128,1024]{1,2,0:T(8,128)(2,1)S(1)}, bf16[2,128,1024]{1,2,0:T(8,128)(2,1)S(1)}, u32[]{:S(2)}, u32[]{:S(2)}) collective-permute-start(bf16[2,128,1024]{1,2,0:T(8,128)(2,1)S(1)} %get-tuple-element.167), channel_id=1, source_target_pairs={{0,16},{16,32},{32,48},{48,64},{64,80},{80,96},{96,112},{112,128},... | collective-permute-start | bytes 1572872 | tf_op jit(solution)/shard_map/while/body/eval_jaxpr/ppermute | solution.py:13
  133.9 12.3 %collective-permute-start = (bf16[2,128,1024]{1,2,0:T(8,128)(2,1)S(1)}, bf16[2,128,1024]{1,2,0:T(8,128)(2,1)S(1)}, u32[]{:S(2)}, u32[]{:S(2)}) collective-permute-start(bf16[2,128,1024]{1,2,0:T(8,128)(2,1)S(1)} %get-tuple-element.167), channel_id=1, source_target_pairs={{0,16},{16,32},{32,48},{48,64},{64,80},{80,96},{96,112},{112,128},... | collective-permute-start | bytes 1572872 | tf_op jit(solution)/shard_map/while/body/eval_jaxpr/ppermute | solution.py:13
  153.0 12.3 %collective-permute-start = (bf16[2,128,1024]{1,2,0:T(8,128)(2,1)S(1)}, bf16[2,128,1024]{1,2,0:T(8,128)(2,1)S(1)}, u32[]{:S(2)}, u32[]{:S(2)}) collective-permute-start(bf16[2,128,1024]{1,2,0:T(8,128)(2,1)S(1)} %get-tuple-element.167), channel_id=1, source_target_pairs={{0,16},{16,32},{32,48},{48,64},{64,80},{80,96},{96,112},{112,128},... | collective-permute-start | bytes 1572872 | tf_op jit(solution)/shard_map/while/body/eval_jaxpr/ppermute | solution.py:13
  172.1 12.3 %collective-permute-start = (bf16[2,128,1024]{1,2,0:T(8,128)(2,1)S(1)}, bf16[2,128,1024]{1,2,0:T(8,128)(2,1)S(1)}, u32[]{:S(2)}, u32[]{:S(2)}) collective-permute-start(bf16[2,128,1024]{1,2,0:T(8,128)(2,1)S(1)} %get-tuple-element.167), channel_id=1, source_target_pairs={{0,16},{16,32},{32,48},{48,64},{64,80},{80,96},{96,112},{112,128},... | collective-permute-start | bytes 1572872 | tf_op jit(solution)/shard_map/while/body/eval_jaxpr/ppermute | solution.py:13
  191.1 12.3 %collective-permute-start = (bf16[2,128,1024]{1,2,0:T(8,128)(2,1)S(1)}, bf16[2,128,1024]{1,2,0:T(8,128)(2,1)S(1)}, u32[]{:S(2)}, u32[]{:S(2)}) collective-permute-start(bf16[2,128,1024]{1,2,0:T(8,128)(2,1)S(1)} %get-tuple-element.167), channel_id=1, source_target_pairs={{0,16},{16,32},{32,48},{48,64},{64,80},{80,96},{96,112},{112,128},... | collective-permute-start | bytes 1572872 | tf_op jit(solution)/shard_map/while/body/eval_jaxpr/ppermute | solution.py:13
  210.2 12.3 %collective-permute-start = (bf16[2,128,1024]{1,2,0:T(8,128)(2,1)S(1)}, bf16[2,128,1024]{1,2,0:T(8,128)(2,1)S(1)}, u32[]{:S(2)}, u32[]{:S(2)}) collective-permute-start(bf16[2,128,1024]{1,2,0:T(8,128)(2,1)S(1)} %get-tuple-element.167), channel_id=1, source_target_pairs={{0,16},{16,32},{32,48},{48,64},{64,80},{80,96},{96,112},{112,128},... | collective-permute-start | bytes 1572872 | tf_op jit(solution)/shard_map/while/body/eval_jaxpr/ppermute | solution.py:13
  229.3 12.3 %collective-permute-start = (bf16[2,128,1024]{1,2,0:T(8,128)(2,1)S(1)}, bf16[2,128,1024]{1,2,0:T(8,128)(2,1)S(1)}, u32[]{:S(2)}, u32[]{:S(2)}) collective-permute-start(bf16[2,128,1024]{1,2,0:T(8,128)(2,1)S(1)} %get-tuple-element.167), channel_id=1, source_target_pairs={{0,16},{16,32},{32,48},{48,64},{64,80},{80,96},{96,112},{112,128},... | collective-permute-start | bytes 1572872 | tf_op jit(solution)/shard_map/while/body/eval_jaxpr/ppermute | solution.py:13
  248.3 12.3 %collective-permute-start = (bf16[2,128,1024]{1,2,0:T(8,128)(2,1)S(1)}, bf16[2,128,1024]{1,2,0:T(8,128)(2,1)S(1)}, u32[]{:S(2)}, u32[]{:S(2)}) collective-permute-start(bf16[2,128,1024]{1,2,0:T(8,128)(2,1)S(1)} %get-tuple-element.167), channel_id=1, source_target_pairs={{0,16},{16,32},{32,48},{48,64},{64,80},{80,96},{96,112},{112,128},... | collective-permute-start | bytes 1572872 | tf_op jit(solution)/shard_map/while/body/eval_jaxpr/ppermute | solution.py:13
  267.4 12.3 %collective-permute-start = (bf16[2,128,1024]{1,2,0:T(8,128)(2,1)S(1)}, bf16[2,128,1024]{1,2,0:T(8,128)(2,1)S(1)}, u32[]{:S(2)}, u32[]{:S(2)}) collective-permute-start(bf16[2,128,1024]{1,2,0:T(8,128)(2,1)S(1)} %get-tuple-element.167), channel_id=1, source_target_pairs={{0,16},{16,32},{32,48},{48,64},{64,80},{80,96},{96,112},{112,128},... | collective-permute-start | bytes 1572872 | tf_op jit(solution)/shard_map/while/body/eval_jaxpr/ppermute | solution.py:13
  286.5 12.3 %collective-permute-start = (bf16[2,128,1024]{1,2,0:T(8,128)(2,1)S(1)}, bf16[2,128,1024]{1,2,0:T(8,128)(2,1)S(1)}, u32[]{:S(2)}, u32[]{:S(2)}) collective-permute-start(bf16[2,128,1024]{1,2,0:T(8,128)(2,1)S(1)} %get-tuple-element.167), channel_id=1, source_target_pairs={{0,16},{16,32},{32,48},{48,64},{64,80},{80,96},{96,112},{112,128},... | collective-permute-start | bytes 1572872 | tf_op jit(solution)/shard_map/while/body/eval_jaxpr/ppermute | solution.py:13
  305.5 12.3 %collective-permute-start = (bf16[2,128,1024]{1,2,0:T(8,128)(2,1)S(1)}, bf16[2,128,1024]{1,2,0:T(8,128)(2,1)S(1)}, u32[]{:S(2)}, u32[]{:S(2)}) collective-permute-start(bf16[2,128,1024]{1,2,0:T(8,128)(2,1)S(1)} %get-tuple-element.167), channel_id=1, source_target_pairs={{0,16},{16,32},{32,48},{48,64},{64,80},{80,96},{96,112},{112,128},... | collective-permute-start | bytes 1572872 | tf_op jit(solution)/shard_map/while/body/eval_jaxpr/ppermute | solution.py:13
  324.6 12.3 %collective-permute-start = (bf16[2,128,1024]{1,2,0:T(8,128)(2,1)S(1)}, bf16[2,128,1024]{1,2,0:T(8,128)(2,1)S(1)}, u32[]{:S(2)}, u32[]{:S(2)}) collective-permute-start(bf16[2,128,1024]{1,2,0:T(8,128)(2,1)S(1)} %get-tuple-element.167), channel_id=1, source_target_pairs={{0,16},{16,32},{32,48},{48,64},{64,80},{80,96},{96,112},{112,128},... | collective-permute-start | bytes 1572872 | tf_op jit(solution)/shard_map/while/body/eval_jaxpr/ppermute | solution.py:13
  343.6 12.3 %collective-permute-start = (bf16[2,128,1024]{1,2,0:T(8,128)(2,1)S(1)}, bf16[2,128,1024]{1,2,0:T(8,128)(2,1)S(1)}, u32[]{:S(2)}, u32[]{:S(2)}) collective-permute-start(bf16[2,128,1024]{1,2,0:T(8,128)(2,1)S(1)} %get-tuple-element.167), channel_id=1, source_target_pairs={{0,16},{16,32},{32,48},{48,64},{64,80},{80,96},{96,112},{112,128},... | collective-permute-start | bytes 1572872 | tf_op jit(solution)/shard_map/while/body/eval_jaxpr/ppermute | solution.py:13
  362.7 12.4 %collective-permute-start = (bf16[2,128,1024]{1,2,0:T(8,128)(2,1)S(1)}, bf16[2,128,1024]{1,2,0:T(8,128)(2,1)S(1)}, u32[]{:S(2)}, u32[]{:S(2)}) collective-permute-start(bf16[2,128,1024]{1,2,0:T(8,128)(2,1)S(1)} %get-tuple-element.167), channel_id=1, source_target_pairs={{0,16},{16,32},{32,48},{48,64},{64,80},{80,96},{96,112},{112,128},... | collective-permute-start | bytes 1572872 | tf_op jit(solution)/shard_map/while/body/eval_jaxpr/ppermute | solution.py:13
  382.8 14.2 %all-to-all-start.1 = ((f32[16,1,256]{2,1,0:T(1,128)}), f32[16,1,256]{2,1,0:T(1,128)S(1)}, u32[]{:S(2)}, u32[]{:S(2)}) async-start(f32[16,1,256]{2,1,0:T(1,128)} %reshape.140), calls=%async_computation.1 | async-start | bytes 32768 | tf_op jit(solution)/shard_map/all_to_all | solution.py:93
  397.0 12.8 %all-to-all-start.2 = ((f32[16,1,256]{2,1,0:T(1,128)}), f32[16,1,256]{2,1,0:T(1,128)S(1)}, u32[]{:S(2)}, u32[]{:S(2)}) async-start(f32[16,1,256]{2,1,0:T(1,128)} %reshape.142), calls=%async_computation.2 | async-start | bytes 32768 | tf_op jit(solution)/shard_map/all_to_all | solution.py:94
  409.8 6.7 %copy-start.9 = (s32[4]{0:T(128)S(1)}, s32[4]{0:T(128)}, u32[]{:S(2)}) copy-start(s32[4]{0:T(128)} %param.23) | copy-start | bytes 52
  409.8 6.8 %copy-start.2 = (bf16[4,128,1024]{2,1,0:T(8,128)(2,1)S(1)}, bf16[4,128,1024]{2,1,0:T(8,128)(2,1)}, u32[]{:S(2)}) copy-start(bf16[4,128,1024]{2,1,0:T(8,128)(2,1)} %param.21) | copy-start | bytes 3145732
  409.8 6.8 %copy-start.7 = (bf16[4,8192]{1,0:T(4,128)(2,1)S(1)}, bf16[4,8192]{1,0:T(4,128)(2,1)}, u32[]{:S(2)}) copy-start(bf16[4,8192]{1,0:T(4,128)(2,1)} %param.14) | copy-start | bytes 196612
  409.8 41.3 %all-to-all-start = ((f32[1,64,8,8,128]{4,3,2,0,1:T(8,128)}), f32[1,64,8,8,128]{4,3,2,0,1:T(8,128)}, u32[]{:S(2)}, u32[]{:S(2)}) async-start(f32[1,64,8,8,128]{4,3,2,0,1:T(8,128)} %bitcast.147), calls=%async_computation | async-start | bytes 4194304 | tf_op jit(solution)/shard_map/all_to_all | solution.py:95
  419.8 33.3 %copy-start.8 = (bf16[4,128,1024]{2,1,0:T(8,128)(2,1)S(1)}, bf16[4,128,1024]{2,1,0:T(8,128)(2,1)}, u32[]{:S(2)}) copy-start(bf16[4,128,1024]{2,1,0:T(8,128)(2,1)} %param.22) | copy-start | bytes 3145732
Sparse Core Ops, SparseCore 0:
  9.1 71.3 all-gather.2
where the time goes:
time: 462 us; the launch traced here: 461 us
  waiting for transfers between devices  292 us (63%)
  matrix products  76.2 us (16%)
  other arithmetic  36.3 us (8%)
  local copies, waits for them, and re-layouts  22.2 us (5%)
  starting transfers between devices  19.7 us (4%)
  between operations  14.3 us (3%)
    ppermute x15, waiting for transfers between devices, passed_along(): lax.ppermute(array, axis, [(i, (i + by) % size) for i in range(size)])  183 us
    all_gather x1, waiting for transfers between devices, per_device(): group_queries = lax.all_gather(queries, 'dev', axis=0, tiled=True)  65.5 us
    dot_general x17, matrix products, partial_attention(): jnp.einsum('rkgt,tkd->rkgd', weights.astype(jnp.bfloat16), value_heads, p...  60.1 us
    all_to_all x1, waiting for transfers between devices, per_device(): lax.all_to_all(weighted[None], 'dev', split_axis=1, concat_axis=0, tiled=...  31.1 us
    convert_element_type x15, other arithmetic, partial_attention(): weights.astype(jnp.bfloat16)  27.6 us
    dot_general x17, matrix products, partial_attention(): jnp.einsum('rkgd,tkd->rkgt', query_heads, key_heads, preferred_element_ty...  14.9 us
  transfers between devices with their start and end apart: 19, of which 19 were waited for; matrix products, arithmetic and copies ran while one was open for 3% of the time, Pallas kernels for 0%

commit v1 on v0

v1 whole, which is shorter than its diff:
```python
import functools

import jax
import jax.numpy as jnp
from jax import lax
from jax.experimental import pallas as pl
from jax.experimental.pallas import tpu as pltpu
from jax.sharding import PartitionSpec as P

HD = 128
KVH = 8
QPK = 8
MEMBERS = 16
OWN = 4
UNIT = OWN * QPK
SUF = 128
PPD = 4
PAGE = 64
SCALE = HD ** (-0.5)
LOG2E = 1.4426950408889634
VMEM_LIMIT = 40 * 1024 * 1024
O_CHUNKS = ((0, 4), (4, 4))


def grp_index(x, y_hi, core):
    return (x % 4) * 4 + (y_hi % 2) * 2 + core


def grp_pairs(target):
    return [
        (grp_index(x, y, c), grp_index(*target(x, y, c)))
        for x in range(4)
        for y in range(2)
        for c in range(2)
    ]


def to_other_core(array):
    return lax.ppermute(array, "grp", grp_pairs(lambda x, y, c: (x, y, 1 - c)))


def along_y(array):
    return lax.ppermute(array, "grp", grp_pairs(lambda x, y, c: (x, 1 - y, c)))


def along_x(array):
    return lax.ppermute(array, "grp", grp_pairs(lambda x, y, c: (x + 1 - 2 * c, y, c)))


def gather_root(own):
    other = to_other_core(own)
    near = along_x(own)
    across = along_y(own)
    near_other = along_x(other)
    far = along_x(near)
    across_near = along_y(near)
    across_other = to_other_core(across)
    across_near_other = along_x(across_other)
    across_far = along_x(across_near)
    received = [near, near_other, far, across_near, across_near_other, across_far]
    return [own, other, across, across_other] + received + [to_other_core(r) for r in received]


def nt_dot(a, b):
    return lax.dot_general(a, b, (((1,), (1,)), ((), ())), preferred_element_type=jnp.float32)


def split_three(value):
    first = value.astype(jnp.bfloat16)
    rest = value - first.astype(jnp.float32)
    second = rest.astype(jnp.bfloat16)
    third = (rest - second.astype(jnp.float32)).astype(jnp.bfloat16)
    return first, second, third


def attention_kernel(head_start, heads, pieces, *refs):
    task_ref, table_ref, q_ref = refs[:3]
    piece_refs = refs[3 : 3 + pieces]
    pool_k, pool_v, out_ref = refs[3 + pieces : 6 + pieces]
    page_k, page_v, stats_ref, sems = refs[6 + pieces :]
    task = task_ref[0]
    copies = []
    for j in range(PPD):
        page = table_ref[task, j]
        rows = pl.ds(j * PAGE, PAGE)
        copies.append(pltpu.make_async_copy(pool_k.at[page], page_k.at[rows], sems.at[j]))
        copies.append(pltpu.make_async_copy(pool_v.at[page], page_v.at[rows], sems.at[PPD + j]))
    for copy in copies:
        copy.start()
    stats_ref[...] = jnp.zeros_like(stats_ref)
    for copy in copies:
        copy.wait()
    rows_all = MEMBERS * UNIT

    def one_head(index, carry):
        lanes = pl.ds(pl.multiple_of((head_start + index) * HD, HD), HD)
        q = q_ref[:, head_start + index].reshape(rows_all, HD)
        keys = jnp.concatenate([r[0, :, lanes] for r in piece_refs] + [page_k[:, lanes]], axis=0)
        scores = nt_dot(q, keys)
        peaks = jnp.max(scores, axis=1, keepdims=True)
        weights = jnp.exp2((scores - peaks) * (SCALE * LOG2E))
        totals = jnp.sum(weights, axis=1, keepdims=True)
        values = jnp.concatenate([r[1, :, lanes] for r in piece_refs] + [page_v[:, lanes]], axis=0)
        weighted = jnp.dot(weights.astype(jnp.bfloat16), values, preferred_element_type=jnp.float32)
        out_ref[:, pl.ds(index, 1)] = (
            (weighted / totals).astype(jnp.bfloat16).reshape(MEMBERS, 1, UNIT, HD)
        )
        lse = peaks * SCALE + jnp.log(totals)
        lane = lax.broadcasted_iota(jnp.int32, (rows_all, HD), 1)
        stats_ref[...] = jnp.where(lane == index, lse, stats_ref[...])
        return carry

    lax.fori_loop(0, heads, one_head, 0)
    lane = lax.broadcasted_iota(jnp.int32, (rows_all, HD), 1)
    first, second, third = split_three(stats_ref[...])
    packed = (
        first.astype(jnp.float32)
        + pltpu.roll(second.astype(jnp.float32), KVH, 1)
        + pltpu.roll(third.astype(jnp.float32), 2 * KVH, 1)
    )
    packed = jnp.where(lane < 3 * KVH, packed, 0.0)
    out_ref[:, heads] = packed.astype(jnp.bfloat16).reshape(MEMBERS, UNIT, HD)


def attend(head_start, heads, task, table, q_all, pieces, pool_k, pool_v):
    rows_all = MEMBERS * UNIT
    keys = 128 * len(pieces) + PPD * PAGE
    vmem = pl.BlockSpec(memory_space=pltpu.VMEM)
    smem = pl.BlockSpec(memory_space=pltpu.SMEM)
    hbm = pl.BlockSpec(memory_space=pl.ANY)
    return pl.pallas_call(
        functools.partial(attention_kernel, head_start, heads, len(pieces)),
        out_shape=jax.ShapeDtypeStruct((MEMBERS, heads + 1, UNIT, HD), jnp.bfloat16),
        in_specs=[smem, smem, vmem] + [vmem] * len(pieces) + [hbm, hbm],
        out_specs=vmem,
        scratch_shapes=[
            pltpu.VMEM((PPD * PAGE, KVH * HD), jnp.bfloat16),
            pltpu.VMEM((PPD * PAGE, KVH * HD), jnp.bfloat16),
            pltpu.VMEM((rows_all, HD), jnp.float32),
            pltpu.SemaphoreType.DMA((2 * PPD,)),
        ],
        compiler_params=pltpu.CompilerParams(vmem_limit_bytes=VMEM_LIMIT),
        cost_estimate=pl.CostEstimate(
            flops=4 * heads * rows_all * keys * HD,
            bytes_accessed=4 * keys * heads * HD,
            transcendentals=heads * rows_all * keys,
        ),
        name="attend",
    )(task, table, q_all, *pieces, pool_k, pool_v)


def suffix_kernel(length_ref, q_ref, k_ref, v_ref, out_ref, lse_ref):
    slots = OWN * SUF
    row = lax.broadcasted_iota(jnp.int32, (UNIT, slots), 0) // QPK
    slot = lax.broadcasted_iota(jnp.int32, (UNIT, slots), 1)
    live = jnp.zeros((UNIT, slots), jnp.bool_)
    for i in range(OWN):
        low = i * SUF
        live = live | ((row == i) & (slot >= low) & (slot < low + length_ref[i]))
    for k in range(KVH):
        lanes = slice(k * HD, (k + 1) * HD)
        keys = jnp.concatenate([k_ref[i, :, lanes] for i in range(OWN)], axis=0)
        values = jnp.concatenate([v_ref[i, :, lanes] for i in range(OWN)], axis=0)
        scores = jnp.where(live, nt_dot(q_ref[k], keys) * SCALE, -1e30)
        peaks = jnp.max(scores, axis=1, keepdims=True)
        weights = jnp.where(live, jnp.exp(scores - peaks), 0.0)
        totals = jnp.sum(weights, axis=1, keepdims=True)
        weighted = jnp.dot(weights.astype(jnp.bfloat16), values, preferred_element_type=jnp.float32)
        out_ref[k] = weighted / totals
        lse_ref[k] = jnp.broadcast_to(peaks + jnp.log(totals), (UNIT, HD))


def attend_suffix(lengths, q_units, suffix_keys, suffix_values):
    vmem = pl.BlockSpec(memory_space=pltpu.VMEM)
    shape = jax.ShapeDtypeStruct((KVH, UNIT, HD), jnp.float32)
    return pl.pallas_call(
        suffix_kernel,
        out_shape=(shape, shape),
        in_specs=[pl.BlockSpec(memory_space=pltpu.SMEM), vmem, vmem, vmem],
        out_specs=(vmem, vmem),
        compiler_params=pltpu.CompilerParams(vmem_limit_bytes=VMEM_LIMIT),
        cost_estimate=pl.CostEstimate(
            flops=4 * KVH * UNIT * OWN * SUF * HD, bytes_accessed=2 << 20, transcendentals=KVH * UNIT * OWN * SUF
        ),
        name="attend_suffix",
    )(lengths, q_units, suffix_keys, suffix_values)


def merge_kernel(head_start, heads, parts_ref, out_suf_ref, lse_suf_ref, out_ref):
    stats = parts_ref[:, heads].astype(jnp.float32).reshape(MEMBERS * UNIT, HD)
    lse = stats + pltpu.roll(stats, HD - KVH, 1) + pltpu.roll(stats, HD - 2 * KVH, 1)
    for k in range(heads):
        own_lse = lse_suf_ref[head_start + k]
        column = jnp.broadcast_to(lse[:, k : k + 1], (MEMBERS * UNIT, HD)).reshape(MEMBERS, UNIT, HD)
        top = jnp.maximum(jnp.max(column, axis=0), own_lse)
        factor = jnp.exp(column - top[None])
        own_factor = jnp.exp(own_lse - top)
        weighted = jnp.sum(parts_ref[:, k].astype(jnp.float32) * factor, axis=0)
        weighted = weighted + out_suf_ref[head_start + k] * own_factor
        totals = jnp.sum(factor, axis=0) + own_factor
        out_ref[k] = (weighted / totals).astype(jnp.bfloat16)


def merge(head_start, heads, parts, out_suf, lse_suf):
    vmem = pl.BlockSpec(memory_space=pltpu.VMEM)
    return pl.pallas_call(
        functools.partial(merge_kernel, head_start, heads),
        out_shape=jax.ShapeDtypeStruct((heads, UNIT, HD), jnp.bfloat16),
        in_specs=[vmem] * 3,
        out_specs=vmem,
        compiler_params=pltpu.CompilerParams(vmem_limit_bytes=VMEM_LIMIT),
        cost_estimate=pl.CostEstimate(
            flops=4 * MEMBERS * heads * UNIT * HD, bytes_accessed=2 * MEMBERS * heads * UNIT * HD, transcendentals=0
        ),
        name="merge",
    )(parts, out_suf, lse_suf)


def per_device(
    queries,
    root_keys,
    root_values,
    prefix_keys,
    prefix_values,
    page_table,
    task_ids,
    suffix_keys,
    suffix_values,
    suffix_lengths,
):
    q_units = queries.reshape(OWN, KVH, QPK, HD).transpose(1, 0, 2, 3).reshape(KVH, UNIT, HD)
    pieces = gather_root(jnp.stack((root_keys, root_values)))
    q_tiled = jnp.broadcast_to(q_units[None], (MEMBERS, KVH, UNIT, HD))
    q_all = lax.all_to_all(q_tiled, "dev", 0, 0)
    out_suf, lse_suf = attend_suffix(suffix_lengths, q_units, suffix_keys, suffix_values)
    outs = []
    for head_start, heads in O_CHUNKS:
        part = attend(
            head_start, heads, task_ids, page_table[:, 0], q_all, pieces, prefix_keys[0, 0], prefix_values[0, 0]
        )
        parts = lax.all_to_all(part, "dev", 0, 0)
        outs.append(merge(head_start, heads, parts, out_suf, lse_suf))
    merged = jnp.concatenate(outs, axis=0)
    return merged.reshape(KVH, OWN, QPK, HD).transpose(1, 0, 2, 3).reshape(OWN, KVH * QPK * HD)


def solution(mesh):
    placed = (
        P(("grp", "dev"), None),
        P(("grp", "dev"), None),
        P(("grp", "dev"), None),
        P("grp", "dev", None, None, None),
        P("grp", "dev", None, None, None),
        P(None, "dev", None),
        P("grp"),
        P(("grp", "dev"), None, None),
        P(("grp", "dev"), None, None),
        P(("grp", "dev")),
    )
    return jax.shard_map(
        per_device, mesh=mesh, in_specs=placed, out_specs=P(("grp", "dev"), None), check_vma=False
    )
```

time: 462 us -> 158 us (0.34)
  waiting for transfers between devices: 292 us -> 37.4 us
  matrix products: 76.2 us -> 0 us
  Pallas kernels: 0 us -> 37.2 us
  other arithmetic: 36.3 us -> 1.12 us
  starting transfers between devices: 19.7 us -> 45.7 us
  between operations: 14.3 us -> 0.86 us
  local copies, waits for them, and re-layouts: 22.2 us -> 33.4 us
    ppermute x15, waiting for transfers between devices: 183 us -> 22.7 us  [the longest x2 16.2 us: along_y(): return lax.ppermute(array, 'grp', grp_pairs(lambda x, y, c: (x, 1 - y, c)))]
    dot_general x36 -> x0, matrix products: 76.2 us -> none  [the longest x17 60.1 us: partial_attention(): jnp.einsum('rkgt,tkd->rkgd', weights.astype(jnp.bfloat16), value_heads, p...]
    all_gather x1 -> x0, waiting for transfers between devices: 65.5 us -> none  [per_device(): group_queries = lax.all_gather(queries, 'dev', axis=0, tiled=True)]
    pallas_call x0 -> x5, Pallas kernels: none -> 37.2 us  [the longest x2 33.4 us: attend(): pl.pallas_call(functools.partial(attention_kernel, head_start, heads, len...]
    convert_element_type x15 -> x0, other arithmetic: 27.6 us -> none  [partial_attention(): weights.astype(jnp.bfloat16)]
    all_to_all x3, waiting for transfers between devices: 42.2 us -> 14.7 us  [the longest x2 14.7 us: per_device(): parts = lax.all_to_all(part, 'dev', 0, 0)]
    unnamed x33 -> x75, local copies, waits for them, and re-layouts: 5.59 us -> 32.2 us
    ppermute x15, starting transfers between devices: 1.17 us -> 15.8 us  [the longest x5 11.2 us: along_x(): lax.ppermute(array, 'grp', grp_pairs(lambda x, y, c: (x + 1 - 2 * c, y, c)))]
  transfers between devices with their start and end apart: 19 -> 18, of which waited for: 19 -> 5; matrix products, arithmetic and copies ran while one was open for 3% -> 1% of each run, Pallas kernels for 0% -> 13%
where the time goes in v1:
time: 158 us; the launch traced here: 156 us
  starting transfers between devices  45.7 us (29%)
  waiting for transfers between devices  37.4 us (24%)
  Pallas kernels  37.2 us (24%)
  local copies, waits for them, and re-layouts  33.4 us (21%)
    pallas_call x2, Pallas kernels, attend(): pl.pallas_call(functools.partial(attention_kernel, head_start, heads, len...  33.4 us
    unnamed x75, local copies, waits for them, and re-layouts  32.2 us
    all_to_all x2, starting transfers between devices, per_device(): parts = lax.all_to_all(part, 'dev', 0, 0)  19.9 us
    ppermute x2, waiting for transfers between devices, along_y(): return lax.ppermute(array, 'grp', grp_pairs(lambda x, y, c: (x, 1 - y, c)))  16.2 us
    all_to_all x2, waiting for transfers between devices, per_device(): parts = lax.all_to_all(part, 'dev', 0, 0)  14.7 us
    ppermute x5, starting transfers between devices, along_x(): lax.ppermute(array, 'grp', grp_pairs(lambda x, y, c: (x + 1 - 2 * c, y, c)))  11.2 us
    all_to_all x1, starting transfers between devices, per_device(): q_all = lax.all_to_all(q_tiled, 'dev', 0, 0)  10.1 us
    ppermute x5, waiting for transfers between devices, along_x(): lax.ppermute(array, 'grp', grp_pairs(lambda x, y, c: (x + 1 - 2 * c, y, c)))  6.46 us
  transfers between devices with their start and end apart: 18, of which 5 were waited for; matrix products, arithmetic and copies ran while one was open for 1% of the time, Pallas kernels for 13%

profile of v1, /device:TPU:8, one launch (start us, length us, event | category | flops | bytes accessed | tf_op | source)
XLA Modules:
  0.0 155.6 jit_solution(15061899789377018865)
XLA Ops:
  0.0 1.1 pad_maximum_fusion.refs_3_
  1.1 1.6 %collective-permute-start.3 = (bf16[2,128,1024]{2,1,0:T(8,128)(2,1)S(1)}, bf16[2,128,1024]{2,1,0:T(8,128)(2,1)S(1)}, u32[]{:S(2)}, u32[]{:S(2)}) collective-permute-start(bf16[2,128,1024]{2,1,0:T(8,128)(2,1)S(1)} %pad_maximum_fusion.refs_3_), channel_id=1, source_target_pairs={{0,64},{16,208},{32,96},{48,240},{64,128},{80,16},{96,160},{112,48... | collective-permute-start | bytes 1572872 | tf_op jit(solution)/shard_map/ppermute | solution.py:47
  2.7 2.3 %collective-permute-start.1 = (bf16[2,128,1024]{2,1,0:T(8,128)(2,1)S(1)}, bf16[2,128,1024]{2,1,0:T(8,128)(2,1)}, u32[]{:S(2)}, u32[]{:S(2)}) collective-permute-start(bf16[2,128,1024]{2,1,0:T(8,128)(2,1)S(1)} %pad_maximum_fusion.refs_3_), channel_id=1, source_target_pairs={{0,32},{16,48},{32,0},{48,16},{64,96},{80,112},{96,64},{112,80},{1... | collective-permute-start | bytes 1572872 | tf_op jit(solution)/shard_map/ppermute | solution.py:43
  5.0 1.2 broadcast_in_dim.8
  6.2 10.1 %all-to-all-start = ((bf16[16,8,32,128]{3,2,1,0:T(8,128)(2,1)}), bf16[16,8,32,128]{3,2,1,0:T(8,128)(2,1)S(1)}, u32[]{:S(2)}, u32[]{:S(2)}) async-start(bf16[16,8,32,128]{3,2,1,0:T(8,128)(2,1)} %broadcast_in_dim.8), calls=%async_computation | async-start | bytes 2097152 | tf_op jit(solution)/shard_map/all_to_all | solution.py:234
  16.3 1.3 collective-permute-start.6
  17.7 1.4 collective-permute-done.1.refs_5_
  19.3 1.2 collective-permute-start.4
  21.7 14.7 %collective-permute-done.6.refs_10_ = bf16[2,128,1024]{2,1,0:T(8,128)(2,1)S(1)} collective-permute-done((bf16[2,128,1024]{2,1,0:T(8,128)(2,1)S(1)}, bf16[2,128,1024]{2,1,0:T(8,128)(2,1)S(1)}, u32[]{:S(2)}, u32[]{:S(2)}) %collective-permute-start.6) | collective-permute-done | bytes 524320 | tf_op jit(solution)/shard_map/ppermute | solution.py:43
  36.4 7.0 %collective-permute-start.8 = (bf16[2,128,1024]{2,1,0:T(8,128)(2,1)S(1)}, bf16[2,128,1024]{2,1,0:T(8,128)(2,1)}, u32[]{:S(2)}, u32[]{:S(2)}) collective-permute-start(bf16[2,128,1024]{2,1,0:T(8,128)(2,1)S(1)} %collective-permute-done.6.refs_10_), channel_id=1, source_target_pairs={{0,64},{16,208},{32,96},{48,240},{64,128},{80,16},{96,160},{112,48... | collective-permute-start | bytes 1572872 | tf_op jit(solution)/shard_map/ppermute | solution.py:47
  43.4 1.3 collective-permute-start.7
  50.1 5.6 %collective-permute-done.7.refs_11_ = bf16[2,128,1024]{2,1,0:T(8,128)(2,1)} collective-permute-done((bf16[2,128,1024]{2,1,0:T(8,128)(2,1)S(1)}, bf16[2,128,1024]{2,1,0:T(8,128)(2,1)}, u32[]{:S(2)}, u32[]{:S(2)}) %collective-permute-start.7) | collective-permute-done | bytes 524320 | tf_op jit(solution)/shard_map/ppermute | solution.py:47
  59.6 1.2 copy-done.1
  61.9 1.0 copy-done.9
  62.9 1.0 copy-done.12
  64.0 1.0 copy-done.15
  66.0 1.0 copy-done.21
  67.1 1.0 copy-done.24
  68.1 1.0 copy-done.27
  70.2 16.7 %attend.2 = bf16[16,5,32,128]{3,2,1,0:T(8,128)(2,1)} custom-call(s32[1]{0:T(128)S(6)} %copy.21.refs_0_, s32[4,4]{1,0:T(4,128)S(1)} %bitcast.29, bf16[16,8,32,128]{3,2,1,0:T(8,128)(2,1)S(1)} %all-to-all-done.refs_2_, bf16[2,128,1024]{2,1,0:T(8,128)(2,1)S(1)} %pad_maximum_fusion.refs_3_, bf16[2,128,1024]{2,1,0:T(8,128)(2,1)S(1)} %copy-done.6, ...), custom_call_target="tpu_custom_call" | custom-call | flops 2415919104 | bytes 4718592 | tf_op jit(solution)/shard_map/attend/pallas_call | solution.py:131
  87.0 11.6 %all-to-all-start.1 = ((bf16[16,5,32,128]{3,2,1,0:T(8,128)(2,1)}), bf16[16,5,32,128]{3,2,1,0:T(8,128)(2,1)S(1)}, u32[]{:S(2)}, u32[]{:S(2)}) async-start(bf16[16,5,32,128]{3,2,1,0:T(8,128)(2,1)} %attend.2), calls=%async_computation.1 | async-start | bytes 1310720 | tf_op jit(solution)/shard_map/all_to_all | solution.py:241
  98.6 1.2 copy-done.2
  99.8 1.0 copy-done.4
  101.9 1.0 copy-done.10
  102.9 1.0 copy-done.13
  106.1 1.0 copy-done.22
  107.1 1.0 copy-done.25
  110.2 16.7 %attend.3 = bf16[16,5,32,128]{3,2,1,0:T(8,128)(2,1)} custom-call(s32[1]{0:T(128)S(6)} %copy.21.refs_0_, s32[4,4]{1,0:T(4,128)S(1)} %bitcast.30, bf16[16,8,32,128]{3,2,1,0:T(8,128)(2,1)S(1)} %all-to-all-done.refs_2_, bf16[2,128,1024]{2,1,0:T(8,128)(2,1)S(1)} %pad_maximum_fusion.refs_3_, bf16[2,128,1024]{2,1,0:T(8,128)(2,1)S(1)} %copy-done.7, ...), custom_call_target="tpu_custom_call" | custom-call | flops 2415919104 | bytes 4718592 | tf_op jit(solution)/shard_map/attend/pallas_call | solution.py:131
  127.0 8.3 %all-to-all-start.2 = ((bf16[16,5,32,128]{3,2,1,0:T(8,128)(2,1)}), bf16[16,5,32,128]{3,2,1,0:T(8,128)(2,1)S(1)}, u32[]{:S(2)}, u32[]{:S(2)}) async-start(bf16[16,5,32,128]{3,2,1,0:T(8,128)(2,1)} %attend.3), calls=%async_computation.2 | async-start | bytes 1310720 | tf_op jit(solution)/shard_map/all_to_all | solution.py:241
  135.3 1.2 copy-done.33
  136.5 2.6 %attend_suffix.1 = (f32[8,32,128]{2,1,0:T(8,128)S(1)}, f32[8,32,128]{2,1,0:T(8,128)S(1)}) custom-call(s32[4]{0:T(128)S(1)} %copy-done.35, bf16[8,32,128]{2,1,0:T(8,128)(2,1)S(1)} %copy_bitcast_fusion.3.q_ref, bf16[4,128,1024]{2,1,0:T(8,128)(2,1)S(1)} %copy-done.32, bf16[4,128,1024]{2,1,0:T(8,128)(2,1)S(1)} %copy-done.33), custom_call_target="tpu_custom_call" | custom-call | flops 67108864 | bytes 2097152 | tf_op jit(solution)/shard_map/attend_suffix/pallas_call | solution.py:176
  139.7 14.7 %all-to-all-done.2.parts_ref = bf16[16,5,32,128]{3,2,1,0:T(8,128)(2,1)S(1)} async-done(((bf16[16,5,32,128]{3,2,1,0:T(8,128)(2,1)}), bf16[16,5,32,128]{3,2,1,0:T(8,128)(2,1)S(1)}, u32[]{:S(2)}, u32[]{:S(2)}) %all-to-all-start.2) | async-done | bytes 655392 | tf_op jit(solution)/shard_map/all_to_all | solution.py:241
  (88 shorter events, 20.2 us)
Async XLA Ops:
  0.0 5.0 %copy-start.36 = (bf16[4,8192]{1,0:T(4,128)(2,1)S(1)}, bf16[4,8192]{1,0:T(4,128)(2,1)}, u32[]{:S(2)}) copy-start(bf16[4,8192]{1,0:T(4,128)(2,1)} %param.10) | copy-start | bytes 196612
  1.1 15.2 %collective-permute-start.3 = (bf16[2,128,1024]{2,1,0:T(8,128)(2,1)S(1)}, bf16[2,128,1024]{2,1,0:T(8,128)(2,1)S(1)}, u32[]{:S(2)}, u32[]{:S(2)}) collective-permute-start(bf16[2,128,1024]{2,1,0:T(8,128)(2,1)S(1)} %pad_maximum_fusion.refs_3_), channel_id=1, source_target_pairs={{0,64},{16,208},{32,96},{48,240},{64,128},{80,16},{96,160},{112,48... | collective-permute-start | bytes 1572872 | tf_op jit(solution)/shard_map/ppermute | solution.py:47
  2.7 16.4 %collective-permute-start.1 = (bf16[2,128,1024]{2,1,0:T(8,128)(2,1)S(1)}, bf16[2,128,1024]{2,1,0:T(8,128)(2,1)}, u32[]{:S(2)}, u32[]{:S(2)}) collective-permute-start(bf16[2,128,1024]{2,1,0:T(8,128)(2,1)S(1)} %pad_maximum_fusion.refs_3_), channel_id=1, source_target_pairs={{0,32},{16,48},{32,0},{48,16},{64,96},{80,112},{96,64},{112,80},{1... | collective-permute-start | bytes 1572872 | tf_op jit(solution)/shard_map/ppermute | solution.py:43
  6.2 52.7 %copy-start = (bf16[1,1,8,64,1024]{4,3,2,1,0:T(8,128)(2,1)S(1)}, bf16[1,1,8,64,1024]{4,3,2,1,0:T(8,128)(2,1)}, u32[]{:S(2)}) copy-start(bf16[1,1,8,64,1024]{4,3,2,1,0:T(8,128)(2,1)} %param.13) | copy-start | bytes 3145732
  6.2 52.7 %all-to-all-start = ((bf16[16,8,32,128]{3,2,1,0:T(8,128)(2,1)}), bf16[16,8,32,128]{3,2,1,0:T(8,128)(2,1)S(1)}, u32[]{:S(2)}, u32[]{:S(2)}) async-start(bf16[16,8,32,128]{3,2,1,0:T(8,128)(2,1)} %broadcast_in_dim.8), calls=%async_computation | async-start | bytes 2097152 | tf_op jit(solution)/shard_map/all_to_all | solution.py:234
  16.3 3.0 %collective-permute-start = (bf16[2,128,1024]{2,1,0:T(8,128)(2,1)S(1)}, bf16[2,128,1024]{2,1,0:T(8,128)(2,1)S(1)}, u32[]{:S(2)}, u32[]{:S(2)}) collective-permute-start(bf16[2,128,1024]{2,1,0:T(8,128)(2,1)S(1)} %pad_maximum_fusion.refs_3_), channel_id=1, source_target_pairs={{0,16},{16,0},{32,48},{48,32},{64,80},{80,64},{96,112},{112,96},{1... | collective-permute-start | bytes 1572872 | tf_op jit(solution)/shard_map/ppermute | solution.py:39
  16.3 70.6 %copy-start.3 = (bf16[2,128,1024]{2,1,0:T(8,128)(2,1)}, bf16[2,128,1024]{2,1,0:T(8,128)(2,1)S(1)}, u32[]{:S(2)}) copy-start(bf16[2,128,1024]{2,1,0:T(8,128)(2,1)S(1)} %collective-permute-done.3.refs_7_) | copy-start | bytes 1572868
  16.3 20.1 %collective-permute-start.6 = (bf16[2,128,1024]{2,1,0:T(8,128)(2,1)S(1)}, bf16[2,128,1024]{2,1,0:T(8,128)(2,1)S(1)}, u32[]{:S(2)}, u32[]{:S(2)}) collective-permute-start(bf16[2,128,1024]{2,1,0:T(8,128)(2,1)S(1)} %collective-permute-done.3.refs_7_), channel_id=1, source_target_pairs={{0,32},{16,48},{32,0},{48,16},{64,96},{80,112},{96,64},{112,80},{1... | collective-permute-start | bytes 1572872 | tf_op jit(solution)/shard_map/ppermute | solution.py:43
  19.1 24.3 %collective-permute-start.2 = (bf16[2,128,1024]{2,1,0:T(8,128)(2,1)}, bf16[2,128,1024]{2,1,0:T(8,128)(2,1)S(1)}, u32[]{:S(2)}, u32[]{:S(2)}) collective-permute-start(bf16[2,128,1024]{2,1,0:T(8,128)(2,1)} %collective-permute-done.1.refs_5_), channel_id=1, source_target_pairs={{0,16},{16,0},{32,48},{48,32},{64,80},{80,64},{96,112},{112,96},{1... | collective-permute-start | bytes 1572872 | tf_op jit(solution)/shard_map/ppermute | solution.py:39
  19.1 26.4 %collective-permute-start.5 = (bf16[2,128,1024]{2,1,0:T(8,128)(2,1)S(1)}, bf16[2,128,1024]{2,1,0:T(8,128)(2,1)S(1)}, u32[]{:S(2)}, u32[]{:S(2)}) collective-permute-start(bf16[2,128,1024]{2,1,0:T(8,128)(2,1)S(1)} %collective-permute-done.3.refs_7_), channel_id=1, source_target_pairs={{0,64},{16,208},{32,96},{48,240},{64,128},{80,16},{96,160},{112,48... | collective-permute-start | bytes 1572872 | tf_op jit(solution)/shard_map/ppermute | solution.py:47
  19.3 27.0 %collective-permute-start.4 = (bf16[2,128,1024]{2,1,0:T(8,128)(2,1)S(1)}, bf16[2,128,1024]{2,1,0:T(8,128)(2,1)S(1)}, u32[]{:S(2)}, u32[]{:S(2)}) collective-permute-start(bf16[2,128,1024]{2,1,0:T(8,128)(2,1)S(1)} %collective-permute-done.refs_4_), channel_id=1, source_target_pairs={{0,64},{16,208},{32,96},{48,240},{64,128},{80,16},{96,160},{112,48... | collective-permute-start | bytes 1572872 | tf_op jit(solution)/shard_map/ppermute | solution.py:47
  21.3 26.4 %collective-permute-start.9 = (bf16[2,128,1024]{2,1,0:T(8,128)(2,1)S(1)}, bf16[2,128,1024]{2,1,0:T(8,128)(2,1)S(1)}, u32[]{:S(2)}, u32[]{:S(2)}) collective-permute-start(bf16[2,128,1024]{2,1,0:T(8,128)(2,1)S(1)} %collective-permute-done.3.refs_7_), channel_id=1, source_target_pairs={{0,16},{16,0},{32,48},{48,32},{64,80},{80,64},{96,112},{112,96},{1... | collective-permute-start | bytes 1572872 | tf_op jit(solution)/shard_map/ppermute | solution.py:39
  36.4 13.7 %collective-permute-start.8 = (bf16[2,128,1024]{2,1,0:T(8,128)(2,1)S(1)}, bf16[2,128,1024]{2,1,0:T(8,128)(2,1)}, u32[]{:S(2)}, u32[]{:S(2)}) collective-permute-start(bf16[2,128,1024]{2,1,0:T(8,128)(2,1)S(1)} %collective-permute-done.6.refs_10_), channel_id=1, source_target_pairs={{0,64},{16,208},{32,96},{48,240},{64,128},{80,16},{96,160},{112,48... | collective-permute-start | bytes 1572872 | tf_op jit(solution)/shard_map/ppermute | solution.py:47
  43.4 12.3 %collective-permute-start.7 = (bf16[2,128,1024]{2,1,0:T(8,128)(2,1)S(1)}, bf16[2,128,1024]{2,1,0:T(8,128)(2,1)}, u32[]{:S(2)}, u32[]{:S(2)}) collective-permute-start(bf16[2,128,1024]{2,1,0:T(8,128)(2,1)S(1)} %collective-permute-done.2.refs_6_), channel_id=1, source_target_pairs={{0,64},{16,208},{32,96},{48,240},{64,128},{80,16},{96,160},{112,48... | collective-permute-start | bytes 1572872 | tf_op jit(solution)/shard_map/ppermute | solution.py:47
  45.5 10.9 %collective-permute-start.12 = (bf16[2,128,1024]{2,1,0:T(8,128)(2,1)S(1)}, bf16[2,128,1024]{2,1,0:T(8,128)(2,1)S(1)}, u32[]{:S(2)}, u32[]{:S(2)}) collective-permute-start(bf16[2,128,1024]{2,1,0:T(8,128)(2,1)S(1)} %collective-permute-done.6.refs_10_), channel_id=1, source_target_pairs={{0,16},{16,0},{32,48},{48,32},{64,80},{80,64},{96,112},{112,96},{1... | collective-permute-start | bytes 1572872 | tf_op jit(solution)/shard_map/ppermute | solution.py:39
  46.4 10.9 %collective-permute-start.11 = (bf16[2,128,1024]{2,1,0:T(8,128)(2,1)S(1)}, bf16[2,128,1024]{2,1,0:T(8,128)(2,1)S(1)}, u32[]{:S(2)}, u32[]{:S(2)}) collective-permute-start(bf16[2,128,1024]{2,1,0:T(8,128)(2,1)S(1)} %collective-permute-done.5.refs_9_), channel_id=1, source_target_pairs={{0,16},{16,0},{32,48},{48,32},{64,80},{80,64},{96,112},{112,96},{1... | collective-permute-start | bytes 1572872 | tf_op jit(solution)/shard_map/ppermute | solution.py:39
  48.5 9.6 %collective-permute-start.10 = (bf16[2,128,1024]{2,1,0:T(8,128)(2,1)S(1)}, bf16[2,128,1024]{2,1,0:T(8,128)(2,1)S(1)}, u32[]{:S(2)}, u32[]{:S(2)}) collective-permute-start(bf16[2,128,1024]{2,1,0:T(8,128)(2,1)S(1)} %collective-permute-done.4.refs_8_), channel_id=1, source_target_pairs={{0,16},{16,0},{32,48},{48,32},{64,80},{80,64},{96,112},{112,96},{1... | collective-permute-start | bytes 1572872 | tf_op jit(solution)/shard_map/ppermute | solution.py:39
  50.1 8.8 %collective-permute-start.14 = (bf16[2,128,1024]{2,1,0:T(8,128)(2,1)}, bf16[2,128,1024]{2,1,0:T(8,128)(2,1)}, u32[]{:S(2)}, u32[]{:S(2)}) collective-permute-start(bf16[2,128,1024]{2,1,0:T(8,128)(2,1)} %collective-permute-done.8.refs_12_), channel_id=1, source_target_pairs={{0,16},{16,0},{32,48},{48,32},{64,80},{80,64},{96,112},{112,96},{1... | collective-permute-start | bytes 1572872 | tf_op jit(solution)/shard_map/ppermute | solution.py:39
  55.7 3.2 %collective-permute-start.13 = (bf16[2,128,1024]{2,1,0:T(8,128)(2,1)}, bf16[2,128,1024]{2,1,0:T(8,128)(2,1)}, u32[]{:S(2)}, u32[]{:S(2)}) collective-permute-start(bf16[2,128,1024]{2,1,0:T(8,128)(2,1)} %collective-permute-done.7.refs_11_), channel_id=1, source_target_pairs={{0,16},{16,0},{32,48},{48,32},{64,80},{80,64},{96,112},{112,96},{1... | collective-permute-start | bytes 1572872 | tf_op jit(solution)/shard_map/ppermute | solution.py:39
  59.6 1.2 copy-start.1
  60.8 1.0 copy-start.6
  61.9 1.0 copy-start.9
  62.9 1.0 copy-start.12
  64.0 1.0 copy-start.15
  65.0 1.0 copy-start.18
  66.0 1.0 copy-start.21
  87.0 40.0 %all-to-all-start.1 = ((bf16[16,5,32,128]{3,2,1,0:T(8,128)(2,1)}), bf16[16,5,32,128]{3,2,1,0:T(8,128)(2,1)S(1)}, u32[]{:S(2)}, u32[]{:S(2)}) async-start(bf16[16,5,32,128]{3,2,1,0:T(8,128)(2,1)} %attend.2), calls=%async_computation.1 | async-start | bytes 1310720 | tf_op jit(solution)/shard_map/all_to_all | solution.py:241
  98.6 1.2 copy-start.2
  126.9 8.3 %copy-start.32 = (bf16[4,128,1024]{2,1,0:T(8,128)(2,1)S(1)}, bf16[4,128,1024]{2,1,0:T(8,128)(2,1)}, u32[]{:S(2)}) copy-start(bf16[4,128,1024]{2,1,0:T(8,128)(2,1)} %k_ref.1) | copy-start | bytes 3145732
  126.9 8.3 %copy-start.35 = (s32[4]{0:T(128)S(1)}, s32[4]{0:T(128)}, u32[]{:S(2)}) copy-start(s32[4]{0:T(128)} %length_ref.1) | copy-start | bytes 52
  127.0 27.4 %all-to-all-start.2 = ((bf16[16,5,32,128]{3,2,1,0:T(8,128)(2,1)}), bf16[16,5,32,128]{3,2,1,0:T(8,128)(2,1)S(1)}, u32[]{:S(2)}, u32[]{:S(2)}) async-start(bf16[16,5,32,128]{3,2,1,0:T(8,128)(2,1)} %attend.3), calls=%async_computation.2 | async-start | bytes 1310720 | tf_op jit(solution)/shard_map/all_to_all | solution.py:241
  135.2 1.2 copy-start.33
  (23 other events, 21.6 us)

commit v2 on v1

v2 whole, which is shorter than its diff:
```python
import functools

import jax
import jax.numpy as jnp
from jax import lax
from jax.experimental import pallas as pl
from jax.experimental.pallas import tpu as pltpu
from jax.sharding import PartitionSpec as P

HD = 128
KVH = 8
QPK = 8
MEMBERS = 16
OWN = 4
UNIT = OWN * QPK
SUF = 128
PPD = 4
PAGE = 64
SCALE = HD ** (-0.5)
LOG2E = 1.4426950408889634
ROWS_ALL = MEMBERS * UNIT
VMEM_LIMIT = 16 * 1024 * 1024
ATTEND_VMEM = 60 * 1024 * 1024
PARTS = 2
STEPS = 3


def grp_index(x, y_hi, core):
    return (x % 4) * 4 + (y_hi % 2) * 2 + core


def grp_pairs(target):
    return [
        (grp_index(x, y, c), grp_index(*target(x, y, c)))
        for x in range(4)
        for y in range(2)
        for c in range(2)
    ]


def to_other_core(array):
    return lax.ppermute(array, "grp", grp_pairs(lambda x, y, c: (x, y, 1 - c)))


def along_y(array):
    return lax.ppermute(array, "grp", grp_pairs(lambda x, y, c: (x, 1 - y, c)))


def along_x(array):
    return lax.ppermute(array, "grp", grp_pairs(lambda x, y, c: (x + 1 - 2 * c, y, c)))


def after(array, *others):
    return lax.optimization_barrier((array, *others))[0]


def gather_root(own):
    other = to_other_core(own)
    near = along_x(own)
    across = along_y(own)
    near_other = along_x(other)
    far = along_x(near)
    across = after(across, near_other)
    across_near = along_x(across)
    across_other = to_other_core(across)
    across_near_other = along_x(across_other)
    across_far = along_x(across_near)
    received = [near, near_other, far, across_near, across_near_other, across_far]
    return [own, other, across, across_other] + received + [to_other_core(r) for r in received]


def nt_dot(a, b):
    return lax.dot_general(a, b, (((1,), (1,)), ((), ())), preferred_element_type=jnp.float32)


def split_three(value):
    first = value.astype(jnp.bfloat16)
    rest = value - first.astype(jnp.float32)
    second = rest.astype(jnp.bfloat16)
    third = (rest - second.astype(jnp.float32)).astype(jnp.bfloat16)
    return first, second, third


def flash_step(q, keys, values, state):
    scores = nt_dot(q, keys)
    peaks = jnp.max(scores, axis=1, keepdims=True)
    if state is not None:
        peaks = jnp.maximum(peaks, state[0])
    weights = jnp.exp2((scores - peaks) * (SCALE * LOG2E)).astype(jnp.bfloat16)
    widened = jnp.concatenate([values, jnp.ones_like(values)], axis=1)
    both = jnp.dot(weights, widened, preferred_element_type=jnp.float32)
    weighted, totals = both[:, :HD], both[:, HD:]
    if state is not None:
        factor = jnp.exp2((state[0] - peaks) * (SCALE * LOG2E))
        totals = totals + state[1] * factor
        weighted = weighted + state[2] * factor
    return peaks, totals, weighted


def attention_kernel(pieces, *refs):
    task_ref, table_ref, q_ref = refs[:3]
    piece_refs = refs[3 : 3 + pieces]
    pool_k, pool_v, out_ref, held_ref, stats_ref, sems = refs[3 + pieces :]
    task = task_ref[0]
    root_rows = 128 * pieces
    copies = []
    for part in range(PARTS):
        lanes = pl.ds(part * (KVH * HD // PARTS), KVH * HD // PARTS)
        group = []
        for i, piece in enumerate(piece_refs):
            target = held_ref.at[:, pl.ds(i * 128, 128), lanes]
            group.append(pltpu.make_async_copy(piece.at[:, :, lanes], target, sems.at[part, i]))
        for j in range(PPD):
            page = table_ref[task, j]
            rows = pl.ds(root_rows + j * PAGE, PAGE)
            for side, pool in enumerate((pool_k, pool_v)):
                target = held_ref.at[side, rows, lanes]
                sem = sems.at[part, pieces + 2 * j + side]
                group.append(pltpu.make_async_copy(pool.at[page, :, lanes], target, sem))
        copies.append(group)
    for group in copies:
        for copy in group:
            copy.start()
    stats_ref[...] = jnp.zeros_like(stats_ref)
    size = (root_rows + PPD * PAGE) // STEPS

    def one_head(k, carry):
        lanes = pl.ds(pl.multiple_of(k * HD, HD), HD)
        q = q_ref[:, k].reshape(ROWS_ALL, HD)
        state = None
        for i in range(STEPS):
            rows = slice(i * size, (i + 1) * size)
            state = flash_step(q, held_ref[0, rows, lanes], held_ref[1, rows, lanes], state)
        peaks, totals, weighted = state
        rows = pl.ds(pl.multiple_of(k * UNIT, UNIT), UNIT)
        out_ref[:, rows] = (weighted / totals).astype(jnp.bfloat16).reshape(MEMBERS, UNIT, HD)
        lse = peaks * SCALE + jnp.log(totals)
        lane = lax.broadcasted_iota(jnp.int32, (ROWS_ALL, HD), 1)
        stats_ref[...] = jnp.where(lane == k, lse, stats_ref[...])
        return carry

    for part, group in enumerate(copies):
        for copy in group:
            copy.wait()
        lax.fori_loop(part * (KVH // PARTS), (part + 1) * (KVH // PARTS), one_head, 0)
    first, second, third = split_three(stats_ref[...])
    packed = (
        first.astype(jnp.float32)
        + pltpu.roll(second.astype(jnp.float32), KVH, 1)
        + pltpu.roll(third.astype(jnp.float32), 2 * KVH, 1)
    )
    packed = packed.reshape(MEMBERS, 2, UNIT // 2, HD)
    upper = pltpu.roll(packed[:, 1].reshape(ROWS_ALL // 2, HD), HD // 2, 1)
    packed = packed[:, 0].reshape(ROWS_ALL // 2, HD) + upper
    out_ref[:, KVH * UNIT :] = packed.astype(jnp.bfloat16).reshape(MEMBERS, UNIT // 2, HD)


def attend(task, table, q_all, pieces, pool_k, pool_v):
    keys = 128 * len(pieces) + PPD * PAGE
    vmem = pl.BlockSpec(memory_space=pltpu.VMEM)
    smem = pl.BlockSpec(memory_space=pltpu.SMEM)
    hbm = pl.BlockSpec(memory_space=pl.ANY)
    return pl.pallas_call(
        functools.partial(attention_kernel, len(pieces)),
        out_shape=jax.ShapeDtypeStruct((MEMBERS, KVH * UNIT + UNIT // 2, HD), jnp.bfloat16),
        in_specs=[smem, smem, vmem] + [hbm] * len(pieces) + [hbm, hbm],
        out_specs=vmem,
        scratch_shapes=[
            pltpu.VMEM((2, keys, KVH * HD), jnp.bfloat16),
            pltpu.VMEM((ROWS_ALL, HD), jnp.float32),
            pltpu.SemaphoreType.DMA((PARTS, len(pieces) + 2 * PPD)),
        ],
        compiler_params=pltpu.CompilerParams(vmem_limit_bytes=ATTEND_VMEM),
        cost_estimate=attend_cost(keys),
        name="attend",
    )(task, table, q_all, *pieces, pool_k, pool_v)


def attend_cost(keys):
    return pl.CostEstimate(
        flops=8 * KVH * ROWS_ALL * keys * HD,
        bytes_accessed=4 * keys * KVH * HD,
        transcendentals=KVH * ROWS_ALL * keys,
    )


def suffix_kernel(length_ref, q_ref, k_ref, v_ref, out_ref, lse_ref):
    slots = OWN * SUF
    row = lax.broadcasted_iota(jnp.int32, (UNIT, slots), 0) // QPK
    slot = lax.broadcasted_iota(jnp.int32, (UNIT, slots), 1)
    live = jnp.zeros((UNIT, slots), jnp.bool_)
    for i in range(OWN):
        low = i * SUF
        live = live | ((row == i) & (slot >= low) & (slot < low + length_ref[i]))
    for k in range(KVH):
        lanes = slice(k * HD, (k + 1) * HD)
        keys = jnp.concatenate([k_ref[i, :, lanes] for i in range(OWN)], axis=0)
        values = jnp.concatenate([v_ref[i, :, lanes] for i in range(OWN)], axis=0)
        scores = jnp.where(live, nt_dot(q_ref[k], keys) * SCALE, -1e30)
        peaks = jnp.max(scores, axis=1, keepdims=True)
        weights = jnp.where(live, jnp.exp(scores - peaks), 0.0)
        totals = jnp.sum(weights, axis=1, keepdims=True)
        weighted = jnp.dot(weights.astype(jnp.bfloat16), values, preferred_element_type=jnp.float32)
        out_ref[k] = weighted / totals
        lse_ref[k] = jnp.broadcast_to(peaks + jnp.log(totals), (UNIT, HD))


def attend_suffix(lengths, q_units, suffix_keys, suffix_values):
    vmem = pl.BlockSpec(memory_space=pltpu.VMEM)
    shape = jax.ShapeDtypeStruct((KVH, UNIT, HD), jnp.float32)
    return pl.pallas_call(
        suffix_kernel,
        out_shape=(shape, shape),
        in_specs=[pl.BlockSpec(memory_space=pltpu.SMEM), vmem, vmem, vmem],
        out_specs=(vmem, vmem),
        compiler_params=pltpu.CompilerParams(vmem_limit_bytes=VMEM_LIMIT),
        cost_estimate=pl.CostEstimate(
            flops=4 * KVH * UNIT * OWN * SUF * HD, bytes_accessed=2 << 20, transcendentals=KVH * UNIT * OWN * SUF
        ),
        name="attend_suffix",
    )(lengths, q_units, suffix_keys, suffix_values)


def merge_kernel(parts_ref, out_suf_ref, lse_suf_ref, out_ref):
    stats = parts_ref[:, KVH * UNIT :].astype(jnp.float32)
    upper = pltpu.roll(stats.reshape(ROWS_ALL // 2, HD), HD // 2, 1).reshape(MEMBERS, UNIT // 2, HD)
    stats = jnp.concatenate([stats, upper], axis=1).reshape(ROWS_ALL, HD)
    lse = stats + pltpu.roll(stats, HD - KVH, 1) + pltpu.roll(stats, HD - 2 * KVH, 1)
    for k in range(KVH):
        own_lse = lse_suf_ref[k]
        column = jnp.broadcast_to(lse[:, k : k + 1], (ROWS_ALL, HD)).reshape(MEMBERS, UNIT, HD)
        top = jnp.maximum(jnp.max(column, axis=0), own_lse)
        factor = jnp.exp(column - top[None])
        own_factor = jnp.exp(own_lse - top)
        part = parts_ref[:, k * UNIT : (k + 1) * UNIT].astype(jnp.float32)
        weighted = jnp.sum(part * factor, axis=0) + out_suf_ref[k] * own_factor
        totals = jnp.sum(factor, axis=0) + own_factor
        out_ref[k] = (weighted / totals).astype(jnp.bfloat16)


def merge(parts, out_suf, lse_suf):
    vmem = pl.BlockSpec(memory_space=pltpu.VMEM)
    return pl.pallas_call(
        merge_kernel,
        out_shape=jax.ShapeDtypeStruct((KVH, UNIT, HD), jnp.bfloat16),
        in_specs=[vmem] * 3,
        out_specs=vmem,
        compiler_params=pltpu.CompilerParams(vmem_limit_bytes=VMEM_LIMIT),
        cost_estimate=pl.CostEstimate(
            flops=4 * KVH * ROWS_ALL * HD, bytes_accessed=2 * KVH * ROWS_ALL * HD, transcendentals=0
        ),
        name="merge",
    )(parts, out_suf, lse_suf)


def per_device(
    queries,
    root_keys,
    root_values,
    prefix_keys,
    prefix_values,
    page_table,
    task_ids,
    suffix_keys,
    suffix_values,
    suffix_lengths,
):
    q_units = queries.reshape(OWN, KVH, QPK, HD).transpose(1, 0, 2, 3).reshape(KVH, UNIT, HD)
    pieces = gather_root(jnp.stack((root_keys, root_values)))
    q_tiled = jnp.broadcast_to(q_units[None], (MEMBERS, KVH, UNIT, HD))
    q_all = lax.all_to_all(q_tiled, "dev", 0, 0)
    out_suf, lse_suf = attend_suffix(suffix_lengths, q_units, suffix_keys, suffix_values)
    part = attend(task_ids, page_table[:, 0], q_all, pieces, prefix_keys[0, 0], prefix_values[0, 0])
    parts = lax.all_to_all(part, "dev", 0, 0)
    merged = merge(parts, out_suf, lse_suf)
    return merged.reshape(KVH, OWN, QPK, HD).transpose(1, 0, 2, 3).reshape(OWN, KVH * QPK * HD)


def solution(mesh):
    placed = (
        P(("grp", "dev"), None),
        P(("grp", "dev"), None),
        P(("grp", "dev"), None),
        P("grp", "dev", None, None, None),
        P("grp", "dev", None, None, None),
        P(None, "dev", None),
        P("grp"),
        P(("grp", "dev"), None, None),
        P(("grp", "dev"), None, None),
        P(("grp", "dev")),
    )
    return jax.shard_map(
        per_device, mesh=mesh, in_specs=placed, out_specs=P(("grp", "dev"), None), check_vma=False
    )
```

time: 158 us -> 113 us (0.72); the launches traced: 156 us -> 113 us
  local copies, waits for them, and re-layouts: 33.4 us -> 3.81 us
  starting transfers between devices: 45.7 us -> 27.4 us
  waiting for transfers between devices: 37.4 us -> 55.3 us
  Pallas kernels: 37.2 us -> 24.5 us
    unnamed x75 -> x30, local copies, waits for them, and re-layouts: 32.2 us -> 1.78 us
    ppermute x5 -> x6, waiting for transfers between devices: 6.46 us -> 27.8 us  [along_x(): lax.ppermute(array, 'grp', grp_pairs(lambda x, y, c: (x + 1 - 2 * c, y, c)))]
    ppermute x2 -> x1, waiting for transfers between devices: 16.2 us -> 0.01 us  [along_y(): return lax.ppermute(array, 'grp', grp_pairs(lambda x, y, c: (x, 1 - y, c)))]
    pallas_call x4 -> x2, Pallas kernels: 34.5 us -> 21.8 us  [the longest x1 20.9 us: attend(): pl.pallas_call(functools.partial(attention_kernel, len(pieces)), out_shap...]
    all_to_all x2 -> x1, waiting for transfers between devices: 14.7 us -> 26.7 us  [per_device(): parts = lax.all_to_all(part, 'dev', 0, 0)]
    all_to_all x2 -> x1, starting transfers between devices: 19.9 us -> 8.26 us  [per_device(): parts = lax.all_to_all(part, 'dev', 0, 0)]
    ppermute x5 -> x6, starting transfers between devices: 11.2 us -> 6.17 us  [along_x(): lax.ppermute(array, 'grp', grp_pairs(lambda x, y, c: (x + 1 - 2 * c, y, c)))]
    ppermute x2 -> x1, starting transfers between devices: 3.62 us -> 2.38 us  [along_y(): return lax.ppermute(array, 'grp', grp_pairs(lambda x, y, c: (x, 1 - y, c)))]
  transfers between devices with their start and end apart: 18 -> 17, of which waited for: 5 -> 7; matrix products, arithmetic and copies ran while one was open for 1% -> 2% of each run, Pallas kernels for 13% -> 2%
where the time goes in v2:
time: 113 us
  waiting for transfers between devices  55.3 us (49%)
  starting transfers between devices  27.4 us (24%)
  Pallas kernels  24.5 us (22%)
  local copies, waits for them, and re-layouts  3.81 us (3%)
    ppermute x6, waiting for transfers between devices, along_x(): lax.ppermute(array, 'grp', grp_pairs(lambda x, y, c: (x + 1 - 2 * c, y, c)))  27.8 us
    all_to_all x1, waiting for transfers between devices, per_device(): parts = lax.all_to_all(part, 'dev', 0, 0)  26.7 us
    pallas_call x1, Pallas kernels, attend(): pl.pallas_call(functools.partial(attention_kernel, len(pieces)), out_shap...  20.9 us
    all_to_all x1, starting transfers between devices, per_device(): q_all = lax.all_to_all(q_tiled, 'dev', 0, 0)  9.94 us
    all_to_all x1, starting transfers between devices, per_device(): parts = lax.all_to_all(part, 'dev', 0, 0)  8.26 us
    ppermute x6, starting transfers between devices, along_x(): lax.ppermute(array, 'grp', grp_pairs(lambda x, y, c: (x + 1 - 2 * c, y, c)))  6.17 us
    pallas_call x1, Pallas kernels, attend_suffix(): pl.pallas_call(suffix_kernel, out_shape=(shape, shape), in_specs=[pl.Bloc...  2.65 us
    ppermute x1, starting transfers between devices, along_y(): return lax.ppermute(array, 'grp', grp_pairs(lambda x, y, c: (x, 1 - y, c)))  2.38 us
  transfers between devices with their start and end apart: 17, of which 7 were waited for; matrix products, arithmetic and copies ran while one was open for 2% of the time, Pallas kernels for 2%

profile of v2, /device:TPU:8, one launch (start us, length us, event | category | flops | bytes accessed | tf_op | source)
XLA Modules:
  0.0 112.8 jit_solution(113284338442362376)
XLA Ops:
  0.0 1.1 pad_maximum_fusion.refs_3_
  1.1 0.1 collective-permute-start
  1.2 2.4 %collective-permute-start.1 = (bf16[2,128,1024]{2,1,0:T(8,128)(2,1)S(1)}, bf16[2,128,1024]{2,1,0:T(8,128)(2,1)S(1)}, u32[]{:S(2)}, u32[]{:S(2)}) collective-permute-start(bf16[2,128,1024]{2,1,0:T(8,128)(2,1)S(1)} %pad_maximum_fusion.refs_3_), channel_id=1, source_target_pairs={{0,32},{16,48},{32,0},{48,16},{64,96},{80,112},{96,64},{112,80},{1... | collective-permute-start | bytes 1572872 | tf_op jit(solution)/shard_map/ppermute | solution.py:46
  3.6 1.5 %collective-permute-start.2 = (bf16[2,128,1024]{2,1,0:T(8,128)(2,1)S(1)}, bf16[2,128,1024]{2,1,0:T(8,128)(2,1)S(1)}, u32[]{:S(2)}, u32[]{:S(2)}) collective-permute-start(bf16[2,128,1024]{2,1,0:T(8,128)(2,1)S(1)} %collective-permute-done.refs_4_), channel_id=1, source_target_pairs={{0,64},{16,208},{32,96},{48,240},{64,128},{80,16},{96,160},{112,48... | collective-permute-start | bytes 1572872 | tf_op jit(solution)/shard_map/ppermute | solution.py:50
  5.1 0.8 copy_bitcast_fusion.3.q_ref
  5.9 1.2 %broadcast_in_dim.8 = bf16[16,8,32,128]{3,2,1,0:T(8,128)(2,1)} broadcast(bf16[8,32,128]{2,1,0:T(8,128)(2,1)S(1)} %copy_bitcast_fusion.3.q_ref), dimensions={1,2,3} | broadcast | bytes 1114112 | tf_op jit(solution)/shard_map/broadcast_in_dim | solution.py:270
  7.1 9.9 %all-to-all-start = ((bf16[16,8,32,128]{3,2,1,0:T(8,128)(2,1)}), bf16[16,8,32,128]{3,2,1,0:T(8,128)(2,1)S(1)}, u32[]{:S(2)}, u32[]{:S(2)}) async-start(bf16[16,8,32,128]{3,2,1,0:T(8,128)(2,1)} %broadcast_in_dim.8), calls=%async_computation | async-start | bytes 2097152 | tf_op jit(solution)/shard_map/all_to_all | solution.py:271
  17.1 1.6 %collective-permute-start.4 = (bf16[2,128,1024]{2,1,0:T(8,128)(2,1)S(1)}, bf16[2,128,1024]{2,1,0:T(8,128)(2,1)S(1)}, u32[]{:S(2)}, u32[]{:S(2)}) collective-permute-start(bf16[2,128,1024]{2,1,0:T(8,128)(2,1)S(1)} %pad_maximum_fusion.refs_3_), channel_id=1, source_target_pairs={{0,64},{16,208},{32,96},{48,240},{64,128},{80,16},{96,160},{112,48... | collective-permute-start | bytes 1572872 | tf_op jit(solution)/shard_map/ppermute | solution.py:50
  18.6 0.0 collective-permute-done.1.refs_5_
  18.6 1.3 %collective-permute-start.6 = (bf16[2,128,1024]{2,1,0:T(8,128)(2,1)S(1)}, bf16[2,128,1024]{2,1,0:T(8,128)(2,1)S(1)}, u32[]{:S(2)}, u32[]{:S(2)}) collective-permute-start(bf16[2,128,1024]{2,1,0:T(8,128)(2,1)S(1)} %collective-permute-done.1.refs_5_), channel_id=1, source_target_pairs={{0,64},{16,208},{32,96},{48,240},{64,128},{80,16},{96,160},{112,48... | collective-permute-start | bytes 1572872 | tf_op jit(solution)/shard_map/ppermute | solution.py:50
  19.9 7.6 %collective-permute-done.4.refs_7_ = bf16[2,128,1024]{2,1,0:T(8,128)(2,1)S(1)} collective-permute-done((bf16[2,128,1024]{2,1,0:T(8,128)(2,1)S(1)}, bf16[2,128,1024]{2,1,0:T(8,128)(2,1)S(1)}, u32[]{:S(2)}, u32[]{:S(2)}) %collective-permute-start.4) | collective-permute-done | bytes 524320 | tf_op jit(solution)/shard_map/ppermute | solution.py:50
  27.5 0.3 collective-permute-start.5
  27.8 5.3 %collective-permute-done.6.refs_10_ = bf16[2,128,1024]{2,1,0:T(8,128)(2,1)S(1)} collective-permute-done((bf16[2,128,1024]{2,1,0:T(8,128)(2,1)S(1)}, bf16[2,128,1024]{2,1,0:T(8,128)(2,1)S(1)}, u32[]{:S(2)}, u32[]{:S(2)}) %collective-permute-start.6) | collective-permute-done | bytes 524320 | tf_op jit(solution)/shard_map/ppermute | solution.py:50
  33.1 0.3 collective-permute-start.8
  33.4 1.3 %collective-permute-start.7 = (bf16[2,128,1024]{2,1,0:T(8,128)(2,1)S(1)}, bf16[2,128,1024]{2,1,0:T(8,128)(2,1)}, u32[]{:S(2)}, u32[]{:S(2)}) collective-permute-start(bf16[2,128,1024]{2,1,0:T(8,128)(2,1)S(1)} %collective-permute-done.3.refs_6_), channel_id=1, source_target_pairs={{0,64},{16,208},{32,96},{48,240},{64,128},{80,16},{96,160},{112,48... | collective-permute-start | bytes 1572872 | tf_op jit(solution)/shard_map/ppermute | solution.py:50
  34.7 4.1 %collective-permute-done.5.refs_9_ = bf16[2,128,1024]{2,1,0:T(8,128)(2,1)S(1)} collective-permute-done((bf16[2,128,1024]{2,1,0:T(8,128)(2,1)S(1)}, bf16[2,128,1024]{2,1,0:T(8,128)(2,1)S(1)}, u32[]{:S(2)}, u32[]{:S(2)}) %collective-permute-start.5) | collective-permute-done | bytes 524320 | tf_op jit(solution)/shard_map/ppermute | solution.py:50
  38.8 0.5 collective-permute-start.12
  39.3 5.2 %collective-permute-done.8.refs_12_ = bf16[2,128,1024]{2,1,0:T(8,128)(2,1)} collective-permute-done((bf16[2,128,1024]{2,1,0:T(8,128)(2,1)S(1)}, bf16[2,128,1024]{2,1,0:T(8,128)(2,1)}, u32[]{:S(2)}, u32[]{:S(2)}) %collective-permute-start.8) | collective-permute-done | bytes 524320 | tf_op jit(solution)/shard_map/ppermute | solution.py:50
  44.5 5.6 %collective-permute-done.7.refs_11_ = bf16[2,128,1024]{2,1,0:T(8,128)(2,1)} collective-permute-done((bf16[2,128,1024]{2,1,0:T(8,128)(2,1)S(1)}, bf16[2,128,1024]{2,1,0:T(8,128)(2,1)}, u32[]{:S(2)}, u32[]{:S(2)}) %collective-permute-start.7) | collective-permute-done | bytes 524320 | tf_op jit(solution)/shard_map/ppermute | solution.py:50
  50.1 0.0 collective-permute-start.13
  50.8 0.8 copy-done.13
  51.6 0.7 collective-permute-done.13.refs_17_
  52.4 0.2 copy-done.3
  52.6 20.9 %attend.1 = bf16[16,272,128]{2,1,0:T(8,128)(2,1)} custom-call(s32[1]{0:T(128)S(6)} %copy.21.refs_0_, s32[4,4]{1,0:T(4,128)} %bitcast.30, bf16[16,8,32,128]{3,2,1,0:T(8,128)(2,1)} %copy-done.3, bf16[2,128,1024]{2,1,0:T(8,128)(2,1)} %copy-done.4, bf16[2,128,1024]{2,1,0:T(8,128)(2,1)} %copy-done.5, bf16[2,128,1024]{2,1,0:T(8,128)(2,1)} %copy-done.6, ...), custom_call_target="tpu_custom_call" | custom-call | flops 9663676416 | bytes 9437184 | tf_op jit(solution)/shard_map/attend/pallas_call | solution.py:163
  73.5 0.0 copy-start
  73.5 0.0 copy-start.1
  73.5 0.0 copy-start.2
  73.6 8.3 %all-to-all-start.1 = ((bf16[16,272,128]{2,1,0:T(8,128)(2,1)}), bf16[16,272,128]{2,1,0:T(8,128)(2,1)S(1)}, u32[]{:S(2)}, u32[]{:S(2)}) async-start(bf16[16,272,128]{2,1,0:T(8,128)(2,1)} %attend.1), calls=%async_computation.1 | async-start | bytes 2228224 | tf_op jit(solution)/shard_map/all_to_all | solution.py:274
  81.8 2.6 %attend_suffix.1 = (f32[8,32,128]{2,1,0:T(8,128)S(1)}, f32[8,32,128]{2,1,0:T(8,128)S(1)}) custom-call(s32[4]{0:T(128)S(1)} %copy-done.2, bf16[8,32,128]{2,1,0:T(8,128)(2,1)S(1)} %copy_bitcast_fusion.3.q_ref, bf16[4,128,1024]{2,1,0:T(8,128)(2,1)S(1)} %copy-done, bf16[4,128,1024]{2,1,0:T(8,128)(2,1)S(1)} %copy-done.1), custom_call_target="tpu_custom_call" | custom-call | flops 67108864 | bytes 2097152 | tf_op jit(solution)/shard_map/attend_suffix/pallas_call | solution.py:211
  84.5 26.7 %all-to-all-done.1.parts_ref = bf16[16,272,128]{2,1,0:T(8,128)(2,1)S(1)} async-done(((bf16[16,272,128]{2,1,0:T(8,128)(2,1)}), bf16[16,272,128]{2,1,0:T(8,128)(2,1)S(1)}, u32[]{:S(2)}, u32[]{:S(2)}) %all-to-all-start.1) | async-done | bytes 1114144 | tf_op jit(solution)/shard_map/all_to_all | solution.py:274
  111.2 0.9 merge.1
  112.1 0.7 copy.20
  (38 shorter events, 0.1 us)
Async XLA Ops:
  1.1 16.0 %copy-start.4 = (bf16[2,128,1024]{2,1,0:T(8,128)(2,1)}, bf16[2,128,1024]{2,1,0:T(8,128)(2,1)S(1)}, u32[]{:S(2)}) copy-start(bf16[2,128,1024]{2,1,0:T(8,128)(2,1)S(1)} %pad_maximum_fusion.refs_3_) | copy-start | bytes 1572868
  1.1 2.5 %collective-permute-start = (bf16[2,128,1024]{2,1,0:T(8,128)(2,1)S(1)}, bf16[2,128,1024]{2,1,0:T(8,128)(2,1)S(1)}, u32[]{:S(2)}, u32[]{:S(2)}) collective-permute-start(bf16[2,128,1024]{2,1,0:T(8,128)(2,1)S(1)} %pad_maximum_fusion.refs_3_), channel_id=1, source_target_pairs={{0,16},{16,0},{32,48},{48,32},{64,80},{80,64},{96,112},{112,96},{1... | collective-permute-start | bytes 1572872 | tf_op jit(solution)/shard_map/ppermute | solution.py:42
  1.2 17.4 %collective-permute-start.1 = (bf16[2,128,1024]{2,1,0:T(8,128)(2,1)S(1)}, bf16[2,128,1024]{2,1,0:T(8,128)(2,1)S(1)}, u32[]{:S(2)}, u32[]{:S(2)}) collective-permute-start(bf16[2,128,1024]{2,1,0:T(8,128)(2,1)S(1)} %pad_maximum_fusion.refs_3_), channel_id=1, source_target_pairs={{0,32},{16,48},{32,0},{48,16},{64,96},{80,112},{96,64},{112,80},{1... | collective-permute-start | bytes 1572872 | tf_op jit(solution)/shard_map/ppermute | solution.py:46
  3.6 3.5 %copy-start.5 = (bf16[2,128,1024]{2,1,0:T(8,128)(2,1)}, bf16[2,128,1024]{2,1,0:T(8,128)(2,1)S(1)}, u32[]{:S(2)}) copy-start(bf16[2,128,1024]{2,1,0:T(8,128)(2,1)S(1)} %collective-permute-done.refs_4_) | copy-start | bytes 1572868
  3.6 15.0 %collective-permute-start.2 = (bf16[2,128,1024]{2,1,0:T(8,128)(2,1)S(1)}, bf16[2,128,1024]{2,1,0:T(8,128)(2,1)S(1)}, u32[]{:S(2)}, u32[]{:S(2)}) collective-permute-start(bf16[2,128,1024]{2,1,0:T(8,128)(2,1)S(1)} %collective-permute-done.refs_4_), channel_id=1, source_target_pairs={{0,64},{16,208},{32,96},{48,240},{64,128},{80,16},{96,160},{112,48... | collective-permute-start | bytes 1572872 | tf_op jit(solution)/shard_map/ppermute | solution.py:50
  7.1 44.5 %all-to-all-start = ((bf16[16,8,32,128]{3,2,1,0:T(8,128)(2,1)}), bf16[16,8,32,128]{3,2,1,0:T(8,128)(2,1)S(1)}, u32[]{:S(2)}, u32[]{:S(2)}) async-start(bf16[16,8,32,128]{3,2,1,0:T(8,128)(2,1)} %broadcast_in_dim.8), calls=%async_computation | async-start | bytes 2097152 | tf_op jit(solution)/shard_map/all_to_all | solution.py:271
  17.1 10.5 %collective-permute-start.4 = (bf16[2,128,1024]{2,1,0:T(8,128)(2,1)S(1)}, bf16[2,128,1024]{2,1,0:T(8,128)(2,1)S(1)}, u32[]{:S(2)}, u32[]{:S(2)}) collective-permute-start(bf16[2,128,1024]{2,1,0:T(8,128)(2,1)S(1)} %pad_maximum_fusion.refs_3_), channel_id=1, source_target_pairs={{0,64},{16,208},{32,96},{48,240},{64,128},{80,16},{96,160},{112,48... | collective-permute-start | bytes 1572872 | tf_op jit(solution)/shard_map/ppermute | solution.py:50
  18.6 33.7 %copy-start.6 = (bf16[2,128,1024]{2,1,0:T(8,128)(2,1)}, bf16[2,128,1024]{2,1,0:T(8,128)(2,1)S(1)}, u32[]{:S(2)}) copy-start(bf16[2,128,1024]{2,1,0:T(8,128)(2,1)S(1)} %collective-permute-done.1.refs_5_) | copy-start | bytes 1572868
  18.6 33.7 %copy-start.7 = (bf16[2,128,1024]{2,1,0:T(8,128)(2,1)}, bf16[2,128,1024]{2,1,0:T(8,128)(2,1)S(1)}, u32[]{:S(2)}) copy-start(bf16[2,128,1024]{2,1,0:T(8,128)(2,1)S(1)} %collective-permute-done.2.refs_8_) | copy-start | bytes 1572868
  18.6 14.5 %collective-permute-start.6 = (bf16[2,128,1024]{2,1,0:T(8,128)(2,1)S(1)}, bf16[2,128,1024]{2,1,0:T(8,128)(2,1)S(1)}, u32[]{:S(2)}, u32[]{:S(2)}) collective-permute-start(bf16[2,128,1024]{2,1,0:T(8,128)(2,1)S(1)} %collective-permute-done.1.refs_5_), channel_id=1, source_target_pairs={{0,64},{16,208},{32,96},{48,240},{64,128},{80,16},{96,160},{112,48... | collective-permute-start | bytes 1572872 | tf_op jit(solution)/shard_map/ppermute | solution.py:50
  19.9 13.5 %collective-permute-start.3 = (bf16[2,128,1024]{2,1,0:T(8,128)(2,1)S(1)}, bf16[2,128,1024]{2,1,0:T(8,128)(2,1)S(1)}, u32[]{:S(2)}, u32[]{:S(2)}) collective-permute-start(bf16[2,128,1024]{2,1,0:T(8,128)(2,1)S(1)} %collective-permute-done.1.refs_5_), channel_id=1, source_target_pairs={{0,16},{16,0},{32,48},{48,32},{64,80},{80,64},{96,112},{112,96},{1... | collective-permute-start | bytes 1572872 | tf_op jit(solution)/shard_map/ppermute | solution.py:42
  27.5 5.9 %copy-start.8 = (bf16[2,128,1024]{2,1,0:T(8,128)(2,1)}, bf16[2,128,1024]{2,1,0:T(8,128)(2,1)S(1)}, u32[]{:S(2)}) copy-start(bf16[2,128,1024]{2,1,0:T(8,128)(2,1)S(1)} %collective-permute-done.4.refs_7_) | copy-start | bytes 1572868
  27.5 11.2 %collective-permute-start.5 = (bf16[2,128,1024]{2,1,0:T(8,128)(2,1)S(1)}, bf16[2,128,1024]{2,1,0:T(8,128)(2,1)S(1)}, u32[]{:S(2)}, u32[]{:S(2)}) collective-permute-start(bf16[2,128,1024]{2,1,0:T(8,128)(2,1)S(1)} %collective-permute-done.4.refs_7_), channel_id=1, source_target_pairs={{0,64},{16,208},{32,96},{48,240},{64,128},{80,16},{96,160},{112,48... | collective-permute-start | bytes 1572872 | tf_op jit(solution)/shard_map/ppermute | solution.py:50
  27.8 11.0 %collective-permute-start.9 = (bf16[2,128,1024]{2,1,0:T(8,128)(2,1)S(1)}, bf16[2,128,1024]{2,1,0:T(8,128)(2,1)S(1)}, u32[]{:S(2)}, u32[]{:S(2)}) collective-permute-start(bf16[2,128,1024]{2,1,0:T(8,128)(2,1)S(1)} %collective-permute-done.4.refs_7_), channel_id=1, source_target_pairs={{0,16},{16,0},{32,48},{48,32},{64,80},{80,64},{96,112},{112,96},{1... | collective-permute-start | bytes 1572872 | tf_op jit(solution)/shard_map/ppermute | solution.py:42
  33.1 19.2 %copy-start.9 = (bf16[2,128,1024]{2,1,0:T(8,128)(2,1)}, bf16[2,128,1024]{2,1,0:T(8,128)(2,1)S(1)}, u32[]{:S(2)}) copy-start(bf16[2,128,1024]{2,1,0:T(8,128)(2,1)S(1)} %collective-permute-done.6.refs_10_) | copy-start | bytes 1572868
  33.1 11.3 %collective-permute-start.8 = (bf16[2,128,1024]{2,1,0:T(8,128)(2,1)S(1)}, bf16[2,128,1024]{2,1,0:T(8,128)(2,1)}, u32[]{:S(2)}, u32[]{:S(2)}) collective-permute-start(bf16[2,128,1024]{2,1,0:T(8,128)(2,1)S(1)} %collective-permute-done.6.refs_10_), channel_id=1, source_target_pairs={{0,64},{16,208},{32,96},{48,240},{64,128},{80,16},{96,160},{112,48... | collective-permute-start | bytes 1572872 | tf_op jit(solution)/shard_map/ppermute | solution.py:50
  33.4 11.1 %copy-start.10 = (bf16[2,128,1024]{2,1,0:T(8,128)(2,1)}, bf16[2,128,1024]{2,1,0:T(8,128)(2,1)S(1)}, u32[]{:S(2)}) copy-start(bf16[2,128,1024]{2,1,0:T(8,128)(2,1)S(1)} %collective-permute-done.3.refs_6_) | copy-start | bytes 1572868
  33.4 16.7 %collective-permute-start.7 = (bf16[2,128,1024]{2,1,0:T(8,128)(2,1)S(1)}, bf16[2,128,1024]{2,1,0:T(8,128)(2,1)}, u32[]{:S(2)}, u32[]{:S(2)}) collective-permute-start(bf16[2,128,1024]{2,1,0:T(8,128)(2,1)S(1)} %collective-permute-done.3.refs_6_), channel_id=1, source_target_pairs={{0,64},{16,208},{32,96},{48,240},{64,128},{80,16},{96,160},{112,48... | collective-permute-start | bytes 1572872 | tf_op jit(solution)/shard_map/ppermute | solution.py:50
  34.7 16.1 %collective-permute-start.10 = (bf16[2,128,1024]{2,1,0:T(8,128)(2,1)S(1)}, bf16[2,128,1024]{2,1,0:T(8,128)(2,1)S(1)}, u32[]{:S(2)}, u32[]{:S(2)}) collective-permute-start(bf16[2,128,1024]{2,1,0:T(8,128)(2,1)S(1)} %collective-permute-done.2.refs_8_), channel_id=1, source_target_pairs={{0,16},{16,0},{32,48},{48,32},{64,80},{80,64},{96,112},{112,96},{1... | collective-permute-start | bytes 1572872 | tf_op jit(solution)/shard_map/ppermute | solution.py:42
  38.8 13.6 %copy-start.11 = (bf16[2,128,1024]{2,1,0:T(8,128)(2,1)}, bf16[2,128,1024]{2,1,0:T(8,128)(2,1)S(1)}, u32[]{:S(2)}) copy-start(bf16[2,128,1024]{2,1,0:T(8,128)(2,1)S(1)} %collective-permute-done.5.refs_9_) | copy-start | bytes 1572868
  38.8 12.8 %collective-permute-start.11 = (bf16[2,128,1024]{2,1,0:T(8,128)(2,1)S(1)}, bf16[2,128,1024]{2,1,0:T(8,128)(2,1)}, u32[]{:S(2)}, u32[]{:S(2)}) collective-permute-start(bf16[2,128,1024]{2,1,0:T(8,128)(2,1)S(1)} %collective-permute-done.5.refs_9_), channel_id=1, source_target_pairs={{0,16},{16,0},{32,48},{48,32},{64,80},{80,64},{96,112},{112,96},{1... | collective-permute-start | bytes 1572872 | tf_op jit(solution)/shard_map/ppermute | solution.py:42
  38.8 11.3 %copy-start.12 = (bf16[2,128,1024]{2,1,0:T(8,128)(2,1)}, bf16[2,128,1024]{2,1,0:T(8,128)(2,1)S(1)}, u32[]{:S(2)}) copy-start(bf16[2,128,1024]{2,1,0:T(8,128)(2,1)S(1)} %collective-permute-done.9.refs_13_) | copy-start | bytes 1572868
  38.8 12.8 %collective-permute-start.12 = (bf16[2,128,1024]{2,1,0:T(8,128)(2,1)S(1)}, bf16[2,128,1024]{2,1,0:T(8,128)(2,1)}, u32[]{:S(2)}, u32[]{:S(2)}) collective-permute-start(bf16[2,128,1024]{2,1,0:T(8,128)(2,1)S(1)} %collective-permute-done.6.refs_10_), channel_id=1, source_target_pairs={{0,16},{16,0},{32,48},{48,32},{64,80},{80,64},{96,112},{112,96},{1... | collective-permute-start | bytes 1572872 | tf_op jit(solution)/shard_map/ppermute | solution.py:42
  44.5 7.1 %collective-permute-start.14 = (bf16[2,128,1024]{2,1,0:T(8,128)(2,1)}, bf16[2,128,1024]{2,1,0:T(8,128)(2,1)}, u32[]{:S(2)}, u32[]{:S(2)}) collective-permute-start(bf16[2,128,1024]{2,1,0:T(8,128)(2,1)} %collective-permute-done.8.refs_12_), channel_id=1, source_target_pairs={{0,16},{16,0},{32,48},{48,32},{64,80},{80,64},{96,112},{112,96},{1... | collective-permute-start | bytes 1572872 | tf_op jit(solution)/shard_map/ppermute | solution.py:42
  50.1 2.3 %collective-permute-start.13 = (bf16[2,128,1024]{2,1,0:T(8,128)(2,1)}, bf16[2,128,1024]{2,1,0:T(8,128)(2,1)}, u32[]{:S(2)}, u32[]{:S(2)}) collective-permute-start(bf16[2,128,1024]{2,1,0:T(8,128)(2,1)} %collective-permute-done.7.refs_11_), channel_id=1, source_target_pairs={{0,16},{16,0},{32,48},{48,32},{64,80},{80,64},{96,112},{112,96},{1... | collective-permute-start | bytes 1572872 | tf_op jit(solution)/shard_map/ppermute | solution.py:42
  50.8 0.8 copy-start.13
  51.6 1.0 copy-start.3
  73.5 8.3 %copy-start = (bf16[4,128,1024]{2,1,0:T(8,128)(2,1)S(1)}, bf16[4,128,1024]{2,1,0:T(8,128)(2,1)}, u32[]{:S(2)}) copy-start(bf16[4,128,1024]{2,1,0:T(8,128)(2,1)} %k_ref.1) | copy-start | bytes 3145732
  73.5 8.3 %copy-start.1 = (bf16[4,128,1024]{2,1,0:T(8,128)(2,1)S(1)}, bf16[4,128,1024]{2,1,0:T(8,128)(2,1)}, u32[]{:S(2)}) copy-start(bf16[4,128,1024]{2,1,0:T(8,128)(2,1)} %v_ref.1) | copy-start | bytes 3145732
  73.5 8.3 %copy-start.2 = (s32[4]{0:T(128)S(1)}, s32[4]{0:T(128)}, u32[]{:S(2)}) copy-start(s32[4]{0:T(128)} %length_ref.1) | copy-start | bytes 52
  73.6 37.6 %all-to-all-start.1 = ((bf16[16,272,128]{2,1,0:T(8,128)(2,1)}), bf16[16,272,128]{2,1,0:T(8,128)(2,1)S(1)}, u32[]{:S(2)}, u32[]{:S(2)}) async-start(bf16[16,272,128]{2,1,0:T(8,128)(2,1)} %attend.1), calls=%async_computation.1 | async-start | bytes 2228224 | tf_op jit(solution)/shard_map/all_to_all | solution.py:274

commit v3 on v2

--- a/solution.py
+++ b/solution.py
@@ -21,8 +21,8 @@
 ROWS_ALL = MEMBERS * UNIT
 VMEM_LIMIT = 16 * 1024 * 1024
 ATTEND_VMEM = 60 * 1024 * 1024
-PARTS = 2
-STEPS = 3
+PARTS = (2, 3, 3)
+STEPS = 2
 
 
 def grp_index(x, y_hi, core):
@@ -60,7 +60,7 @@
     across = along_y(own)
     near_other = along_x(other)
     far = along_x(near)
-    across = after(across, near_other)
+    across = after(across, near, near_other)
     across_near = along_x(across)
     across_other = to_other_core(across)
     across_near_other = along_x(across_other)
@@ -100,12 +100,14 @@
 def attention_kernel(pieces, *refs):
     task_ref, table_ref, q_ref = refs[:3]
     piece_refs = refs[3 : 3 + pieces]
-    pool_k, pool_v, out_ref, held_ref, stats_ref, sems = refs[3 + pieces :]
+    pool_k, pool_v, out_ref, held_ref, peaks_ref, totals_ref, sems = refs[3 + pieces :]
     task = task_ref[0]
     root_rows = 128 * pieces
     copies = []
-    for part in range(PARTS):
-        lanes = pl.ds(part * (KVH * HD // PARTS), KVH * HD // PARTS)
+    first_head = 0
+    for part, heads in enumerate(PARTS):
+        lanes = pl.ds(first_head * HD, heads * HD)
+        first_head += heads
         group = []
         for i, piece in enumerate(piece_refs):
             target = held_ref.at[:, pl.ds(i * 128, 128), lanes]
@@ -118,32 +120,39 @@
                 sem = sems.at[part, pieces + 2 * j + side]
                 group.append(pltpu.make_async_copy(pool.at[page, :, lanes], target, sem))
         copies.append(group)
-    for group in copies:
+    for group in copies[:2]:
         for copy in group:
             copy.start()
-    stats_ref[...] = jnp.zeros_like(stats_ref)
+    peaks_ref[...] = jnp.zeros_like(peaks_ref)
+    totals_ref[...] = jnp.ones_like(totals_ref)
     size = (root_rows + PPD * PAGE) // STEPS
-
-    def one_head(k, carry):
-        lanes = pl.ds(pl.multiple_of(k * HD, HD), HD)
+    lane = lax.broadcasted_iota(jnp.int32, (ROWS_ALL, HD), 1)
+
+    def one_head(k):
+        lanes = slice(k * HD, (k + 1) * HD)
         q = q_ref[:, k].reshape(ROWS_ALL, HD)
         state = None
         for i in range(STEPS):
             rows = slice(i * size, (i + 1) * size)
             state = flash_step(q, held_ref[0, rows, lanes], held_ref[1, rows, lanes], state)
         peaks, totals, weighted = state
-        rows = pl.ds(pl.multiple_of(k * UNIT, UNIT), UNIT)
-        out_ref[:, rows] = (weighted / totals).astype(jnp.bfloat16).reshape(MEMBERS, UNIT, HD)
-        lse = peaks * SCALE + jnp.log(totals)
-        lane = lax.broadcasted_iota(jnp.int32, (ROWS_ALL, HD), 1)
-        stats_ref[...] = jnp.where(lane == k, lse, stats_ref[...])
-        return carry
-
-    for part, group in enumerate(copies):
-        for copy in group:
+        out_ref[:, k * UNIT : (k + 1) * UNIT] = (
+            (weighted / totals).astype(jnp.bfloat16).reshape(MEMBERS, UNIT, HD)
+        )
+        peaks_ref[...] = jnp.where(lane == k, peaks, peaks_ref[...])
+        totals_ref[...] = jnp.where(lane == k, totals, totals_ref[...])
+
+    first_head = 0
+    for part, heads in enumerate(PARTS):
+        for copy in copies[part]:
             copy.wait()
-        lax.fori_loop(part * (KVH // PARTS), (part + 1) * (KVH // PARTS), one_head, 0)
-    first, second, third = split_three(stats_ref[...])
+        for k in range(first_head, first_head + heads):
+            one_head(k)
+        first_head += heads
+        if part + 2 < len(PARTS):
+            for copy in copies[part + 2]:
+                copy.start()
+    first, second, third = split_three(peaks_ref[...] * SCALE + jnp.log(totals_ref[...]))
     packed = (
         first.astype(jnp.float32)
         + pltpu.roll(second.astype(jnp.float32), KVH, 1)
@@ -168,7 +177,8 @@
         scratch_shapes=[
             pltpu.VMEM((2, keys, KVH * HD), jnp.bfloat16),
             pltpu.VMEM((ROWS_ALL, HD), jnp.float32),
-            pltpu.SemaphoreType.DMA((PARTS, len(pieces) + 2 * PPD)),
+            pltpu.VMEM((ROWS_ALL, HD), jnp.float32),
+            pltpu.SemaphoreType.DMA((len(PARTS), len(pieces) + 2 * PPD)),
         ],
         compiler_params=pltpu.CompilerParams(vmem_limit_bytes=ATTEND_VMEM),
         cost_estimate=attend_cost(keys),
@@ -186,7 +196,7 @@
 
 def suffix_kernel(length_ref, q_ref, k_ref, v_ref, out_ref, lse_ref):
     slots = OWN * SUF
-    row = lax.broadcasted_iota(jnp.int32, (UNIT, slots), 0) // QPK
+    row = lax.broadcasted_iota(jnp.int32, (UNIT, slots), 0) % OWN
     slot = lax.broadcasted_iota(jnp.int32, (UNIT, slots), 1)
     live = jnp.zeros((UNIT, slots), jnp.bool_)
     for i in range(OWN):
@@ -235,14 +245,17 @@
         part = parts_ref[:, k * UNIT : (k + 1) * UNIT].astype(jnp.float32)
         weighted = jnp.sum(part * factor, axis=0) + out_suf_ref[k] * own_factor
         totals = jnp.sum(factor, axis=0) + own_factor
-        out_ref[k] = (weighted / totals).astype(jnp.bfloat16)
+        result = (weighted / totals).astype(jnp.bfloat16)
+        for g in range(QPK):
+            head = k * QPK + g
+            out_ref[:, head * HD : (head + 1) * HD] = result[g * OWN : (g + 1) * OWN]
 
 
 def merge(parts, out_suf, lse_suf):
     vmem = pl.BlockSpec(memory_space=pltpu.VMEM)
     return pl.pallas_call(
         merge_kernel,
-        out_shape=jax.ShapeDtypeStruct((KVH, UNIT, HD), jnp.bfloat16),
+        out_shape=jax.ShapeDtypeStruct((OWN, KVH * QPK * HD), jnp.bfloat16),
         in_specs=[vmem] * 3,
         out_specs=vmem,
         compiler_params=pltpu.CompilerParams(vmem_limit_bytes=VMEM_LIMIT),
@@ -265,15 +278,14 @@
     suffix_values,
     suffix_lengths,
 ):
-    q_units = queries.reshape(OWN, KVH, QPK, HD).transpose(1, 0, 2, 3).reshape(KVH, UNIT, HD)
+    q_units = queries.reshape(OWN, KVH, QPK, HD).transpose(1, 2, 0, 3).reshape(KVH, UNIT, HD)
     pieces = gather_root(jnp.stack((root_keys, root_values)))
     q_tiled = jnp.broadcast_to(q_units[None], (MEMBERS, KVH, UNIT, HD))
     q_all = lax.all_to_all(q_tiled, "dev", 0, 0)
     out_suf, lse_suf = attend_suffix(suffix_lengths, q_units, suffix_keys, suffix_values)
     part = attend(task_ids, page_table[:, 0], q_all, pieces, prefix_keys[0, 0], prefix_values[0, 0])
     parts = lax.all_to_all(part, "dev", 0, 0)
-    merged = merge(parts, out_suf, lse_suf)
-    return merged.reshape(KVH, OWN, QPK, HD).transpose(1, 0, 2, 3).reshape(OWN, KVH * QPK * HD)
+    return merge(parts, out_suf, lse_suf)
 
 
 def solution(mesh):

time: 113 us -> 109 us (0.965)
  waiting for transfers between devices: 55.3 us -> 50.6 us
  starting transfers between devices: 27.4 us -> 29.8 us
  Pallas kernels: 24.5 us -> 22.3 us
    ppermute x6, waiting for transfers between devices: 27.8 us -> 23 us  [along_x(): lax.ppermute(array, 'grp', grp_pairs(lambda x, y, c: (x + 1 - 2 * c, y, c)))]
    pallas_call x1, Pallas kernels: 20.9 us -> 18.1 us  [attend(): pl.pallas_call(functools.partial(attention_kernel, len(pieces)), out_shap...]
    all_to_all x1, starting transfers between devices: 8.26 us -> 10.1 us  [per_device(): parts = lax.all_to_all(part, 'dev', 0, 0)]
    ppermute x8, starting transfers between devices: 0.61 us -> 2.15 us  [to_other_core(): return lax.ppermute(array, 'grp', grp_pairs(lambda x, y, c: (x, y, 1 - c)))]
where the time goes in v3:
time: 109 us; the launch traced here: 108 us
  waiting for transfers between devices  50.6 us (46%)
  starting transfers between devices  29.8 us (27%)
  Pallas kernels  22.3 us (20%)
  local copies, waits for them, and re-layouts  3.11 us (3%)
    all_to_all x1, waiting for transfers between devices, per_device(): parts = lax.all_to_all(part, 'dev', 0, 0)  26.7 us
    ppermute x6, waiting for transfers between devices, along_x(): lax.ppermute(array, 'grp', grp_pairs(lambda x, y, c: (x + 1 - 2 * c, y, c)))  23 us
    pallas_call x1, Pallas kernels, attend(): pl.pallas_call(functools.partial(attention_kernel, len(pieces)), out_shap...  18.1 us
    all_to_all x1, starting transfers between devices, per_device(): parts = lax.all_to_all(part, 'dev', 0, 0)  10.1 us
    all_to_all x1, starting transfers between devices, per_device(): q_all = lax.all_to_all(q_tiled, 'dev', 0, 0)  9.94 us
    ppermute x6, starting transfers between devices, along_x(): lax.ppermute(array, 'grp', grp_pairs(lambda x, y, c: (x + 1 - 2 * c, y, c)))  5.36 us
    pallas_call x1, Pallas kernels, attend_suffix(): pl.pallas_call(suffix_kernel, out_shape=(shape, shape), in_specs=[pl.Bloc...  2.65 us
    ppermute x1, starting transfers between devices, along_y(): return lax.ppermute(array, 'grp', grp_pairs(lambda x, y, c: (x, 1 - y, c)))  2.3 us
  transfers between devices with their start and end apart: 17, of which 7 were waited for; matrix products, arithmetic and copies ran while one was open for 2% of the time, Pallas kernels for 2%

profile of v3, /device:TPU:8, one launch (start us, length us, event | category | flops | bytes accessed | tf_op | source)
XLA Modules:
  0.0 107.7 jit_solution(17833815005311982647)
XLA Ops:
  0.0 1.1 %pad_maximum_fusion.refs_3_ = bf16[2,128,1024]{2,1,0:T(8,128)(2,1)S(1)} fusion(bf16[1,128,1024]{2,1,0:T(8,128)(2,1)} %bitcast.12, bf16[1,128,1024]{2,1,0:T(8,128)(2,1)} %bitcast.13), kind=kLoop, calls=%fused_computation | loop fusion | flops 262144 | bytes 1048576 | tf_op jit(solution)/shard_map/stack | solution.py:282
  1.1 0.1 collective-permute-start
  1.2 1.6 %collective-permute-start.2 = (bf16[2,128,1024]{2,1,0:T(8,128)(2,1)S(1)}, bf16[2,128,1024]{2,1,0:T(8,128)(2,1)S(1)}, u32[]{:S(2)}, u32[]{:S(2)}) collective-permute-start(bf16[2,128,1024]{2,1,0:T(8,128)(2,1)S(1)} %pad_maximum_fusion.refs_3_), channel_id=1, source_target_pairs={{0,64},{16,208},{32,96},{48,240},{64,128},{80,16},{96,160},{112,48... | collective-permute-start | bytes 1572872 | tf_op jit(solution)/shard_map/ppermute | solution.py:50
  2.8 2.3 %collective-permute-start.1 = (bf16[2,128,1024]{2,1,0:T(8,128)(2,1)S(1)}, bf16[2,128,1024]{2,1,0:T(8,128)(2,1)S(1)}, u32[]{:S(2)}, u32[]{:S(2)}) collective-permute-start(bf16[2,128,1024]{2,1,0:T(8,128)(2,1)S(1)} %pad_maximum_fusion.refs_3_), channel_id=1, source_target_pairs={{0,32},{16,48},{32,0},{48,16},{64,96},{80,112},{96,64},{112,80},{1... | collective-permute-start | bytes 1572872 | tf_op jit(solution)/shard_map/ppermute | solution.py:46
  5.1 0.0 collective-permute-done.refs_4_
  5.1 1.5 %collective-permute-start.3 = (bf16[2,128,1024]{2,1,0:T(8,128)(2,1)S(1)}, bf16[2,128,1024]{2,1,0:T(8,128)(2,1)}, u32[]{:S(2)}, u32[]{:S(2)}) collective-permute-start(bf16[2,128,1024]{2,1,0:T(8,128)(2,1)S(1)} %collective-permute-done.refs_4_), channel_id=1, source_target_pairs={{0,64},{16,208},{32,96},{48,240},{64,128},{80,16},{96,160},{112,48... | collective-permute-start | bytes 1572872 | tf_op jit(solution)/shard_map/ppermute | solution.py:50
  6.6 2.0 %broadcast_in_dim.8 = bf16[16,8,32,128]{3,2,1,0:T(8,128)(2,1)} broadcast(bf16[8,32,128]{2,1,0:T(8,128)(2,1)} %bitcast.10), dimensions={1,2,3} | broadcast | bytes 1114112 | tf_op jit(solution)/shard_map/broadcast_in_dim | solution.py:283
  8.6 9.9 %all-to-all-start = ((bf16[16,8,32,128]{3,2,1,0:T(8,128)(2,1)}), bf16[16,8,32,128]{3,2,1,0:T(8,128)(2,1)S(1)}, u32[]{:S(2)}, u32[]{:S(2)}) async-start(bf16[16,8,32,128]{3,2,1,0:T(8,128)(2,1)} %broadcast_in_dim.8), calls=%async_computation | async-start | bytes 2097152 | tf_op jit(solution)/shard_map/all_to_all | solution.py:284
  18.5 0.2 collective-permute-done.1.refs_5_
  18.7 0.0 collective-permute-done.3.refs_8_
  18.7 1.1 %collective-permute-start.6 = (bf16[2,128,1024]{2,1,0:T(8,128)(2,1)S(1)}, bf16[2,128,1024]{2,1,0:T(8,128)(2,1)S(1)}, u32[]{:S(2)}, u32[]{:S(2)}) collective-permute-start(bf16[2,128,1024]{2,1,0:T(8,128)(2,1)S(1)} %collective-permute-done.1.refs_5_), channel_id=1, source_target_pairs={{0,64},{16,208},{32,96},{48,240},{64,128},{80,16},{96,160},{112,48... | collective-permute-start | bytes 1572872 | tf_op jit(solution)/shard_map/ppermute | solution.py:50
  19.8 0.8 collective-permute-start.5
  20.6 1.5 %collective-permute-start.9 = (bf16[2,128,1024]{2,1,0:T(8,128)(2,1)S(1)}, bf16[2,128,1024]{2,1,0:T(8,128)(2,1)S(1)}, u32[]{:S(2)}, u32[]{:S(2)}) collective-permute-start(bf16[2,128,1024]{2,1,0:T(8,128)(2,1)S(1)} %collective-permute-done.2.refs_7_), channel_id=1, source_target_pairs={{0,16},{16,0},{32,48},{48,32},{64,80},{80,64},{96,112},{112,96},{1... | collective-permute-start | bytes 1572872 | tf_op jit(solution)/shard_map/ppermute | solution.py:42
  22.2 6.9 %collective-permute-done.6.refs_10_ = bf16[2,128,1024]{2,1,0:T(8,128)(2,1)S(1)} collective-permute-done((bf16[2,128,1024]{2,1,0:T(8,128)(2,1)S(1)}, bf16[2,128,1024]{2,1,0:T(8,128)(2,1)S(1)}, u32[]{:S(2)}, u32[]{:S(2)}) %collective-permute-start.6) | collective-permute-done | bytes 524320 | tf_op jit(solution)/shard_map/ppermute | solution.py:50
  29.1 0.4 collective-permute-start.7
  29.5 5.2 %collective-permute-done.5.refs_9_ = bf16[2,128,1024]{2,1,0:T(8,128)(2,1)S(1)} collective-permute-done((bf16[2,128,1024]{2,1,0:T(8,128)(2,1)S(1)}, bf16[2,128,1024]{2,1,0:T(8,128)(2,1)S(1)}, u32[]{:S(2)}, u32[]{:S(2)}) %collective-permute-start.5) | collective-permute-done | bytes 524320 | tf_op jit(solution)/shard_map/ppermute | solution.py:50
  34.7 0.5 collective-permute-start.12
  35.2 5.2 %collective-permute-done.8.refs_12_ = bf16[2,128,1024]{2,1,0:T(8,128)(2,1)} collective-permute-done((bf16[2,128,1024]{2,1,0:T(8,128)(2,1)S(1)}, bf16[2,128,1024]{2,1,0:T(8,128)(2,1)}, u32[]{:S(2)}, u32[]{:S(2)}) %collective-permute-start.8) | collective-permute-done | bytes 524320 | tf_op jit(solution)/shard_map/ppermute | solution.py:50
  40.5 5.6 %collective-permute-done.7.refs_11_ = bf16[2,128,1024]{2,1,0:T(8,128)(2,1)} collective-permute-done((bf16[2,128,1024]{2,1,0:T(8,128)(2,1)S(1)}, bf16[2,128,1024]{2,1,0:T(8,128)(2,1)}, u32[]{:S(2)}, u32[]{:S(2)}) %collective-permute-start.7) | collective-permute-done | bytes 524320 | tf_op jit(solution)/shard_map/ppermute | solution.py:50
  46.1 0.0 collective-permute-start.13
  46.8 0.8 copy-done.13
  47.6 0.7 collective-permute-done.13.refs_17_
  48.3 0.2 copy-done.4
  48.6 18.1 %attend.1 = bf16[16,272,128]{2,1,0:T(8,128)(2,1)} custom-call(s32[1]{0:T(128)S(6)} %copy.12.refs_0_, s32[4,4]{1,0:T(4,128)} %bitcast.16, bf16[16,8,32,128]{3,2,1,0:T(8,128)(2,1)} %copy-done.4, bf16[2,128,1024]{2,1,0:T(8,128)(2,1)} %copy-done.5, bf16[2,128,1024]{2,1,0:T(8,128)(2,1)} %copy-done.6, bf16[2,128,1024]{2,1,0:T(8,128)(2,1)} %copy-done.8, ...), custom_call_target="tpu_custom_call" | custom-call | flops 9663676416 | bytes 9437184 | tf_op jit(solution)/shard_map/attend/pallas_call | solution.py:172
  66.7 0.0 copy-start
  66.7 0.0 copy-start.1
  66.7 0.0 copy-start.2
  66.7 0.0 copy-start.3
  66.7 10.1 %all-to-all-start.1 = ((bf16[16,272,128]{2,1,0:T(8,128)(2,1)}), bf16[16,272,128]{2,1,0:T(8,128)(2,1)S(1)}, u32[]{:S(2)}, u32[]{:S(2)}) async-start(bf16[16,272,128]{2,1,0:T(8,128)(2,1)} %attend.1), calls=%async_computation.1 | async-start | bytes 2228224 | tf_op jit(solution)/shard_map/all_to_all | solution.py:287
  76.8 2.7 %attend_suffix.1 = (f32[8,32,128]{2,1,0:T(8,128)S(1)}, f32[8,32,128]{2,1,0:T(8,128)S(1)}) custom-call(s32[4]{0:T(128)S(1)} %copy-done.3, bf16[8,32,128]{2,1,0:T(8,128)(2,1)S(1)} %bitcast.11, bf16[4,128,1024]{2,1,0:T(8,128)(2,1)S(1)} %copy-done, bf16[4,128,1024]{2,1,0:T(8,128)(2,1)S(1)} %copy-done.1), custom_call_target="tpu_custom_call" | custom-call | flops 67108864 | bytes 2097152 | tf_op jit(solution)/shard_map/attend_suffix/pallas_call | solution.py:221
  79.5 26.7 %all-to-all-done.1.parts_ref = bf16[16,272,128]{2,1,0:T(8,128)(2,1)S(1)} async-done(((bf16[16,272,128]{2,1,0:T(8,128)(2,1)}), bf16[16,272,128]{2,1,0:T(8,128)(2,1)S(1)}, u32[]{:S(2)}, u32[]{:S(2)}) %all-to-all-start.1) | async-done | bytes 1114144 | tf_op jit(solution)/shard_map/all_to_all | solution.py:287
  106.2 1.5 %merge.1 = bf16[4,8192]{1,0:T(4,128)(2,1)} custom-call(bf16[16,272,128]{2,1,0:T(8,128)(2,1)S(1)} %all-to-all-done.1.parts_ref, f32[8,32,128]{2,1,0:T(8,128)S(1)} %get-tuple-element.9.out_suf_ref, f32[8,32,128]{2,1,0:T(8,128)S(1)} %get-tuple-element.10.lse_suf_ref), custom_call_target="tpu_custom_call" | custom-call | flops 2097152 | bytes 1048576 | tf_op jit(solution)/shard_map/merge/pallas_call | solution.py:256
  (35 shorter events, 0.1 us)
Async XLA Ops:
  1.1 7.5 %copy-start.5 = (bf16[2,128,1024]{2,1,0:T(8,128)(2,1)}, bf16[2,128,1024]{2,1,0:T(8,128)(2,1)S(1)}, u32[]{:S(2)}) copy-start(bf16[2,128,1024]{2,1,0:T(8,128)(2,1)S(1)} %pad_maximum_fusion.refs_3_) | copy-start | bytes 1572868
  1.1 4.0 %collective-permute-start = (bf16[2,128,1024]{2,1,0:T(8,128)(2,1)S(1)}, bf16[2,128,1024]{2,1,0:T(8,128)(2,1)S(1)}, u32[]{:S(2)}, u32[]{:S(2)}) collective-permute-start(bf16[2,128,1024]{2,1,0:T(8,128)(2,1)S(1)} %pad_maximum_fusion.refs_3_), channel_id=1, source_target_pairs={{0,16},{16,0},{32,48},{48,32},{64,80},{80,64},{96,112},{112,96},{1... | collective-permute-start | bytes 1572872 | tf_op jit(solution)/shard_map/ppermute | solution.py:42
  1.2 17.3 %collective-permute-start.2 = (bf16[2,128,1024]{2,1,0:T(8,128)(2,1)S(1)}, bf16[2,128,1024]{2,1,0:T(8,128)(2,1)S(1)}, u32[]{:S(2)}, u32[]{:S(2)}) collective-permute-start(bf16[2,128,1024]{2,1,0:T(8,128)(2,1)S(1)} %pad_maximum_fusion.refs_3_), channel_id=1, source_target_pairs={{0,64},{16,208},{32,96},{48,240},{64,128},{80,16},{96,160},{112,48... | collective-permute-start | bytes 1572872 | tf_op jit(solution)/shard_map/ppermute | solution.py:50
  2.8 15.9 %collective-permute-start.1 = (bf16[2,128,1024]{2,1,0:T(8,128)(2,1)S(1)}, bf16[2,128,1024]{2,1,0:T(8,128)(2,1)S(1)}, u32[]{:S(2)}, u32[]{:S(2)}) collective-permute-start(bf16[2,128,1024]{2,1,0:T(8,128)(2,1)S(1)} %pad_maximum_fusion.refs_3_), channel_id=1, source_target_pairs={{0,32},{16,48},{32,0},{48,16},{64,96},{80,112},{96,64},{112,80},{1... | collective-permute-start | bytes 1572872 | tf_op jit(solution)/shard_map/ppermute | solution.py:46
  5.1 3.5 %copy-start.6 = (bf16[2,128,1024]{2,1,0:T(8,128)(2,1)}, bf16[2,128,1024]{2,1,0:T(8,128)(2,1)S(1)}, u32[]{:S(2)}) copy-start(bf16[2,128,1024]{2,1,0:T(8,128)(2,1)S(1)} %collective-permute-done.refs_4_) | copy-start | bytes 1572868
  5.1 13.7 %collective-permute-start.3 = (bf16[2,128,1024]{2,1,0:T(8,128)(2,1)S(1)}, bf16[2,128,1024]{2,1,0:T(8,128)(2,1)}, u32[]{:S(2)}, u32[]{:S(2)}) collective-permute-start(bf16[2,128,1024]{2,1,0:T(8,128)(2,1)S(1)} %collective-permute-done.refs_4_), channel_id=1, source_target_pairs={{0,64},{16,208},{32,96},{48,240},{64,128},{80,16},{96,160},{112,48... | collective-permute-start | bytes 1572872 | tf_op jit(solution)/shard_map/ppermute | solution.py:50
  8.6 39.0 %all-to-all-start = ((bf16[16,8,32,128]{3,2,1,0:T(8,128)(2,1)}), bf16[16,8,32,128]{3,2,1,0:T(8,128)(2,1)S(1)}, u32[]{:S(2)}, u32[]{:S(2)}) async-start(bf16[16,8,32,128]{3,2,1,0:T(8,128)(2,1)} %broadcast_in_dim.8), calls=%async_computation | async-start | bytes 2097152 | tf_op jit(solution)/shard_map/all_to_all | solution.py:284
  18.5 29.8 %copy-start.7 = (bf16[2,128,1024]{2,1,0:T(8,128)(2,1)}, bf16[2,128,1024]{2,1,0:T(8,128)(2,1)S(1)}, u32[]{:S(2)}) copy-start(bf16[2,128,1024]{2,1,0:T(8,128)(2,1)S(1)} %collective-permute-done.2.refs_7_) | copy-start | bytes 1572868
  18.7 29.6 %copy-start.8 = (bf16[2,128,1024]{2,1,0:T(8,128)(2,1)}, bf16[2,128,1024]{2,1,0:T(8,128)(2,1)S(1)}, u32[]{:S(2)}) copy-start(bf16[2,128,1024]{2,1,0:T(8,128)(2,1)S(1)} %collective-permute-done.1.refs_5_) | copy-start | bytes 1572868
  18.7 10.4 %collective-permute-start.6 = (bf16[2,128,1024]{2,1,0:T(8,128)(2,1)S(1)}, bf16[2,128,1024]{2,1,0:T(8,128)(2,1)S(1)}, u32[]{:S(2)}, u32[]{:S(2)}) collective-permute-start(bf16[2,128,1024]{2,1,0:T(8,128)(2,1)S(1)} %collective-permute-done.1.refs_5_), channel_id=1, source_target_pairs={{0,64},{16,208},{32,96},{48,240},{64,128},{80,16},{96,160},{112,48... | collective-permute-start | bytes 1572872 | tf_op jit(solution)/shard_map/ppermute | solution.py:50
  19.8 9.3 %collective-permute-start.4 = (bf16[2,128,1024]{2,1,0:T(8,128)(2,1)S(1)}, bf16[2,128,1024]{2,1,0:T(8,128)(2,1)S(1)}, u32[]{:S(2)}, u32[]{:S(2)}) collective-permute-start(bf16[2,128,1024]{2,1,0:T(8,128)(2,1)S(1)} %collective-permute-done.1.refs_5_), channel_id=1, source_target_pairs={{0,16},{16,0},{32,48},{48,32},{64,80},{80,64},{96,112},{112,96},{1... | collective-permute-start | bytes 1572872 | tf_op jit(solution)/shard_map/ppermute | solution.py:42
  19.8 14.9 %collective-permute-start.5 = (bf16[2,128,1024]{2,1,0:T(8,128)(2,1)S(1)}, bf16[2,128,1024]{2,1,0:T(8,128)(2,1)S(1)}, u32[]{:S(2)}, u32[]{:S(2)}) collective-permute-start(bf16[2,128,1024]{2,1,0:T(8,128)(2,1)S(1)} %collective-permute-done.2.refs_7_), channel_id=1, source_target_pairs={{0,64},{16,208},{32,96},{48,240},{64,128},{80,16},{96,160},{112,48... | collective-permute-start | bytes 1572872 | tf_op jit(solution)/shard_map/ppermute | solution.py:50
  20.6 14.1 %collective-permute-start.9 = (bf16[2,128,1024]{2,1,0:T(8,128)(2,1)S(1)}, bf16[2,128,1024]{2,1,0:T(8,128)(2,1)S(1)}, u32[]{:S(2)}, u32[]{:S(2)}) collective-permute-start(bf16[2,128,1024]{2,1,0:T(8,128)(2,1)S(1)} %collective-permute-done.2.refs_7_), channel_id=1, source_target_pairs={{0,16},{16,0},{32,48},{48,32},{64,80},{80,64},{96,112},{112,96},{1... | collective-permute-start | bytes 1572872 | tf_op jit(solution)/shard_map/ppermute | solution.py:42
  29.1 19.2 %copy-start.9 = (bf16[2,128,1024]{2,1,0:T(8,128)(2,1)}, bf16[2,128,1024]{2,1,0:T(8,128)(2,1)S(1)}, u32[]{:S(2)}) copy-start(bf16[2,128,1024]{2,1,0:T(8,128)(2,1)S(1)} %collective-permute-done.6.refs_10_) | copy-start | bytes 1572868
  29.1 11.3 %collective-permute-start.8 = (bf16[2,128,1024]{2,1,0:T(8,128)(2,1)S(1)}, bf16[2,128,1024]{2,1,0:T(8,128)(2,1)}, u32[]{:S(2)}, u32[]{:S(2)}) collective-permute-start(bf16[2,128,1024]{2,1,0:T(8,128)(2,1)S(1)} %collective-permute-done.6.refs_10_), channel_id=1, source_target_pairs={{0,64},{16,208},{32,96},{48,240},{64,128},{80,16},{96,160},{112,48... | collective-permute-start | bytes 1572872 | tf_op jit(solution)/shard_map/ppermute | solution.py:50
  29.1 19.2 %copy-start.10 = (bf16[2,128,1024]{2,1,0:T(8,128)(2,1)}, bf16[2,128,1024]{2,1,0:T(8,128)(2,1)S(1)}, u32[]{:S(2)}) copy-start(bf16[2,128,1024]{2,1,0:T(8,128)(2,1)S(1)} %collective-permute-done.4.refs_6_) | copy-start | bytes 1572868
  29.1 16.9 %collective-permute-start.7 = (bf16[2,128,1024]{2,1,0:T(8,128)(2,1)S(1)}, bf16[2,128,1024]{2,1,0:T(8,128)(2,1)}, u32[]{:S(2)}, u32[]{:S(2)}) collective-permute-start(bf16[2,128,1024]{2,1,0:T(8,128)(2,1)S(1)} %collective-permute-done.4.refs_6_), channel_id=1, source_target_pairs={{0,64},{16,208},{32,96},{48,240},{64,128},{80,16},{96,160},{112,48... | collective-permute-start | bytes 1572872 | tf_op jit(solution)/shard_map/ppermute | solution.py:50
  29.5 18.1 %collective-permute-start.10 = (bf16[2,128,1024]{2,1,0:T(8,128)(2,1)}, bf16[2,128,1024]{2,1,0:T(8,128)(2,1)}, u32[]{:S(2)}, u32[]{:S(2)}) collective-permute-start(bf16[2,128,1024]{2,1,0:T(8,128)(2,1)} %collective-permute-done.3.refs_8_), channel_id=1, source_target_pairs={{0,16},{16,0},{32,48},{48,32},{64,80},{80,64},{96,112},{112,96},{1... | collective-permute-start | bytes 1572872 | tf_op jit(solution)/shard_map/ppermute | solution.py:42
  34.7 12.0 %copy-start.11 = (bf16[2,128,1024]{2,1,0:T(8,128)(2,1)}, bf16[2,128,1024]{2,1,0:T(8,128)(2,1)S(1)}, u32[]{:S(2)}) copy-start(bf16[2,128,1024]{2,1,0:T(8,128)(2,1)S(1)} %collective-permute-done.5.refs_9_) | copy-start | bytes 1572868
  34.7 12.0 %collective-permute-start.11 = (bf16[2,128,1024]{2,1,0:T(8,128)(2,1)S(1)}, bf16[2,128,1024]{2,1,0:T(8,128)(2,1)S(1)}, u32[]{:S(2)}, u32[]{:S(2)}) collective-permute-start(bf16[2,128,1024]{2,1,0:T(8,128)(2,1)S(1)} %collective-permute-done.5.refs_9_), channel_id=1, source_target_pairs={{0,16},{16,0},{32,48},{48,32},{64,80},{80,64},{96,112},{112,96},{1... | collective-permute-start | bytes 1572872 | tf_op jit(solution)/shard_map/ppermute | solution.py:42
  34.7 11.3 %copy-start.12 = (bf16[2,128,1024]{2,1,0:T(8,128)(2,1)}, bf16[2,128,1024]{2,1,0:T(8,128)(2,1)S(1)}, u32[]{:S(2)}) copy-start(bf16[2,128,1024]{2,1,0:T(8,128)(2,1)S(1)} %collective-permute-done.9.refs_13_) | copy-start | bytes 1572868
  34.7 12.8 %collective-permute-start.12 = (bf16[2,128,1024]{2,1,0:T(8,128)(2,1)S(1)}, bf16[2,128,1024]{2,1,0:T(8,128)(2,1)}, u32[]{:S(2)}, u32[]{:S(2)}) collective-permute-start(bf16[2,128,1024]{2,1,0:T(8,128)(2,1)S(1)} %collective-permute-done.6.refs_10_), channel_id=1, source_target_pairs={{0,16},{16,0},{32,48},{48,32},{64,80},{80,64},{96,112},{112,96},{1... | collective-permute-start | bytes 1572872 | tf_op jit(solution)/shard_map/ppermute | solution.py:42
  40.4 7.2 %collective-permute-start.14 = (bf16[2,128,1024]{2,1,0:T(8,128)(2,1)}, bf16[2,128,1024]{2,1,0:T(8,128)(2,1)}, u32[]{:S(2)}, u32[]{:S(2)}) collective-permute-start(bf16[2,128,1024]{2,1,0:T(8,128)(2,1)} %collective-permute-done.8.refs_12_), channel_id=1, source_target_pairs={{0,16},{16,0},{32,48},{48,32},{64,80},{80,64},{96,112},{112,96},{1... | collective-permute-start | bytes 1572872 | tf_op jit(solution)/shard_map/ppermute | solution.py:42
  46.1 2.3 %collective-permute-start.13 = (bf16[2,128,1024]{2,1,0:T(8,128)(2,1)}, bf16[2,128,1024]{2,1,0:T(8,128)(2,1)}, u32[]{:S(2)}, u32[]{:S(2)}) collective-permute-start(bf16[2,128,1024]{2,1,0:T(8,128)(2,1)} %collective-permute-done.7.refs_11_), channel_id=1, source_target_pairs={{0,16},{16,0},{32,48},{48,32},{64,80},{80,64},{96,112},{112,96},{1... | collective-permute-start | bytes 1572872 | tf_op jit(solution)/shard_map/ppermute | solution.py:42
  46.7 0.8 copy-start.13
  47.6 1.0 copy-start.4
  66.7 10.1 %copy-start = (bf16[4,128,1024]{2,1,0:T(8,128)(2,1)S(1)}, bf16[4,128,1024]{2,1,0:T(8,128)(2,1)}, u32[]{:S(2)}) copy-start(bf16[4,128,1024]{2,1,0:T(8,128)(2,1)} %k_ref.1) | copy-start | bytes 3145732
  66.7 10.1 %copy-start.1 = (bf16[4,128,1024]{2,1,0:T(8,128)(2,1)S(1)}, bf16[4,128,1024]{2,1,0:T(8,128)(2,1)}, u32[]{:S(2)}) copy-start(bf16[4,128,1024]{2,1,0:T(8,128)(2,1)} %v_ref.1) | copy-start | bytes 3145732
  66.7 10.1 %copy-start.2 = (bf16[4,8192]{1,0:T(4,128)(2,1)S(1)}, bf16[4,8192]{1,0:T(4,128)(2,1)}, u32[]{:S(2)}) copy-start(bf16[4,8192]{1,0:T(4,128)(2,1)} %param.10) | copy-start | bytes 196612
  66.7 10.1 %copy-start.3 = (s32[4]{0:T(128)S(1)}, s32[4]{0:T(128)}, u32[]{:S(2)}) copy-start(s32[4]{0:T(128)} %length_ref.1) | copy-start | bytes 52
  66.7 39.5 %all-to-all-start.1 = ((bf16[16,272,128]{2,1,0:T(8,128)(2,1)}), bf16[16,272,128]{2,1,0:T(8,128)(2,1)S(1)}, u32[]{:S(2)}, u32[]{:S(2)}) async-start(bf16[16,272,128]{2,1,0:T(8,128)(2,1)} %attend.1), calls=%async_computation.1 | async-start | bytes 2228224 | tf_op jit(solution)/shard_map/all_to_all | solution.py:287

commit v4 on v3

--- a/solution.py
+++ b/solution.py
@@ -22,7 +22,7 @@
 VMEM_LIMIT = 16 * 1024 * 1024
 ATTEND_VMEM = 60 * 1024 * 1024
 PARTS = (2, 3, 3)
-STEPS = 2
+STEPS = 1
 
 
 def grp_index(x, y_hi, core):
@@ -81,8 +81,7 @@
     return first, second, third
 
 
-def flash_step(q, keys, values, state):
-    scores = nt_dot(q, keys)
+def flash_step(scores, values, state):
     peaks = jnp.max(scores, axis=1, keepdims=True)
     if state is not None:
         peaks = jnp.maximum(peaks, state[0])
@@ -128,13 +127,11 @@
     size = (root_rows + PPD * PAGE) // STEPS
     lane = lax.broadcasted_iota(jnp.int32, (ROWS_ALL, HD), 1)
 
-    def one_head(k):
-        lanes = slice(k * HD, (k + 1) * HD)
-        q = q_ref[:, k].reshape(ROWS_ALL, HD)
-        state = None
-        for i in range(STEPS):
-            rows = slice(i * size, (i + 1) * size)
-            state = flash_step(q, held_ref[0, rows, lanes], held_ref[1, rows, lanes], state)
+    def scores_of(k, i):
+        keys = held_ref[0, i * size : (i + 1) * size, k * HD : (k + 1) * HD]
+        return nt_dot(q_ref[:, k].reshape(ROWS_ALL, HD), keys)
+
+    def finish_head(k, state):
         peaks, totals, weighted = state
         out_ref[:, k * UNIT : (k + 1) * UNIT] = (
             (weighted / totals).astype(jnp.bfloat16).reshape(MEMBERS, UNIT, HD)
@@ -146,9 +143,18 @@
     for part, heads in enumerate(PARTS):
         for copy in copies[part]:
             copy.wait()
-        for k in range(first_head, first_head + heads):
-            one_head(k)
+        steps = [(k, i) for k in range(first_head, first_head + heads) for i in range(STEPS)]
         first_head += heads
+        scores = scores_of(*steps[0])
+        state = None
+        for (k, i), later in zip(steps, steps[1:] + [None]):
+            later_scores = None if later is None else scores_of(*later)
+            values = held_ref[1, i * size : (i + 1) * size, k * HD : (k + 1) * HD]
+            state = flash_step(scores, values, state)
+            scores = later_scores
+            if i == STEPS - 1:
+                finish_head(k, state)
+                state = None
         if part + 2 < len(PARTS):
             for copy in copies[part + 2]:
                 copy.start()
@@ -194,6 +200,27 @@
     )
 
 
+def spread_kernel(q_ref, out_ref, sems):
+    copies = [pltpu.make_async_copy(q_ref, out_ref.at[m], sems.at[m]) for m in range(MEMBERS)]
+    for copy in copies:
+        copy.start()
+    for copy in copies:
+        copy.wait()
+
+
+def spread(q_units):
+    return pl.pallas_call(
+        spread_kernel,
+        out_shape=jax.ShapeDtypeStruct((MEMBERS, KVH, UNIT, HD), jnp.bfloat16),
+        in_specs=[pl.BlockSpec(memory_space=pltpu.VMEM)],
+        out_specs=pl.BlockSpec(memory_space=pl.ANY),
+        scratch_shapes=[pltpu.SemaphoreType.DMA((MEMBERS,))],
+        compiler_params=pltpu.CompilerParams(vmem_limit_bytes=VMEM_LIMIT),
+        cost_estimate=pl.CostEstimate(flops=0, bytes_accessed=MEMBERS * KVH * UNIT * HD * 2, transcendentals=0),
+        name="spread",
+    )(q_units)
+
+
 def suffix_kernel(length_ref, q_ref, k_ref, v_ref, out_ref, lse_ref):
     slots = OWN * SUF
     row = lax.broadcasted_iota(jnp.int32, (UNIT, slots), 0) % OWN
@@ -280,8 +307,7 @@
 ):
     q_units = queries.reshape(OWN, KVH, QPK, HD).transpose(1, 2, 0, 3).reshape(KVH, UNIT, HD)
     pieces = gather_root(jnp.stack((root_keys, root_values)))
-    q_tiled = jnp.broadcast_to(q_units[None], (MEMBERS, KVH, UNIT, HD))
-    q_all = lax.all_to_all(q_tiled, "dev", 0, 0)
+    q_all = lax.all_to_all(spread(q_units), "dev", 0, 0)
     out_suf, lse_suf = attend_suffix(suffix_lengths, q_units, suffix_keys, suffix_values)
     part = attend(task_ids, page_table[:, 0], q_all, pieces, prefix_keys[0, 0], prefix_values[0, 0])
     parts = lax.all_to_all(part, "dev", 0, 0)

time: 109 us -> 107 us (0.982)
  Pallas kernels: 22.3 us -> 21.1 us
  local copies, waits for them, and re-layouts: 3.11 us -> 1.96 us
    pallas_call x1, Pallas kernels: 18.1 us -> 15.8 us  [attend(): pl.pallas_call(functools.partial(attention_kernel, len(pieces)), out_shap...]
    broadcast_in_dim x1 -> x0, local copies, waits for them, and re-layouts: 2.01 us -> none  [per_device(): q_tiled = jnp.broadcast_to(q_units[None], (MEMBERS, KVH, UNIT, HD))]
    pallas_call x0 -> x1, Pallas kernels: none -> 1.13 us  [spread(): pl.pallas_call(spread_kernel, out_shape=jax.ShapeDtypeStruct((MEMBERS, KV...]
  transfers between devices with their start and end apart: 17 -> 17, of which waited for: 7 -> 7; matrix products, arithmetic and copies ran while one was open for 2% -> 0% of each run, Pallas kernels for 2% -> 4%
where the time goes in v4:
time: 107 us; the launch traced here: 105 us
  waiting for transfers between devices  50.6 us (47%)
  starting transfers between devices  29.8 us (28%)
  Pallas kernels  21.1 us (20%)
  local copies, waits for them, and re-layouts  1.96 us (2%)
  other arithmetic  1.08 us (1%)
    all_to_all x1, waiting for transfers between devices, per_device(): parts = lax.all_to_all(part, 'dev', 0, 0)  26.7 us
    ppermute x6, waiting for transfers between devices, along_x(): lax.ppermute(array, 'grp', grp_pairs(lambda x, y, c: (x + 1 - 2 * c, y, c)))  23 us
    pallas_call x1, Pallas kernels, attend(): pl.pallas_call(functools.partial(attention_kernel, len(pieces)), out_shap...  15.8 us
    all_to_all x1, starting transfers between devices, per_device(): parts = lax.all_to_all(part, 'dev', 0, 0)  10.1 us
    all_to_all x1, starting transfers between devices, per_device(): q_all = lax.all_to_all(spread(q_units), 'dev', 0, 0)  9.95 us
    ppermute x6, starting transfers between devices, along_x(): lax.ppermute(array, 'grp', grp_pairs(lambda x, y, c: (x + 1 - 2 * c, y, c)))  5.35 us
    pallas_call x1, Pallas kernels, attend_suffix(): pl.pallas_call(suffix_kernel, out_shape=(shape, shape), in_specs=[pl.Bloc...  2.65 us
    ppermute x1, starting transfers between devices, along_y(): return lax.ppermute(array, 'grp', grp_pairs(lambda x, y, c: (x, 1 - y, c)))  2.3 us
  transfers between devices with their start and end apart: 17, of which 7 were waited for; matrix products, arithmetic and copies ran while one was open for 0% of the time, Pallas kernels for 4%

profile of v4, /device:TPU:8, one launch (start us, length us, event | category | flops | bytes accessed | tf_op | source)
XLA Modules:
  0.0 105.4 jit_solution(11134142578966683900)
XLA Ops:
  0.0 1.1 %pad_maximum_fusion.refs_3_ = bf16[2,128,1024]{2,1,0:T(8,128)(2,1)S(1)} fusion(bf16[1,128,1024]{2,1,0:T(8,128)(2,1)} %bitcast.12, bf16[1,128,1024]{2,1,0:T(8,128)(2,1)} %bitcast.13), kind=kLoop, calls=%fused_computation | loop fusion | flops 262144 | bytes 1048576 | tf_op jit(solution)/shard_map/stack | solution.py:309
  1.1 0.1 collective-permute-start
  1.2 1.6 %collective-permute-start.2 = (bf16[2,128,1024]{2,1,0:T(8,128)(2,1)S(1)}, bf16[2,128,1024]{2,1,0:T(8,128)(2,1)S(1)}, u32[]{:S(2)}, u32[]{:S(2)}) collective-permute-start(bf16[2,128,1024]{2,1,0:T(8,128)(2,1)S(1)} %pad_maximum_fusion.refs_3_), channel_id=1, source_target_pairs={{0,64},{16,208},{32,96},{48,240},{64,128},{80,16},{96,160},{112,48... | collective-permute-start | bytes 1572872 | tf_op jit(solution)/shard_map/ppermute | solution.py:50
  2.8 2.3 %collective-permute-start.1 = (bf16[2,128,1024]{2,1,0:T(8,128)(2,1)S(1)}, bf16[2,128,1024]{2,1,0:T(8,128)(2,1)S(1)}, u32[]{:S(2)}, u32[]{:S(2)}) collective-permute-start(bf16[2,128,1024]{2,1,0:T(8,128)(2,1)S(1)} %pad_maximum_fusion.refs_3_), channel_id=1, source_target_pairs={{0,32},{16,48},{32,0},{48,16},{64,96},{80,112},{96,64},{112,80},{1... | collective-permute-start | bytes 1572872 | tf_op jit(solution)/shard_map/ppermute | solution.py:46
  5.1 1.5 %collective-permute-start.3 = (bf16[2,128,1024]{2,1,0:T(8,128)(2,1)S(1)}, bf16[2,128,1024]{2,1,0:T(8,128)(2,1)}, u32[]{:S(2)}, u32[]{:S(2)}) collective-permute-start(bf16[2,128,1024]{2,1,0:T(8,128)(2,1)S(1)} %collective-permute-done.refs_4_), channel_id=1, source_target_pairs={{0,64},{16,208},{32,96},{48,240},{64,128},{80,16},{96,160},{112,48... | collective-permute-start | bytes 1572872 | tf_op jit(solution)/shard_map/ppermute | solution.py:50
  6.6 0.8 copy-done.2
  7.4 1.1 %spread.1 = bf16[16,8,32,128]{3,2,1,0:T(8,128)(2,1)} custom-call(bf16[8,32,128]{2,1,0:T(8,128)(2,1)S(1)} %bitcast.10), custom_call_target="tpu_custom_call" | custom-call | bytes 1048576 | tf_op jit(solution)/shard_map/spread/pallas_call | solution.py:212
  8.5 10.0 %all-to-all-start = ((bf16[16,8,32,128]{3,2,1,0:T(8,128)(2,1)}), bf16[16,8,32,128]{3,2,1,0:T(8,128)(2,1)S(1)}, u32[]{:S(2)}, u32[]{:S(2)}) async-start(bf16[16,8,32,128]{3,2,1,0:T(8,128)(2,1)} %spread.1), calls=%async_computation | async-start | bytes 2097152 | tf_op jit(solution)/shard_map/all_to_all | solution.py:310
  18.5 0.0 collective-permute-done.2.refs_7_
  18.5 0.2 collective-permute-done.1.refs_5_
  18.7 1.1 %collective-permute-start.6 = (bf16[2,128,1024]{2,1,0:T(8,128)(2,1)S(1)}, bf16[2,128,1024]{2,1,0:T(8,128)(2,1)S(1)}, u32[]{:S(2)}, u32[]{:S(2)}) collective-permute-start(bf16[2,128,1024]{2,1,0:T(8,128)(2,1)S(1)} %collective-permute-done.1.refs_5_), channel_id=1, source_target_pairs={{0,64},{16,208},{32,96},{48,240},{64,128},{80,16},{96,160},{112,48... | collective-permute-start | bytes 1572872 | tf_op jit(solution)/shard_map/ppermute | solution.py:50
  19.8 0.8 collective-permute-start.5
  20.6 1.5 %collective-permute-start.9 = (bf16[2,128,1024]{2,1,0:T(8,128)(2,1)S(1)}, bf16[2,128,1024]{2,1,0:T(8,128)(2,1)S(1)}, u32[]{:S(2)}, u32[]{:S(2)}) collective-permute-start(bf16[2,128,1024]{2,1,0:T(8,128)(2,1)S(1)} %collective-permute-done.2.refs_7_), channel_id=1, source_target_pairs={{0,16},{16,0},{32,48},{48,32},{64,80},{80,64},{96,112},{112,96},{1... | collective-permute-start | bytes 1572872 | tf_op jit(solution)/shard_map/ppermute | solution.py:42
  22.2 6.9 %collective-permute-done.6.refs_10_ = bf16[2,128,1024]{2,1,0:T(8,128)(2,1)S(1)} collective-permute-done((bf16[2,128,1024]{2,1,0:T(8,128)(2,1)S(1)}, bf16[2,128,1024]{2,1,0:T(8,128)(2,1)S(1)}, u32[]{:S(2)}, u32[]{:S(2)}) %collective-permute-start.6) | collective-permute-done | bytes 524320 | tf_op jit(solution)/shard_map/ppermute | solution.py:50
  29.1 0.4 collective-permute-start.7
  29.5 5.2 %collective-permute-done.5.refs_9_ = bf16[2,128,1024]{2,1,0:T(8,128)(2,1)S(1)} collective-permute-done((bf16[2,128,1024]{2,1,0:T(8,128)(2,1)S(1)}, bf16[2,128,1024]{2,1,0:T(8,128)(2,1)S(1)}, u32[]{:S(2)}, u32[]{:S(2)}) %collective-permute-start.5) | collective-permute-done | bytes 524320 | tf_op jit(solution)/shard_map/ppermute | solution.py:50
  34.7 0.5 collective-permute-start.12
  35.2 5.2 %collective-permute-done.8.refs_12_ = bf16[2,128,1024]{2,1,0:T(8,128)(2,1)} collective-permute-done((bf16[2,128,1024]{2,1,0:T(8,128)(2,1)S(1)}, bf16[2,128,1024]{2,1,0:T(8,128)(2,1)}, u32[]{:S(2)}, u32[]{:S(2)}) %collective-permute-start.8) | collective-permute-done | bytes 524320 | tf_op jit(solution)/shard_map/ppermute | solution.py:50
  40.5 5.6 %collective-permute-done.7.refs_11_ = bf16[2,128,1024]{2,1,0:T(8,128)(2,1)} collective-permute-done((bf16[2,128,1024]{2,1,0:T(8,128)(2,1)S(1)}, bf16[2,128,1024]{2,1,0:T(8,128)(2,1)}, u32[]{:S(2)}, u32[]{:S(2)}) %collective-permute-start.7) | collective-permute-done | bytes 524320 | tf_op jit(solution)/shard_map/ppermute | solution.py:50
  46.1 0.0 collective-permute-start.13
  46.8 0.8 copy-done.14
  47.6 0.7 collective-permute-done.13.refs_17_
  48.3 0.2 copy-done.5
  48.6 15.8 %attend.1 = bf16[16,272,128]{2,1,0:T(8,128)(2,1)} custom-call(s32[1]{0:T(128)S(6)} %copy.12.refs_0_, s32[4,4]{1,0:T(4,128)} %bitcast.16, bf16[16,8,32,128]{3,2,1,0:T(8,128)(2,1)} %copy-done.5, bf16[2,128,1024]{2,1,0:T(8,128)(2,1)} %copy-done.6, bf16[2,128,1024]{2,1,0:T(8,128)(2,1)} %copy-done.7, bf16[2,128,1024]{2,1,0:T(8,128)(2,1)} %copy-done.9, ...), custom_call_target="tpu_custom_call" | custom-call | flops 9663676416 | bytes 9437184 | tf_op jit(solution)/shard_map/attend/pallas_call | solution.py:178
  64.4 0.0 copy-start
  64.4 0.0 copy-start.1
  64.4 0.0 copy-start.3
  64.4 0.0 copy-start.4
  64.5 10.1 %all-to-all-start.1 = ((bf16[16,272,128]{2,1,0:T(8,128)(2,1)}), bf16[16,272,128]{2,1,0:T(8,128)(2,1)S(1)}, u32[]{:S(2)}, u32[]{:S(2)}) async-start(bf16[16,272,128]{2,1,0:T(8,128)(2,1)} %attend.1), calls=%async_computation.1 | async-start | bytes 2228224 | tf_op jit(solution)/shard_map/all_to_all | solution.py:313
  74.6 2.7 %attend_suffix.1 = (f32[8,32,128]{2,1,0:T(8,128)S(1)}, f32[8,32,128]{2,1,0:T(8,128)S(1)}) custom-call(s32[4]{0:T(128)S(1)} %copy-done.4, bf16[8,32,128]{2,1,0:T(8,128)(2,1)S(1)} %bitcast.11, bf16[4,128,1024]{2,1,0:T(8,128)(2,1)S(1)} %copy-done, bf16[4,128,1024]{2,1,0:T(8,128)(2,1)S(1)} %copy-done.1), custom_call_target="tpu_custom_call" | custom-call | flops 67108864 | bytes 2097152 | tf_op jit(solution)/shard_map/attend_suffix/pallas_call | solution.py:248
  77.2 26.7 %all-to-all-done.1.parts_ref = bf16[16,272,128]{2,1,0:T(8,128)(2,1)S(1)} async-done(((bf16[16,272,128]{2,1,0:T(8,128)(2,1)}), bf16[16,272,128]{2,1,0:T(8,128)(2,1)S(1)}, u32[]{:S(2)}, u32[]{:S(2)}) %all-to-all-start.1) | async-done | bytes 1114144 | tf_op jit(solution)/shard_map/all_to_all | solution.py:313
  103.9 1.5 %merge.1 = bf16[4,8192]{1,0:T(4,128)(2,1)} custom-call(bf16[16,272,128]{2,1,0:T(8,128)(2,1)S(1)} %all-to-all-done.1.parts_ref, f32[8,32,128]{2,1,0:T(8,128)S(1)} %get-tuple-element.9.out_suf_ref, f32[8,32,128]{2,1,0:T(8,128)S(1)} %get-tuple-element.10.lse_suf_ref), custom_call_target="tpu_custom_call" | custom-call | flops 2097152 | bytes 1048576 | tf_op jit(solution)/shard_map/merge/pallas_call | solution.py:283
  (37 shorter events, 0.1 us)
Async XLA Ops:
  1.1 7.5 %copy-start.6 = (bf16[2,128,1024]{2,1,0:T(8,128)(2,1)}, bf16[2,128,1024]{2,1,0:T(8,128)(2,1)S(1)}, u32[]{:S(2)}) copy-start(bf16[2,128,1024]{2,1,0:T(8,128)(2,1)S(1)} %pad_maximum_fusion.refs_3_) | copy-start | bytes 1572868
  1.1 4.0 %collective-permute-start = (bf16[2,128,1024]{2,1,0:T(8,128)(2,1)S(1)}, bf16[2,128,1024]{2,1,0:T(8,128)(2,1)S(1)}, u32[]{:S(2)}, u32[]{:S(2)}) collective-permute-start(bf16[2,128,1024]{2,1,0:T(8,128)(2,1)S(1)} %pad_maximum_fusion.refs_3_), channel_id=1, source_target_pairs={{0,16},{16,0},{32,48},{48,32},{64,80},{80,64},{96,112},{112,96},{1... | collective-permute-start | bytes 1572872 | tf_op jit(solution)/shard_map/ppermute | solution.py:42
  1.2 17.3 %collective-permute-start.2 = (bf16[2,128,1024]{2,1,0:T(8,128)(2,1)S(1)}, bf16[2,128,1024]{2,1,0:T(8,128)(2,1)S(1)}, u32[]{:S(2)}, u32[]{:S(2)}) collective-permute-start(bf16[2,128,1024]{2,1,0:T(8,128)(2,1)S(1)} %pad_maximum_fusion.refs_3_), channel_id=1, source_target_pairs={{0,64},{16,208},{32,96},{48,240},{64,128},{80,16},{96,160},{112,48... | collective-permute-start | bytes 1572872 | tf_op jit(solution)/shard_map/ppermute | solution.py:50
  2.8 15.9 %collective-permute-start.1 = (bf16[2,128,1024]{2,1,0:T(8,128)(2,1)S(1)}, bf16[2,128,1024]{2,1,0:T(8,128)(2,1)S(1)}, u32[]{:S(2)}, u32[]{:S(2)}) collective-permute-start(bf16[2,128,1024]{2,1,0:T(8,128)(2,1)S(1)} %pad_maximum_fusion.refs_3_), channel_id=1, source_target_pairs={{0,32},{16,48},{32,0},{48,16},{64,96},{80,112},{96,64},{112,80},{1... | collective-permute-start | bytes 1572872 | tf_op jit(solution)/shard_map/ppermute | solution.py:46
  5.1 3.5 %copy-start.7 = (bf16[2,128,1024]{2,1,0:T(8,128)(2,1)}, bf16[2,128,1024]{2,1,0:T(8,128)(2,1)S(1)}, u32[]{:S(2)}) copy-start(bf16[2,128,1024]{2,1,0:T(8,128)(2,1)S(1)} %collective-permute-done.refs_4_) | copy-start | bytes 1572868
  5.1 13.7 %collective-permute-start.3 = (bf16[2,128,1024]{2,1,0:T(8,128)(2,1)S(1)}, bf16[2,128,1024]{2,1,0:T(8,128)(2,1)}, u32[]{:S(2)}, u32[]{:S(2)}) collective-permute-start(bf16[2,128,1024]{2,1,0:T(8,128)(2,1)S(1)} %collective-permute-done.refs_4_), channel_id=1, source_target_pairs={{0,64},{16,208},{32,96},{48,240},{64,128},{80,16},{96,160},{112,48... | collective-permute-start | bytes 1572872 | tf_op jit(solution)/shard_map/ppermute | solution.py:50
  6.6 0.8 copy-start.2
  8.5 39.0 %all-to-all-start = ((bf16[16,8,32,128]{3,2,1,0:T(8,128)(2,1)}), bf16[16,8,32,128]{3,2,1,0:T(8,128)(2,1)S(1)}, u32[]{:S(2)}, u32[]{:S(2)}) async-start(bf16[16,8,32,128]{3,2,1,0:T(8,128)(2,1)} %spread.1), calls=%async_computation | async-start | bytes 2097152 | tf_op jit(solution)/shard_map/all_to_all | solution.py:310
  18.5 29.8 %copy-start.8 = (bf16[2,128,1024]{2,1,0:T(8,128)(2,1)}, bf16[2,128,1024]{2,1,0:T(8,128)(2,1)S(1)}, u32[]{:S(2)}) copy-start(bf16[2,128,1024]{2,1,0:T(8,128)(2,1)S(1)} %collective-permute-done.2.refs_7_) | copy-start | bytes 1572868
  18.7 29.6 %copy-start.9 = (bf16[2,128,1024]{2,1,0:T(8,128)(2,1)}, bf16[2,128,1024]{2,1,0:T(8,128)(2,1)S(1)}, u32[]{:S(2)}) copy-start(bf16[2,128,1024]{2,1,0:T(8,128)(2,1)S(1)} %collective-permute-done.1.refs_5_) | copy-start | bytes 1572868
  18.7 10.4 %collective-permute-start.6 = (bf16[2,128,1024]{2,1,0:T(8,128)(2,1)S(1)}, bf16[2,128,1024]{2,1,0:T(8,128)(2,1)S(1)}, u32[]{:S(2)}, u32[]{:S(2)}) collective-permute-start(bf16[2,128,1024]{2,1,0:T(8,128)(2,1)S(1)} %collective-permute-done.1.refs_5_), channel_id=1, source_target_pairs={{0,64},{16,208},{32,96},{48,240},{64,128},{80,16},{96,160},{112,48... | collective-permute-start | bytes 1572872 | tf_op jit(solution)/shard_map/ppermute | solution.py:50
  19.8 9.3 %collective-permute-start.4 = (bf16[2,128,1024]{2,1,0:T(8,128)(2,1)S(1)}, bf16[2,128,1024]{2,1,0:T(8,128)(2,1)S(1)}, u32[]{:S(2)}, u32[]{:S(2)}) collective-permute-start(bf16[2,128,1024]{2,1,0:T(8,128)(2,1)S(1)} %collective-permute-done.1.refs_5_), channel_id=1, source_target_pairs={{0,16},{16,0},{32,48},{48,32},{64,80},{80,64},{96,112},{112,96},{1... | collective-permute-start | bytes 1572872 | tf_op jit(solution)/shard_map/ppermute | solution.py:42
  19.8 14.9 %collective-permute-start.5 = (bf16[2,128,1024]{2,1,0:T(8,128)(2,1)S(1)}, bf16[2,128,1024]{2,1,0:T(8,128)(2,1)S(1)}, u32[]{:S(2)}, u32[]{:S(2)}) collective-permute-start(bf16[2,128,1024]{2,1,0:T(8,128)(2,1)S(1)} %collective-permute-done.2.refs_7_), channel_id=1, source_target_pairs={{0,64},{16,208},{32,96},{48,240},{64,128},{80,16},{96,160},{112,48... | collective-permute-start | bytes 1572872 | tf_op jit(solution)/shard_map/ppermute | solution.py:50
  20.6 14.1 %collective-permute-start.9 = (bf16[2,128,1024]{2,1,0:T(8,128)(2,1)S(1)}, bf16[2,128,1024]{2,1,0:T(8,128)(2,1)S(1)}, u32[]{:S(2)}, u32[]{:S(2)}) collective-permute-start(bf16[2,128,1024]{2,1,0:T(8,128)(2,1)S(1)} %collective-permute-done.2.refs_7_), channel_id=1, source_target_pairs={{0,16},{16,0},{32,48},{48,32},{64,80},{80,64},{96,112},{112,96},{1... | collective-permute-start | bytes 1572872 | tf_op jit(solution)/shard_map/ppermute | solution.py:42
  29.1 19.2 %copy-start.10 = (bf16[2,128,1024]{2,1,0:T(8,128)(2,1)}, bf16[2,128,1024]{2,1,0:T(8,128)(2,1)S(1)}, u32[]{:S(2)}) copy-start(bf16[2,128,1024]{2,1,0:T(8,128)(2,1)S(1)} %collective-permute-done.6.refs_10_) | copy-start | bytes 1572868
  29.1 11.3 %collective-permute-start.8 = (bf16[2,128,1024]{2,1,0:T(8,128)(2,1)S(1)}, bf16[2,128,1024]{2,1,0:T(8,128)(2,1)}, u32[]{:S(2)}, u32[]{:S(2)}) collective-permute-start(bf16[2,128,1024]{2,1,0:T(8,128)(2,1)S(1)} %collective-permute-done.6.refs_10_), channel_id=1, source_target_pairs={{0,64},{16,208},{32,96},{48,240},{64,128},{80,16},{96,160},{112,48... | collective-permute-start | bytes 1572872 | tf_op jit(solution)/shard_map/ppermute | solution.py:50
  29.1 19.2 %copy-start.11 = (bf16[2,128,1024]{2,1,0:T(8,128)(2,1)}, bf16[2,128,1024]{2,1,0:T(8,128)(2,1)S(1)}, u32[]{:S(2)}) copy-start(bf16[2,128,1024]{2,1,0:T(8,128)(2,1)S(1)} %collective-permute-done.4.refs_6_) | copy-start | bytes 1572868
  29.1 16.9 %collective-permute-start.7 = (bf16[2,128,1024]{2,1,0:T(8,128)(2,1)S(1)}, bf16[2,128,1024]{2,1,0:T(8,128)(2,1)}, u32[]{:S(2)}, u32[]{:S(2)}) collective-permute-start(bf16[2,128,1024]{2,1,0:T(8,128)(2,1)S(1)} %collective-permute-done.4.refs_6_), channel_id=1, source_target_pairs={{0,64},{16,208},{32,96},{48,240},{64,128},{80,16},{96,160},{112,48... | collective-permute-start | bytes 1572872 | tf_op jit(solution)/shard_map/ppermute | solution.py:50
  29.5 18.1 %collective-permute-start.10 = (bf16[2,128,1024]{2,1,0:T(8,128)(2,1)}, bf16[2,128,1024]{2,1,0:T(8,128)(2,1)}, u32[]{:S(2)}, u32[]{:S(2)}) collective-permute-start(bf16[2,128,1024]{2,1,0:T(8,128)(2,1)} %collective-permute-done.3.refs_8_), channel_id=1, source_target_pairs={{0,16},{16,0},{32,48},{48,32},{64,80},{80,64},{96,112},{112,96},{1... | collective-permute-start | bytes 1572872 | tf_op jit(solution)/shard_map/ppermute | solution.py:42
  34.7 12.0 %copy-start.12 = (bf16[2,128,1024]{2,1,0:T(8,128)(2,1)}, bf16[2,128,1024]{2,1,0:T(8,128)(2,1)S(1)}, u32[]{:S(2)}) copy-start(bf16[2,128,1024]{2,1,0:T(8,128)(2,1)S(1)} %collective-permute-done.5.refs_9_) | copy-start | bytes 1572868
  34.7 12.0 %collective-permute-start.11 = (bf16[2,128,1024]{2,1,0:T(8,128)(2,1)S(1)}, bf16[2,128,1024]{2,1,0:T(8,128)(2,1)S(1)}, u32[]{:S(2)}, u32[]{:S(2)}) collective-permute-start(bf16[2,128,1024]{2,1,0:T(8,128)(2,1)S(1)} %collective-permute-done.5.refs_9_), channel_id=1, source_target_pairs={{0,16},{16,0},{32,48},{48,32},{64,80},{80,64},{96,112},{112,96},{1... | collective-permute-start | bytes 1572872 | tf_op jit(solution)/shard_map/ppermute | solution.py:42
  34.7 11.3 %copy-start.13 = (bf16[2,128,1024]{2,1,0:T(8,128)(2,1)}, bf16[2,128,1024]{2,1,0:T(8,128)(2,1)S(1)}, u32[]{:S(2)}) copy-start(bf16[2,128,1024]{2,1,0:T(8,128)(2,1)S(1)} %collective-permute-done.9.refs_13_) | copy-start | bytes 1572868
  34.7 12.8 %collective-permute-start.12 = (bf16[2,128,1024]{2,1,0:T(8,128)(2,1)S(1)}, bf16[2,128,1024]{2,1,0:T(8,128)(2,1)}, u32[]{:S(2)}, u32[]{:S(2)}) collective-permute-start(bf16[2,128,1024]{2,1,0:T(8,128)(2,1)S(1)} %collective-permute-done.6.refs_10_), channel_id=1, source_target_pairs={{0,16},{16,0},{32,48},{48,32},{64,80},{80,64},{96,112},{112,96},{1... | collective-permute-start | bytes 1572872 | tf_op jit(solution)/shard_map/ppermute | solution.py:42
  40.4 7.2 %collective-permute-start.14 = (bf16[2,128,1024]{2,1,0:T(8,128)(2,1)}, bf16[2,128,1024]{2,1,0:T(8,128)(2,1)}, u32[]{:S(2)}, u32[]{:S(2)}) collective-permute-start(bf16[2,128,1024]{2,1,0:T(8,128)(2,1)} %collective-permute-done.8.refs_12_), channel_id=1, source_target_pairs={{0,16},{16,0},{32,48},{48,32},{64,80},{80,64},{96,112},{112,96},{1... | collective-permute-start | bytes 1572872 | tf_op jit(solution)/shard_map/ppermute | solution.py:42
  46.1 2.3 %collective-permute-start.13 = (bf16[2,128,1024]{2,1,0:T(8,128)(2,1)}, bf16[2,128,1024]{2,1,0:T(8,128)(2,1)}, u32[]{:S(2)}, u32[]{:S(2)}) collective-permute-start(bf16[2,128,1024]{2,1,0:T(8,128)(2,1)} %collective-permute-done.7.refs_11_), channel_id=1, source_target_pairs={{0,16},{16,0},{32,48},{48,32},{64,80},{80,64},{96,112},{112,96},{1... | collective-permute-start | bytes 1572872 | tf_op jit(solution)/shard_map/ppermute | solution.py:42
  46.7 0.8 copy-start.14
  47.6 1.0 copy-start.5
  64.4 10.1 %copy-start = (bf16[4,128,1024]{2,1,0:T(8,128)(2,1)S(1)}, bf16[4,128,1024]{2,1,0:T(8,128)(2,1)}, u32[]{:S(2)}) copy-start(bf16[4,128,1024]{2,1,0:T(8,128)(2,1)} %k_ref.1) | copy-start | bytes 3145732
  64.4 10.1 %copy-start.1 = (bf16[4,128,1024]{2,1,0:T(8,128)(2,1)S(1)}, bf16[4,128,1024]{2,1,0:T(8,128)(2,1)}, u32[]{:S(2)}) copy-start(bf16[4,128,1024]{2,1,0:T(8,128)(2,1)} %v_ref.1) | copy-start | bytes 3145732
  64.4 10.1 %copy-start.3 = (bf16[4,8192]{1,0:T(4,128)(2,1)S(1)}, bf16[4,8192]{1,0:T(4,128)(2,1)}, u32[]{:S(2)}) copy-start(bf16[4,8192]{1,0:T(4,128)(2,1)} %param.10) | copy-start | bytes 196612
  64.4 10.1 %copy-start.4 = (s32[4]{0:T(128)S(1)}, s32[4]{0:T(128)}, u32[]{:S(2)}) copy-start(s32[4]{0:T(128)} %length_ref.1) | copy-start | bytes 52
  64.5 39.5 %all-to-all-start.1 = ((bf16[16,272,128]{2,1,0:T(8,128)(2,1)}), bf16[16,272,128]{2,1,0:T(8,128)(2,1)S(1)}, u32[]{:S(2)}, u32[]{:S(2)}) async-start(bf16[16,272,128]{2,1,0:T(8,128)(2,1)} %attend.1), calls=%async_computation.1 | async-start | bytes 2228224 | tf_op jit(solution)/shard_map/all_to_all | solution.py:313

commit v5 on v4

--- a/solution.py
+++ b/solution.py
@@ -63,7 +63,7 @@
     across = after(across, near, near_other)
     across_near = along_x(across)
     across_other = to_other_core(across)
-    across_near_other = along_x(across_other)
+    across_near_other = along_x(after(across_other, far))
     across_far = along_x(across_near)
     received = [near, near_other, far, across_near, across_near_other, across_far]
     return [own, other, across, across_other] + received + [to_other_core(r) for r in received]

time: 107 us -> 104 us (0.972); the launches traced: 105 us -> 104 us
  starting transfers between devices: 29.8 us -> 28 us
    all_to_all x1, starting transfers between devices: 10.1 us -> 8.26 us  [per_device(): parts = lax.all_to_all(part, 'dev', 0, 0)]
  transfers between devices with their start and end apart: 17 -> 17, of which waited for: 7 -> 6; matrix products, arithmetic and copies ran while one was open for 0% -> 0% of each run, Pallas kernels for 4% -> 4%
where the time goes in v5:
time: 104 us
  waiting for transfers between devices  50.5 us (49%)
  starting transfers between devices  28 us (27%)
  Pallas kernels  21.2 us (20%)
  local copies, waits for them, and re-layouts  1.95 us (2%)
  other arithmetic  1.08 us (1%)
    all_to_all x1, waiting for transfers between devices, per_device(): parts = lax.all_to_all(part, 'dev', 0, 0)  26.7 us
    ppermute x6, waiting for transfers between devices, along_x(): lax.ppermute(array, 'grp', grp_pairs(lambda x, y, c: (x + 1 - 2 * c, y, c)))  23.1 us
    pallas_call x1, Pallas kernels, attend(): pl.pallas_call(functools.partial(attention_kernel, len(pieces)), out_shap...  15.8 us
    all_to_all x1, starting transfers between devices, per_device(): q_all = lax.all_to_all(spread(q_units), 'dev', 0, 0)  9.95 us
    all_to_all x1, starting transfers between devices, per_device(): parts = lax.all_to_all(part, 'dev', 0, 0)  8.26 us
    ppermute x6, starting transfers between devices, along_x(): lax.ppermute(array, 'grp', grp_pairs(lambda x, y, c: (x + 1 - 2 * c, y, c)))  4.97 us
    pallas_call x1, Pallas kernels, attend_suffix(): pl.pallas_call(suffix_kernel, out_shape=(shape, shape), in_specs=[pl.Bloc...  2.65 us
    ppermute x8, starting transfers between devices, to_other_core(): return lax.ppermute(array, 'grp', grp_pairs(lambda x, y, c: (x, y, 1 - c)))  2.49 us
  transfers between devices with their start and end apart: 17, of which 6 were waited for; matrix products, arithmetic and copies ran while one was open for 0% of the time, Pallas kernels for 4%

profile of v5, /device:TPU:8, one launch (start us, length us, event | category | flops | bytes accessed | tf_op | source)
XLA Modules:
  0.0 103.5 jit_solution(17252594309009438810)
XLA Ops:
  0.0 1.1 %pad_maximum_fusion.refs_3_ = bf16[2,128,1024]{2,1,0:T(8,128)(2,1)S(1)} fusion(bf16[1,128,1024]{2,1,0:T(8,128)(2,1)} %bitcast.12, bf16[1,128,1024]{2,1,0:T(8,128)(2,1)} %bitcast.13), kind=kLoop, calls=%fused_computation | loop fusion | flops 262144 | bytes 1048576 | tf_op jit(solution)/shard_map/stack | solution.py:309
  1.1 0.1 collective-permute-start
  1.2 1.6 %collective-permute-start.2 = (bf16[2,128,1024]{2,1,0:T(8,128)(2,1)S(1)}, bf16[2,128,1024]{2,1,0:T(8,128)(2,1)S(1)}, u32[]{:S(2)}, u32[]{:S(2)}) collective-permute-start(bf16[2,128,1024]{2,1,0:T(8,128)(2,1)S(1)} %pad_maximum_fusion.refs_3_), channel_id=1, source_target_pairs={{0,64},{16,208},{32,96},{48,240},{64,128},{80,16},{96,160},{112,48... | collective-permute-start | bytes 1572872 | tf_op jit(solution)/shard_map/ppermute | solution.py:50
  2.8 2.3 %collective-permute-start.1 = (bf16[2,128,1024]{2,1,0:T(8,128)(2,1)S(1)}, bf16[2,128,1024]{2,1,0:T(8,128)(2,1)S(1)}, u32[]{:S(2)}, u32[]{:S(2)}) collective-permute-start(bf16[2,128,1024]{2,1,0:T(8,128)(2,1)S(1)} %pad_maximum_fusion.refs_3_), channel_id=1, source_target_pairs={{0,32},{16,48},{32,0},{48,16},{64,96},{80,112},{96,64},{112,80},{1... | collective-permute-start | bytes 1572872 | tf_op jit(solution)/shard_map/ppermute | solution.py:46
  5.1 1.5 %collective-permute-start.3 = (bf16[2,128,1024]{2,1,0:T(8,128)(2,1)S(1)}, bf16[2,128,1024]{2,1,0:T(8,128)(2,1)}, u32[]{:S(2)}, u32[]{:S(2)}) collective-permute-start(bf16[2,128,1024]{2,1,0:T(8,128)(2,1)S(1)} %collective-permute-done.refs_4_), channel_id=1, source_target_pairs={{0,64},{16,208},{32,96},{48,240},{64,128},{80,16},{96,160},{112,48... | collective-permute-start | bytes 1572872 | tf_op jit(solution)/shard_map/ppermute | solution.py:50
  6.6 0.8 copy-done.2
  7.4 1.1 %spread.1 = bf16[16,8,32,128]{3,2,1,0:T(8,128)(2,1)} custom-call(bf16[8,32,128]{2,1,0:T(8,128)(2,1)S(1)} %bitcast.10), custom_call_target="tpu_custom_call" | custom-call | bytes 1048576 | tf_op jit(solution)/shard_map/spread/pallas_call | solution.py:212
  8.5 10.0 %all-to-all-start = ((bf16[16,8,32,128]{3,2,1,0:T(8,128)(2,1)}), bf16[16,8,32,128]{3,2,1,0:T(8,128)(2,1)S(1)}, u32[]{:S(2)}, u32[]{:S(2)}) async-start(bf16[16,8,32,128]{3,2,1,0:T(8,128)(2,1)} %spread.1), calls=%async_computation | async-start | bytes 2097152 | tf_op jit(solution)/shard_map/all_to_all | solution.py:310
  18.5 1.3 %collective-permute-start.5 = (bf16[2,128,1024]{2,1,0:T(8,128)(2,1)S(1)}, bf16[2,128,1024]{2,1,0:T(8,128)(2,1)S(1)}, u32[]{:S(2)}, u32[]{:S(2)}) collective-permute-start(bf16[2,128,1024]{2,1,0:T(8,128)(2,1)S(1)} %collective-permute-done.2.refs_7_), channel_id=1, source_target_pairs={{0,64},{16,208},{32,96},{48,240},{64,128},{80,16},{96,160},{112,48... | collective-permute-start | bytes 1572872 | tf_op jit(solution)/shard_map/ppermute | solution.py:50
  19.8 0.1 collective-permute-start.4
  19.9 0.6 collective-permute-start.6
  20.5 1.7 %collective-permute-start.9 = (bf16[2,128,1024]{2,1,0:T(8,128)(2,1)S(1)}, bf16[2,128,1024]{2,1,0:T(8,128)(2,1)S(1)}, u32[]{:S(2)}, u32[]{:S(2)}) collective-permute-start(bf16[2,128,1024]{2,1,0:T(8,128)(2,1)S(1)} %collective-permute-done.2.refs_7_), channel_id=1, source_target_pairs={{0,16},{16,0},{32,48},{48,32},{64,80},{80,64},{96,112},{112,96},{1... | collective-permute-start | bytes 1572872 | tf_op jit(solution)/shard_map/ppermute | solution.py:42
  22.2 6.8 %collective-permute-done.5.refs_9_ = bf16[2,128,1024]{2,1,0:T(8,128)(2,1)S(1)} collective-permute-done((bf16[2,128,1024]{2,1,0:T(8,128)(2,1)S(1)}, bf16[2,128,1024]{2,1,0:T(8,128)(2,1)S(1)}, u32[]{:S(2)}, u32[]{:S(2)}) %collective-permute-start.5) | collective-permute-done | bytes 524320 | tf_op jit(solution)/shard_map/ppermute | solution.py:50
  29.0 0.1 collective-permute-start.7
  29.1 5.5 %collective-permute-done.6.refs_10_ = bf16[2,128,1024]{2,1,0:T(8,128)(2,1)S(1)} collective-permute-done((bf16[2,128,1024]{2,1,0:T(8,128)(2,1)S(1)}, bf16[2,128,1024]{2,1,0:T(8,128)(2,1)S(1)}, u32[]{:S(2)}, u32[]{:S(2)}) %collective-permute-start.6) | collective-permute-done | bytes 524320 | tf_op jit(solution)/shard_map/ppermute | solution.py:50
  34.6 0.5 collective-permute-start.10
  35.1 0.1 collective-permute-start.12
  35.2 5.1 %collective-permute-done.7.refs_11_ = bf16[2,128,1024]{2,1,0:T(8,128)(2,1)} collective-permute-done((bf16[2,128,1024]{2,1,0:T(8,128)(2,1)S(1)}, bf16[2,128,1024]{2,1,0:T(8,128)(2,1)}, u32[]{:S(2)}, u32[]{:S(2)}) %collective-permute-start.7) | collective-permute-done | bytes 524320 | tf_op jit(solution)/shard_map/ppermute | solution.py:50
  40.3 5.6 %collective-permute-done.8.refs_12_ = bf16[2,128,1024]{2,1,0:T(8,128)(2,1)} collective-permute-done((bf16[2,128,1024]{2,1,0:T(8,128)(2,1)S(1)}, bf16[2,128,1024]{2,1,0:T(8,128)(2,1)}, u32[]{:S(2)}, u32[]{:S(2)}) %collective-permute-start.8) | collective-permute-done | bytes 524320 | tf_op jit(solution)/shard_map/ppermute | solution.py:50
  45.9 0.0 collective-permute-start.14
  46.6 0.8 copy-done.14
  47.5 0.7 collective-permute-done.14.refs_18_
  48.2 0.2 copy-done.5
  48.5 15.8 %attend.1 = bf16[16,272,128]{2,1,0:T(8,128)(2,1)} custom-call(s32[1]{0:T(128)S(6)} %copy.12.refs_0_, s32[4,4]{1,0:T(4,128)} %bitcast.16, bf16[16,8,32,128]{3,2,1,0:T(8,128)(2,1)} %copy-done.5, bf16[2,128,1024]{2,1,0:T(8,128)(2,1)} %copy-done.6, bf16[2,128,1024]{2,1,0:T(8,128)(2,1)} %copy-done.7, bf16[2,128,1024]{2,1,0:T(8,128)(2,1)} %copy-done.9, ...), custom_call_target="tpu_custom_call" | custom-call | flops 9663676416 | bytes 9437184 | tf_op jit(solution)/shard_map/attend/pallas_call | solution.py:178
  64.3 0.0 copy-start
  64.3 0.0 copy-start.1
  64.3 0.0 copy-start.3
  64.3 0.0 copy-start.4
  64.4 8.3 %all-to-all-start.1 = ((bf16[16,272,128]{2,1,0:T(8,128)(2,1)}), bf16[16,272,128]{2,1,0:T(8,128)(2,1)S(1)}, u32[]{:S(2)}, u32[]{:S(2)}) async-start(bf16[16,272,128]{2,1,0:T(8,128)(2,1)} %attend.1), calls=%async_computation.1 | async-start | bytes 2228224 | tf_op jit(solution)/shard_map/all_to_all | solution.py:313
  72.6 2.7 %attend_suffix.1 = (f32[8,32,128]{2,1,0:T(8,128)S(1)}, f32[8,32,128]{2,1,0:T(8,128)S(1)}) custom-call(s32[4]{0:T(128)S(1)} %copy-done.4, bf16[8,32,128]{2,1,0:T(8,128)(2,1)S(1)} %bitcast.11, bf16[4,128,1024]{2,1,0:T(8,128)(2,1)S(1)} %copy-done, bf16[4,128,1024]{2,1,0:T(8,128)(2,1)S(1)} %copy-done.1), custom_call_target="tpu_custom_call" | custom-call | flops 67108864 | bytes 2097152 | tf_op jit(solution)/shard_map/attend_suffix/pallas_call | solution.py:248
  75.3 26.7 %all-to-all-done.1.parts_ref = bf16[16,272,128]{2,1,0:T(8,128)(2,1)S(1)} async-done(((bf16[16,272,128]{2,1,0:T(8,128)(2,1)}), bf16[16,272,128]{2,1,0:T(8,128)(2,1)S(1)}, u32[]{:S(2)}, u32[]{:S(2)}) %all-to-all-start.1) | async-done | bytes 1114144 | tf_op jit(solution)/shard_map/all_to_all | solution.py:313
  102.0 1.5 %merge.1 = bf16[4,8192]{1,0:T(4,128)(2,1)} custom-call(bf16[16,272,128]{2,1,0:T(8,128)(2,1)S(1)} %all-to-all-done.1.parts_ref, f32[8,32,128]{2,1,0:T(8,128)S(1)} %get-tuple-element.11.out_suf_ref, f32[8,32,128]{2,1,0:T(8,128)S(1)} %get-tuple-element.12.lse_suf_ref), custom_call_target="tpu_custom_call" | custom-call | flops 2097152 | bytes 1048576 | tf_op jit(solution)/shard_map/merge/pallas_call | solution.py:283
  (37 shorter events, 0.1 us)
Async XLA Ops:
  1.1 7.5 %copy-start.6 = (bf16[2,128,1024]{2,1,0:T(8,128)(2,1)}, bf16[2,128,1024]{2,1,0:T(8,128)(2,1)S(1)}, u32[]{:S(2)}) copy-start(bf16[2,128,1024]{2,1,0:T(8,128)(2,1)S(1)} %pad_maximum_fusion.refs_3_) | copy-start | bytes 1572868
  1.1 4.0 %collective-permute-start = (bf16[2,128,1024]{2,1,0:T(8,128)(2,1)S(1)}, bf16[2,128,1024]{2,1,0:T(8,128)(2,1)S(1)}, u32[]{:S(2)}, u32[]{:S(2)}) collective-permute-start(bf16[2,128,1024]{2,1,0:T(8,128)(2,1)S(1)} %pad_maximum_fusion.refs_3_), channel_id=1, source_target_pairs={{0,16},{16,0},{32,48},{48,32},{64,80},{80,64},{96,112},{112,96},{1... | collective-permute-start | bytes 1572872 | tf_op jit(solution)/shard_map/ppermute | solution.py:42
  1.2 17.3 %collective-permute-start.2 = (bf16[2,128,1024]{2,1,0:T(8,128)(2,1)S(1)}, bf16[2,128,1024]{2,1,0:T(8,128)(2,1)S(1)}, u32[]{:S(2)}, u32[]{:S(2)}) collective-permute-start(bf16[2,128,1024]{2,1,0:T(8,128)(2,1)S(1)} %pad_maximum_fusion.refs_3_), channel_id=1, source_target_pairs={{0,64},{16,208},{32,96},{48,240},{64,128},{80,16},{96,160},{112,48... | collective-permute-start | bytes 1572872 | tf_op jit(solution)/shard_map/ppermute | solution.py:50
  2.8 17.0 %collective-permute-start.1 = (bf16[2,128,1024]{2,1,0:T(8,128)(2,1)S(1)}, bf16[2,128,1024]{2,1,0:T(8,128)(2,1)S(1)}, u32[]{:S(2)}, u32[]{:S(2)}) collective-permute-start(bf16[2,128,1024]{2,1,0:T(8,128)(2,1)S(1)} %pad_maximum_fusion.refs_3_), channel_id=1, source_target_pairs={{0,32},{16,48},{32,0},{48,16},{64,96},{80,112},{96,64},{112,80},{1... | collective-permute-start | bytes 1572872 | tf_op jit(solution)/shard_map/ppermute | solution.py:46
  5.1 3.5 %copy-start.7 = (bf16[2,128,1024]{2,1,0:T(8,128)(2,1)}, bf16[2,128,1024]{2,1,0:T(8,128)(2,1)S(1)}, u32[]{:S(2)}) copy-start(bf16[2,128,1024]{2,1,0:T(8,128)(2,1)S(1)} %collective-permute-done.refs_4_) | copy-start | bytes 1572868
  5.1 14.7 %collective-permute-start.3 = (bf16[2,128,1024]{2,1,0:T(8,128)(2,1)S(1)}, bf16[2,128,1024]{2,1,0:T(8,128)(2,1)}, u32[]{:S(2)}, u32[]{:S(2)}) collective-permute-start(bf16[2,128,1024]{2,1,0:T(8,128)(2,1)S(1)} %collective-permute-done.refs_4_), channel_id=1, source_target_pairs={{0,64},{16,208},{32,96},{48,240},{64,128},{80,16},{96,160},{112,48... | collective-permute-start | bytes 1572872 | tf_op jit(solution)/shard_map/ppermute | solution.py:50
  6.6 0.8 copy-start.2
  8.5 38.9 %all-to-all-start = ((bf16[16,8,32,128]{3,2,1,0:T(8,128)(2,1)}), bf16[16,8,32,128]{3,2,1,0:T(8,128)(2,1)S(1)}, u32[]{:S(2)}, u32[]{:S(2)}) async-start(bf16[16,8,32,128]{3,2,1,0:T(8,128)(2,1)} %spread.1), calls=%async_computation | async-start | bytes 2097152 | tf_op jit(solution)/shard_map/all_to_all | solution.py:310
  18.5 29.7 %copy-start.8 = (bf16[2,128,1024]{2,1,0:T(8,128)(2,1)}, bf16[2,128,1024]{2,1,0:T(8,128)(2,1)S(1)}, u32[]{:S(2)}) copy-start(bf16[2,128,1024]{2,1,0:T(8,128)(2,1)S(1)} %collective-permute-done.2.refs_7_) | copy-start | bytes 1572868
  18.5 10.5 %collective-permute-start.5 = (bf16[2,128,1024]{2,1,0:T(8,128)(2,1)S(1)}, bf16[2,128,1024]{2,1,0:T(8,128)(2,1)S(1)}, u32[]{:S(2)}, u32[]{:S(2)}) collective-permute-start(bf16[2,128,1024]{2,1,0:T(8,128)(2,1)S(1)} %collective-permute-done.2.refs_7_), channel_id=1, source_target_pairs={{0,64},{16,208},{32,96},{48,240},{64,128},{80,16},{96,160},{112,48... | collective-permute-start | bytes 1572872 | tf_op jit(solution)/shard_map/ppermute | solution.py:50
  19.8 28.4 %copy-start.9 = (bf16[2,128,1024]{2,1,0:T(8,128)(2,1)}, bf16[2,128,1024]{2,1,0:T(8,128)(2,1)S(1)}, u32[]{:S(2)}) copy-start(bf16[2,128,1024]{2,1,0:T(8,128)(2,1)S(1)} %collective-permute-done.1.refs_5_) | copy-start | bytes 1572868
  19.8 9.2 %collective-permute-start.4 = (bf16[2,128,1024]{2,1,0:T(8,128)(2,1)S(1)}, bf16[2,128,1024]{2,1,0:T(8,128)(2,1)S(1)}, u32[]{:S(2)}, u32[]{:S(2)}) collective-permute-start(bf16[2,128,1024]{2,1,0:T(8,128)(2,1)S(1)} %collective-permute-done.1.refs_5_), channel_id=1, source_target_pairs={{0,16},{16,0},{32,48},{48,32},{64,80},{80,64},{96,112},{112,96},{1... | collective-permute-start | bytes 1572872 | tf_op jit(solution)/shard_map/ppermute | solution.py:42
  19.9 14.7 %collective-permute-start.6 = (bf16[2,128,1024]{2,1,0:T(8,128)(2,1)S(1)}, bf16[2,128,1024]{2,1,0:T(8,128)(2,1)S(1)}, u32[]{:S(2)}, u32[]{:S(2)}) collective-permute-start(bf16[2,128,1024]{2,1,0:T(8,128)(2,1)S(1)} %collective-permute-done.1.refs_5_), channel_id=1, source_target_pairs={{0,64},{16,208},{32,96},{48,240},{64,128},{80,16},{96,160},{112,48... | collective-permute-start | bytes 1572872 | tf_op jit(solution)/shard_map/ppermute | solution.py:50
  20.5 14.7 %collective-permute-start.9 = (bf16[2,128,1024]{2,1,0:T(8,128)(2,1)S(1)}, bf16[2,128,1024]{2,1,0:T(8,128)(2,1)S(1)}, u32[]{:S(2)}, u32[]{:S(2)}) collective-permute-start(bf16[2,128,1024]{2,1,0:T(8,128)(2,1)S(1)} %collective-permute-done.2.refs_7_), channel_id=1, source_target_pairs={{0,16},{16,0},{32,48},{48,32},{64,80},{80,64},{96,112},{112,96},{1... | collective-permute-start | bytes 1572872 | tf_op jit(solution)/shard_map/ppermute | solution.py:42
  29.0 17.6 %copy-start.10 = (bf16[2,128,1024]{2,1,0:T(8,128)(2,1)}, bf16[2,128,1024]{2,1,0:T(8,128)(2,1)S(1)}, u32[]{:S(2)}) copy-start(bf16[2,128,1024]{2,1,0:T(8,128)(2,1)S(1)} %collective-permute-done.5.refs_9_) | copy-start | bytes 1572868
  29.0 19.2 %copy-start.11 = (bf16[2,128,1024]{2,1,0:T(8,128)(2,1)}, bf16[2,128,1024]{2,1,0:T(8,128)(2,1)S(1)}, u32[]{:S(2)}) copy-start(bf16[2,128,1024]{2,1,0:T(8,128)(2,1)S(1)} %collective-permute-done.4.refs_6_) | copy-start | bytes 1572868
  29.0 11.3 %collective-permute-start.7 = (bf16[2,128,1024]{2,1,0:T(8,128)(2,1)S(1)}, bf16[2,128,1024]{2,1,0:T(8,128)(2,1)}, u32[]{:S(2)}, u32[]{:S(2)}) collective-permute-start(bf16[2,128,1024]{2,1,0:T(8,128)(2,1)S(1)} %collective-permute-done.4.refs_6_), channel_id=1, source_target_pairs={{0,64},{16,208},{32,96},{48,240},{64,128},{80,16},{96,160},{112,48... | collective-permute-start | bytes 1572872 | tf_op jit(solution)/shard_map/ppermute | solution.py:50
  34.6 13.6 %copy-start.12 = (bf16[2,128,1024]{2,1,0:T(8,128)(2,1)}, bf16[2,128,1024]{2,1,0:T(8,128)(2,1)S(1)}, u32[]{:S(2)}) copy-start(bf16[2,128,1024]{2,1,0:T(8,128)(2,1)S(1)} %collective-permute-done.6.refs_10_) | copy-start | bytes 1572868
  34.6 11.3 %collective-permute-start.8 = (bf16[2,128,1024]{2,1,0:T(8,128)(2,1)S(1)}, bf16[2,128,1024]{2,1,0:T(8,128)(2,1)}, u32[]{:S(2)}, u32[]{:S(2)}) collective-permute-start(bf16[2,128,1024]{2,1,0:T(8,128)(2,1)S(1)} %collective-permute-done.6.refs_10_), channel_id=1, source_target_pairs={{0,64},{16,208},{32,96},{48,240},{64,128},{80,16},{96,160},{112,48... | collective-permute-start | bytes 1572872 | tf_op jit(solution)/shard_map/ppermute | solution.py:50
  34.6 12.0 %collective-permute-start.11 = (bf16[2,128,1024]{2,1,0:T(8,128)(2,1)S(1)}, bf16[2,128,1024]{2,1,0:T(8,128)(2,1)S(1)}, u32[]{:S(2)}, u32[]{:S(2)}) collective-permute-start(bf16[2,128,1024]{2,1,0:T(8,128)(2,1)S(1)} %collective-permute-done.5.refs_9_), channel_id=1, source_target_pairs={{0,16},{16,0},{32,48},{48,32},{64,80},{80,64},{96,112},{112,96},{1... | collective-permute-start | bytes 1572872 | tf_op jit(solution)/shard_map/ppermute | solution.py:42
  34.6 12.8 %collective-permute-start.10 = (bf16[2,128,1024]{2,1,0:T(8,128)(2,1)}, bf16[2,128,1024]{2,1,0:T(8,128)(2,1)}, u32[]{:S(2)}, u32[]{:S(2)}) collective-permute-start(bf16[2,128,1024]{2,1,0:T(8,128)(2,1)} %collective-permute-done.3.refs_8_), channel_id=1, source_target_pairs={{0,16},{16,0},{32,48},{48,32},{64,80},{80,64},{96,112},{112,96},{1... | collective-permute-start | bytes 1572872 | tf_op jit(solution)/shard_map/ppermute | solution.py:42
  35.1 10.8 %copy-start.13 = (bf16[2,128,1024]{2,1,0:T(8,128)(2,1)}, bf16[2,128,1024]{2,1,0:T(8,128)(2,1)S(1)}, u32[]{:S(2)}) copy-start(bf16[2,128,1024]{2,1,0:T(8,128)(2,1)S(1)} %collective-permute-done.9.refs_13_) | copy-start | bytes 1572868
  35.1 12.3 %collective-permute-start.12 = (bf16[2,128,1024]{2,1,0:T(8,128)(2,1)S(1)}, bf16[2,128,1024]{2,1,0:T(8,128)(2,1)}, u32[]{:S(2)}, u32[]{:S(2)}) collective-permute-start(bf16[2,128,1024]{2,1,0:T(8,128)(2,1)S(1)} %collective-permute-done.6.refs_10_), channel_id=1, source_target_pairs={{0,16},{16,0},{32,48},{48,32},{64,80},{80,64},{96,112},{112,96},{1... | collective-permute-start | bytes 1572872 | tf_op jit(solution)/shard_map/ppermute | solution.py:42
  40.3 7.2 %collective-permute-start.13 = (bf16[2,128,1024]{2,1,0:T(8,128)(2,1)}, bf16[2,128,1024]{2,1,0:T(8,128)(2,1)}, u32[]{:S(2)}, u32[]{:S(2)}) collective-permute-start(bf16[2,128,1024]{2,1,0:T(8,128)(2,1)} %collective-permute-done.7.refs_11_), channel_id=1, source_target_pairs={{0,16},{16,0},{32,48},{48,32},{64,80},{80,64},{96,112},{112,96},{1... | collective-permute-start | bytes 1572872 | tf_op jit(solution)/shard_map/ppermute | solution.py:42
  45.9 2.3 %collective-permute-start.14 = (bf16[2,128,1024]{2,1,0:T(8,128)(2,1)}, bf16[2,128,1024]{2,1,0:T(8,128)(2,1)}, u32[]{:S(2)}, u32[]{:S(2)}) collective-permute-start(bf16[2,128,1024]{2,1,0:T(8,128)(2,1)} %collective-permute-done.8.refs_12_), channel_id=1, source_target_pairs={{0,16},{16,0},{32,48},{48,32},{64,80},{80,64},{96,112},{112,96},{1... | collective-permute-start | bytes 1572872 | tf_op jit(solution)/shard_map/ppermute | solution.py:42
  46.6 0.8 copy-start.14
  47.5 1.0 copy-start.5
  64.3 8.3 %copy-start = (bf16[4,128,1024]{2,1,0:T(8,128)(2,1)S(1)}, bf16[4,128,1024]{2,1,0:T(8,128)(2,1)}, u32[]{:S(2)}) copy-start(bf16[4,128,1024]{2,1,0:T(8,128)(2,1)} %k_ref.1) | copy-start | bytes 3145732
  64.3 8.3 %copy-start.1 = (bf16[4,128,1024]{2,1,0:T(8,128)(2,1)S(1)}, bf16[4,128,1024]{2,1,0:T(8,128)(2,1)}, u32[]{:S(2)}) copy-start(bf16[4,128,1024]{2,1,0:T(8,128)(2,1)} %v_ref.1) | copy-start | bytes 3145732
  64.3 8.3 %copy-start.3 = (bf16[4,8192]{1,0:T(4,128)(2,1)S(1)}, bf16[4,8192]{1,0:T(4,128)(2,1)}, u32[]{:S(2)}) copy-start(bf16[4,8192]{1,0:T(4,128)(2,1)} %param.10) | copy-start | bytes 196612
  64.3 8.3 %copy-start.4 = (s32[4]{0:T(128)S(1)}, s32[4]{0:T(128)}, u32[]{:S(2)}) copy-start(s32[4]{0:T(128)} %length_ref.1) | copy-start | bytes 52
  64.4 37.6 %all-to-all-start.1 = ((bf16[16,272,128]{2,1,0:T(8,128)(2,1)}), bf16[16,272,128]{2,1,0:T(8,128)(2,1)S(1)}, u32[]{:S(2)}, u32[]{:S(2)}) async-start(bf16[16,272,128]{2,1,0:T(8,128)(2,1)} %attend.1), calls=%async_computation.1 | async-start | bytes 2228224 | tf_op jit(solution)/shard_map/all_to_all | solution.py:313
